TPU v7x, 128 devices: a whole 4x4x4 slice. The times are simulated.
128 devices in a mesh: prompt: 8 (over z, core), comp: 16 (over y, x).
Axes of the slice: x: 4, y: 4, z: 4, core: 2. Of those that a mesh axis runs over, the one named last changes fastest.
Arguments:
- queries: bfloat16 [512, 3, 8192], P(('prompt', 'comp')), may hold values from -98 to 98
- new_kv: bfloat16 [512, 3, 2, 512], P(('prompt', 'comp')), may hold values from -8 to 8
- suffix_kv: bfloat16 [512, 256, 2, 512], P(('prompt', 'comp')), may hold values from -8 to 8
- suffix_len: int32 [512], P(('prompt', 'comp')), may hold values from 1 to 256
- pool_kv: bfloat16 [1024, 128, 2, 512], P(('prompt', 'comp')), may hold values from -8 to 8
- sys_kv: bfloat16 [2048, 2, 512], P(('prompt', 'comp')), may hold values from -8 to 8
- block_slot: int32 [8, 128], P('prompt'), may hold values from 0 to 127, as said below
- block_list: int32 [512, 64], P(('prompt', 'comp')), may hold values from 0 to 127, as said below
- prefix_blocks: int32 [512], P(('prompt', 'comp')), may hold values from 32 to 64, as said below
Outputs:
- attn_out: bfloat16 [512, 3, 8192], P(('prompt', 'comp'))
Inputs may be any that keep to these rules, and one draw needn't show every extreme that they name: `block_slot`: each row is a permutation of the 128 slots of one group; the slots d * 8 to (d + 1) * 8 - 1 hold exactly 4 logical blocks of each prompt's region. `block_list`: the 32 consecutive completions of one prompt share one row; entries of a row are distinct blocks of its prompt's region, blocks p * 64 to (p + 1) * 64 - 1 for prompt p = (c % 64) // 32. `prefix_blocks`: shared by the completions of one prompt; in every group some prompt has 64.
All inputs are finite; a program needn't handle non-finite values.
Results may differ from a plain program's by a relative error of at most 0.0055.
Values may be sent and summed in bfloat16 or wider, within the bound.
No kernel may reach another device: no remote copies, remote signals or barrier semaphores. Data moves between devices by JAX's collectives and lax.ppermute only.
A program may use at most 128 MiB of HBM per device.

v0:
```python
import jax
import jax.numpy as jnp
from jax import lax
from jax.sharding import PartitionSpec as P

QH = 64
KVH = 4
HD = 128


def pick_block(total, target):
    length = min(total, target)
    while total % length != 0:
        length = length - 1
    return length


def fresh_state(row_count):
    return (
        jnp.full((KVH, row_count), -jnp.inf, jnp.float32),
        jnp.zeros((KVH, row_count), jnp.float32),
        jnp.zeros((KVH, row_count, HD), jnp.float32),
    )


def head_update(old_max, old_total, old_out, scores, product):
    new_max = jnp.maximum(old_max, jnp.max(scores, axis=-1))
    safe_max = jnp.where(new_max == -jnp.inf, 0.0, new_max)
    weights = jnp.exp(scores - safe_max[:, None])
    factor = jnp.exp(old_max - safe_max)
    new_total = old_total * factor + jnp.sum(weights, axis=-1)
    new_out = old_out * factor[:, None] + product(weights.astype(jnp.bfloat16))
    return (new_max, new_total, new_out)


def restack(pieces):
    return (
        jnp.stack([one[0] for one in pieces], axis=0),
        jnp.stack([one[1] for one in pieces], axis=0),
        jnp.stack([one[2] for one in pieces], axis=0),
    )


def attend_shared(running, head_rows, token_kv, row_mask):
    scaling = head_rows.shape[-1] ** (-0.5)
    old_max, old_total, old_out = running
    pieces = []
    for head in range(KVH):
        key_rows = token_kv[:, 0, head * HD : (head + 1) * HD]
        value_rows = token_kv[:, 1, head * HD : (head + 1) * HD]
        scores = (
            jnp.einsum("qd,nd->qn", head_rows[head], key_rows, preferred_element_type=jnp.float32)
            * scaling
        )
        if row_mask is not None:
            scores = jnp.where(row_mask, scores, -jnp.inf)

        def product(rounded, value_rows=value_rows):
            return jnp.dot(rounded, value_rows, preferred_element_type=jnp.float32)

        pieces.append(head_update(old_max[head], old_total[head], old_out[head], scores, product))
    return restack(pieces)


def attend_own(running, head_rows, own_kv, comp_mask):
    scaling = head_rows.shape[-1] ** (-0.5)
    comp_count = own_kv.shape[0]
    token_count = own_kv.shape[1]
    row_count = head_rows.shape[1]
    step_count = comp_mask.shape[1]
    per_comp = row_count // comp_count
    group_size = per_comp // step_count
    full_mask = jnp.broadcast_to(
        comp_mask[:, :, None, :], (comp_count, step_count, group_size, token_count)
    ).reshape(row_count, token_count)
    old_max, old_total, old_out = running
    pieces = []
    for head in range(KVH):
        key_rows = own_kv[:, :, 0, head * HD : (head + 1) * HD]
        value_rows = own_kv[:, :, 1, head * HD : (head + 1) * HD]
        query_here = head_rows[head].reshape(comp_count, per_comp, HD)
        scores = (
            jnp.einsum("cqd,cnd->cqn", query_here, key_rows, preferred_element_type=jnp.float32)
            * scaling
        )
        scores = jnp.where(full_mask, scores.reshape(row_count, token_count), -jnp.inf)

        def product(rounded, value_rows=value_rows):
            grouped = rounded.reshape(comp_count, per_comp, token_count)
            return jnp.einsum(
                "cqn,cnd->cqd", grouped, value_rows, preferred_element_type=jnp.float32
            ).reshape(row_count, HD)

        pieces.append(head_update(old_max[head], old_total[head], old_out[head], scores, product))
    return restack(pieces)


def blockwise(running, head_rows, token_kv, comp_mask):
    total_tokens = token_kv.shape[0]
    block_len = pick_block(total_tokens, 512)
    block_count = total_tokens // block_len
    blocks = token_kv.reshape(block_count, block_len, 2, token_kv.shape[-1])
    if comp_mask is None:

        def advance(carried, one_block):
            return (attend_shared(carried, head_rows, one_block, None), None)

        running, unused = lax.scan(advance, running, blocks)
    else:
        comp_count = comp_mask.shape[0]
        row_count = head_rows.shape[1]
        per_comp = row_count // comp_count
        mask_rows = comp_mask.reshape(comp_count, block_count, block_len).transpose(1, 0, 2)

        def advance_masked(carried, operands):
            one_block, one_mask = operands
            row_mask = jnp.broadcast_to(
                one_mask[:, None, :], (comp_count, per_comp, block_len)
            ).reshape(row_count, block_len)
            return (attend_shared(carried, head_rows, one_block, row_mask), None)

        running, unused = lax.scan(advance_masked, running, (blocks, mask_rows))
    return running


def block_usage(slot_row, block_list, prefix_blocks, pool_size):
    positions = jnp.arange(pool_size, dtype=jnp.int32)
    picked = block_list[:, :, None] == positions[None, None, :]
    slot_of = jnp.sum(jnp.where(picked, slot_row[None, None, :], 0), axis=-1)
    live = jnp.arange(block_list.shape[1], dtype=jnp.int32)[None, :] < prefix_blocks[:, None]
    return jnp.any((slot_of[:, :, None] == positions[None, None, :]) & live[:, :, None], axis=1)


def to_heads(query_block, comp_count, step_count):
    group_size = QH // KVH
    shaped = query_block.reshape(comp_count, step_count, KVH, group_size, HD)
    return shaped.transpose(2, 0, 1, 3, 4).reshape(KVH, comp_count * step_count * group_size, HD)


def body(
    queries, new_kv, suffix_kv, suffix_len, pool_kv, sys_kv, block_slot, block_list, prefix_blocks
):
    local_count = queries.shape[0]
    step_count = queries.shape[1]
    group_size = QH // KVH
    row_count = local_count * step_count * group_size
    head_rows = to_heads(queries, local_count, step_count)
    carried = fresh_state(row_count)
    suffix_mask = (
        jnp.arange(suffix_kv.shape[1], dtype=jnp.int32)[None, None, :] < suffix_len[:, None, None]
    )
    suffix_mask = jnp.broadcast_to(suffix_mask, (local_count, step_count, suffix_kv.shape[1]))
    carried = attend_own(carried, head_rows, suffix_kv, suffix_mask)
    step_mask = jnp.arange(step_count)[None, :] <= jnp.arange(step_count)[:, None]
    step_mask = jnp.broadcast_to(step_mask[None], (local_count, step_count, step_count))
    carried = attend_own(carried, head_rows, new_kv, step_mask)
    carried = blockwise(
        carried, head_rows, lax.all_gather(sys_kv, ("prompt", "comp"), axis=0, tiled=True), None
    )
    blocks_local = pool_kv.shape[0]
    pool_size = blocks_local * lax.axis_size("comp")
    usage = block_usage(block_slot[0], block_list, prefix_blocks, pool_size)
    portion = lax.all_gather(pool_kv, "comp", axis=0, tiled=True)
    token_mask = usage
    token_mask = jnp.repeat(token_mask, portion.shape[1], axis=1)
    carried = blockwise(carried, head_rows, portion.reshape(-1, 2, KVH * HD), token_mask)
    final_max, final_total, final_out = carried
    result = final_out / final_total[..., None]
    result = result.reshape(KVH, local_count, step_count, group_size, HD).transpose(1, 2, 0, 3, 4)
    return result.reshape(local_count, step_count, QH * HD).astype(jnp.bfloat16)


def solution(mesh):
    in_specs = (
        P(("prompt", "comp"), None, None),
        P(("prompt", "comp"), None, None, None),
        P(("prompt", "comp"), None, None, None),
        P(("prompt", "comp")),
        P(("prompt", "comp"), None, None, None),
        P(("prompt", "comp"), None, None),
        P("prompt", None),
        P(("prompt", "comp"), None),
        P(("prompt", "comp")),
    )
    out_specs = P(("prompt", "comp"), None, None)
    return jax.shard_map(body, mesh=mesh, in_specs=in_specs, out_specs=out_specs, check_vma=False)
```

profile of v0, /device:TPU:0, one launch (start us, length us, event | category | flops | bytes accessed | tf_op | source)
XLA Modules:
  0.0 437.2 jit_solution(10853291156818975360)
XLA Ops:
  6.5 1.5 copy.87
  8.1 3.3 copy.89
  11.8 4.0 fusion.184
  17.6 1.5 fusion.187
  19.4 1.3 fusion.190
  21.2 1.3 fusion.192
  23.1 1.3 fusion.194
  34.4 45.4 %all-gather.3.cloned.1.call-done = bf16[2048,2,512]{2,0,1:T(8,128)(2,1)} async-done(((bf16[16,2,512]{2,0,1:T(8,128)(2,1)}), bf16[2048,2,512]{2,0,1:T(8,128)(2,1)}) %all-gather.3.cloned.1.call-update) | async-done | bytes 4194320 | tf_op jit(solution)/shard_map/all_gather | solution.py:158
  79.8 19.0 %while.28 = (s32[]{:T(128)}, f32[4,192]{1,0:T(4,128)S(1)}, f32[4,192]{1,0:T(4,128)S(1)}, f32[4,192,128]{2,1,0:T(8,128)S(1)}, bf16[4,512,2,512]{3,1,0,2:T(8,128)(...) while((s32[]{:T(128)}, f32[4,192]{1,0:T(4,128)S(1)}, f32[4,192]{1,0:T(4,128)S(1)}, ...), condition=%wide.region_25.26_spmd, body=%wide.region_16.25_spmd.sunk | while | flops 204188160 | bytes 9700441 | solution.py:108
  89.2 1.5 dynamic-slice_bitcast_fusion.6
  94.1 1.3 dynamic-slice_bitcast_fusion.6
  98.8 178.0 %all-gather.5.cloned.1.call-done = bf16[128,128,2,512]{3,1,0,2:T(8,128)(2,1)} async-done(((bf16[8,128,2,512]{3,1,0,2:T(8,128)(2,1)}), bf16[128,128,2,512]{3,1,0,2:T(8,128)(2,1)}) %all-gather.5.cloned.1.call-update) | async-done | bytes 33554448 | tf_op jit(solution)/shard_map/all_gather | solution.py:163
  276.8 152.7 %while.29 = (s32[]{:T(128)}, f32[4,192]{1,0:T(4,128)S(1)}, f32[4,192]{1,0:T(4,128)S(1)}, f32[4,192,128]{2,1,0:T(8,128)S(1)}, pred[32,4,512]{2,1,0:T(4,128)(4,1)S...) while((s32[]{:T(128)}, f32[4,192]{1,0:T(4,128)S(1)}, ...), condition=%wide.region_37.38_spmd, body=%wide.region_28.37_spmd.sunk | while | flops 204581376 | bytes 10198117 | solution.py:122
  276.8 1.3 dynamic-slice_bitcast_fusion.8
  281.6 1.3 dynamic-slice_bitcast_fusion.8
  286.4 1.3 dynamic-slice_bitcast_fusion.8
  291.1 1.3 dynamic-slice_bitcast_fusion.8
  295.9 1.3 dynamic-slice_bitcast_fusion.8
  300.7 1.3 dynamic-slice_bitcast_fusion.8
  305.4 1.3 dynamic-slice_bitcast_fusion.8
  310.2 1.3 dynamic-slice_bitcast_fusion.8
  315.0 1.3 dynamic-slice_bitcast_fusion.8
  319.8 1.3 dynamic-slice_bitcast_fusion.8
  324.5 1.3 dynamic-slice_bitcast_fusion.8
  329.3 1.3 dynamic-slice_bitcast_fusion.8
  334.1 1.3 dynamic-slice_bitcast_fusion.8
  338.9 1.3 dynamic-slice_bitcast_fusion.8
  343.6 1.3 dynamic-slice_bitcast_fusion.8
  367.5 1.3 dynamic-slice_bitcast_fusion.8
  396.1 1.3 dynamic-slice_bitcast_fusion.8
  415.2 1.3 dynamic-slice_bitcast_fusion.8
  424.8 1.3 dynamic-slice_bitcast_fusion.8
  (890 shorter events, 154.0 us)
Async XLA Ops:
  6.5 4.9 %copy-start.3 = (bf16[4,3,8192]{2,0,1:T(4,128)(2,1)S(1)}, bf16[4,3,8192]{2,0,1:T(4,128)(2,1)}, u32[]{:S(2)}) copy-start(bf16[4,3,8192]{2,0,1:T(4,128)(2,1)} %param.13) | copy-start | bytes 589828
  6.5 5.2 %copy-start.4 = (s32[4]{0:T(128)S(1)}, s32[4]{0:T(128)}, u32[]{:S(2)}) copy-start(s32[4]{0:T(128)} %param.16) | copy-start | bytes 52
  6.5 5.3 %copy-start = (bf16[4,256,2,512]{3,2,1,0:T(2,128)(2,1)S(1)}, bf16[4,256,2,512]{3,2,1,0:T(2,128)(2,1)}, u32[]{:S(2)}) copy-start(bf16[4,256,2,512]{3,2,1,0:T(2,128)(2,1)} %param.15) | copy-start | bytes 6291460
  6.5 73.3 %all-gather.3.cloned.1.call-start = ((), (), s32[]{:S(2)}) async-start(), calls=%async_computation | async-start | bytes 4227072 | tf_op jit(solution)/shard_map/all_gather | solution.py:158
  8.1 268.7 %all-gather.5.cloned.1.call-start = ((), (), s32[]{:S(2)}) async-start(), calls=%async_computation.1 | async-start | bytes 35651584 | tf_op jit(solution)/shard_map/all_gather | solution.py:163
  15.9 17.2 %copy-start.2 = (bf16[4,256,1,128]{3,2,1,0:T(2,128)(2,1)S(1)}, bf16[4,256,1,128]{3,2,1,0:T(2,128)(2,1)}, u32[]{:S(2)}) copy-start(bf16[4,256,1,128]{3,2,1,0:T(2,128)(2,1)} %get-tuple-element.228) | copy-start | bytes 786436
  15.9 17.4 %copy-start.1 = (bf16[4,256,1,128]{3,2,1,0:T(2,128)(2,1)S(1)}, bf16[4,256,1,128]{3,2,1,0:T(2,128)(2,1)}, u32[]{:S(2)}) copy-start(bf16[4,256,1,128]{3,2,1,0:T(2,128)(2,1)} %get-tuple-element.222) | copy-start | bytes 786436
Sparse Core Ops, SparseCore 0:
  10.4 69.4 all-gather.2
  82.0 194.7 all-gather.4
where the time goes:
time: 440 us; the launch traced here: 437 us
  waiting for transfers between devices  223 us (51%)
  matrix products  92.5 us (21%)
  local copies, waits for them, and re-layouts  63.5 us (14%)
  other arithmetic  39.9 us (9%)
  between operations  13.7 us (3%)
    all_gather x1, waiting for transfers between devices, body(): portion = lax.all_gather(pool_kv, 'comp', axis=0, tiled=True)  178 us
    all_gather x1, waiting for transfers between devices, body(): lax.all_gather(sys_kv, ('prompt', 'comp'), axis=0, tiled=True)  45.4 us
    dot_general x144, matrix products, attend_shared(): jnp.einsum('qd,nd->qn', head_rows[head], key_rows, preferred_element_type...  45.1 us
    squeeze x32, local copies, waits for them, and re-layouts, blockwise(): running, unused = lax.scan(advance_masked, running, (blocks, mask_rows))  41.7 us
    dot_general x144, matrix products, product(): return jnp.dot(rounded, value_rows, preferred_element_type=jnp.float32)  38.5 us
    reduce_sum x152, other arithmetic, head_update(): new_total = old_total * factor + jnp.sum(weights, axis=-1)  32.2 us
  transfers between devices with their start and end apart: 2, of which 2 were waited for; matrix products, arithmetic and copies ran while one was open for 10% of the time, Pallas kernels for 0%

commit v1 on v0

v1 whole, which is shorter than its diff:
```python
import functools

import jax
import jax.numpy as jnp
from jax import lax
from jax.experimental import pallas as pl
from jax.experimental.pallas import tpu as pltpu
from jax.sharding import PartitionSpec as P

QH = 64
KVH = 4
HD = 128
GQ = QH // KVH
SIDE = 4
BLK = 128
ROWS = 192
MSG = ROWS + 16
SYS_PART = 32
POOL_TOK = 512
ALL_TOK = 5 * POOL_TOK
AXES = ("prompt", "comp")
FLOOR = -1e30
SCALE2 = HD**-0.5 * 1.4426950408889634
BF = jnp.bfloat16
F32 = jnp.float32
NT = (((1,), (1,)), ((), ()))
PARAMS = pltpu.CompilerParams(vmem_limit_bytes=56 * 2**20)
SMEM = pl.BlockSpec(memory_space=pltpu.SMEM)
VMEM = pl.BlockSpec(memory_space=pltpu.VMEM)


def ring_pairs(prompts, role, step):
    pairs = []
    for p in range(prompts):
        along_x = (p % 2 == 0) == (role == "a")
        for y in range(SIDE):
            for x in range(SIDE):
                ty = y if along_x else (y + step) % SIDE
                tx = (x + step) % SIDE if along_x else x
                base = p * SIDE * SIDE
                pairs.append((base + y * SIDE + x, base + ty * SIDE + tx))
    return pairs


def row_pairs(prompts, step):
    count = SIDE * SIDE
    return [(p * count + c, p * count + (c + step * SIDE) % count) for p in range(prompts) for c in range(count)]


def prompt_pairs(prompts, bit):
    count = SIDE * SIDE
    return [(p * count + c, (p ^ bit) * count + c) for p in range(prompts) for c in range(count)]


def turned(meta_ref, k):
    return lax.rem(meta_ref[2] + k, SIDE)


def query_kernel(meta_ref, q_ref, sys_ref, far_ref, o0, o1, o2, o3, tmp, sys_tmp):
    for k, out in enumerate((o0, o1, o2, o3)):
        head = turned(meta_ref, k)
        for t in range(3):
            for g in range(GQ):
                at = pl.ds(pl.multiple_of((head * GQ + g) * HD, HD), HD)
                tmp[pl.ds(t * 64 + g * 4, 4), :] = q_ref[t, :, at].astype(F32)
        out[pl.ds(0, ROWS), :] = tmp[...].astype(BF)
        lanes = pl.ds(pl.multiple_of(head * HD, HD), HD)
        sys_tmp[pl.ds(0, SYS_PART), :] = sys_ref[:, :, lanes].reshape(SYS_PART, HD).astype(F32)
        sys_tmp[pl.ds(SYS_PART, SYS_PART), :] = far_ref[:, :, lanes].reshape(SYS_PART, HD).astype(F32)
        out[pl.ds(ROWS, SYS_PART), :] = sys_tmp[pl.ds(0, SYS_PART, stride=2), :].astype(BF)
        out[pl.ds(ROWS + SYS_PART, SYS_PART), :] = sys_tmp[pl.ds(1, SYS_PART, stride=2), :].astype(BF)


def stage_kernel(m0, m1, m2, m3, stage_ref, sys_ref):
    for k, msg in enumerate((m0, m1, m2, m3)):
        stage_ref[k] = msg[pl.ds(0, ROWS), :]
        for side in range(2):
            at = pl.ds(k * SYS_PART, SYS_PART)
            sys_ref[0, side, at, :] = msg[pl.ds(ROWS + side * SYS_PART, SYS_PART), :]


def flatten_rows(lse):
    lane = lax.broadcasted_iota(jnp.int32, (BLK, HD), 1)
    row = lax.broadcasted_iota(jnp.int32, (BLK, HD), 0)
    rest = ROWS - BLK
    upper = jnp.sum(jnp.where(lane == row, lse[:BLK], 0.0), axis=0, keepdims=True)
    lower = jnp.sum(jnp.where((lane == row)[:rest], lse[BLK:], 0.0), axis=0, keepdims=True)
    return jnp.concatenate([upper, lower], axis=0)


def pack_flat(flat):
    hi = flat.astype(BF).astype(F32)
    mid = (flat - hi).astype(BF).astype(F32)
    low = flat - hi - mid
    return jnp.concatenate([hi, mid, low, jnp.zeros((10, HD), F32)], axis=0).astype(BF)


def unpack_flat(packed):
    wide = packed.astype(F32)
    return wide[0:2] + wide[2:4] + wide[4:6]


def weigh(flats):
    top = functools.reduce(jnp.maximum, flats)
    weights = [jnp.exp2(one - top) for one in flats]
    total = functools.reduce(jnp.add, weights)
    return [w / total for w in weights], top + jnp.log2(total)


def mix_all(weights, outs):
    flat = [w for group in weights for w in group]
    rows = 2 * len(flat)
    stacked = jnp.concatenate(flat + [jnp.zeros((HD - rows, HD), F32)], axis=0)
    columns = stacked.T
    mixed = []
    n = 0
    for group in outs:
        upper = lower = 0.0
        for one in group:
            upper = upper + columns[:, n : n + 1] * one[:BLK]
            lower = lower + columns[: ROWS - BLK, n + 1 : n + 2] * one[BLK:]
            n += 2
        mixed.append(jnp.concatenate([upper, lower], axis=0))
    return mixed


def main_kernel(meta_ref, code_ref, *refs):
    q_refs, pieces, sys_refs, o_refs, refs = refs[:4], refs[4:8], refs[8:10], refs[10:14], refs[14:]
    kc, vc, bias, q_all, o_all, tmp = refs
    j = pl.program_id(0)

    @pl.when(j == 0)
    def _():
        for n, ref in enumerate(q_refs):
            q_all[n] = ref[...]
        for p in range(2):
            vc[p, :, pl.ds(HD, HD)] = jnp.ones((ALL_TOK, HD), BF)
            for n in range(4):
                at = pl.ds(4 * POOL_TOK + n * BLK, BLK)
                kc[p, at, :] = sys_refs[n // 2][n % 2, 0]
                vc[p, at, pl.ds(0, HD)] = sys_refs[n // 2][n % 2, 1]
                bias[p, 16 + n] = jnp.zeros((8, HD), F32)
        for k, ref in enumerate(pieces):
            held = tmp.at[k % 2]
            held[...] = ref[...].astype(F32)
            n0, n1 = jnp.int32(0), jnp.int32(0)
            for blk in range(8):
                code = code_ref[meta_ref[3 + k] + blk]
                prompt = code // 2
                rank = k * 4 + jnp.minimum(jnp.where(prompt == 0, n0, n1), 3)
                at = pl.ds(pl.multiple_of(rank * BLK, BLK), BLK)
                kc[prompt, at, :] = held[pl.ds(blk * 2 * BLK, BLK, stride=2), :].astype(BF)
                vc[prompt, at, pl.ds(0, HD)] = held[pl.ds(blk * 2 * BLK + 1, BLK, stride=2), :].astype(BF)
                dead = jnp.where(code % 2 == 1, 0.0, FLOOR)
                bias[prompt, rank] = jnp.full((8, HD), dead, F32)
                n0 = n0 + 1 - prompt
                n1 = n1 + prompt

    def prompt_of(k):
        shift = jnp.where(meta_ref[7] == 0, j, k)
        return lax.rem(meta_ref[0] - shift + SIDE, SIDE) // 2

    def scores(k):
        p = prompt_of(k)
        s = lax.dot_general(q_all[j, k], kc[p], NT, preferred_element_type=F32)
        return s + jnp.concatenate([bias[p, n, :1, :] for n in range(20)], axis=1)

    def finish(k, s):
        m = jnp.max(s, axis=1, keepdims=True)
        w = jnp.exp2((s - m) * SCALE2).astype(BF)
        acc = jnp.dot(w, vc[prompt_of(k)], preferred_element_type=F32)
        total = acc[:, HD:]
        o_all[k, pl.ds(0, ROWS), :] = (acc[:, :HD] / total).astype(BF)
        o_all[k, pl.ds(ROWS, 16), :] = pack_flat(flatten_rows(m * SCALE2 + jnp.log2(total)))

    s = scores(0)
    for k in range(SIDE):
        following = scores(k + 1) if k + 1 < SIDE else None
        finish(k, s)
        s = following
    for n, ref in enumerate(o_refs):

        @pl.when(j == n)
        def _():
            ref[...] = o_all[...]


def own_kernel(lens_ref, q0, q1, q2, q3, s0, s1, s2, s3, new_ref, o_ref, lse_ref, bias, tmp, vc):
    tokens = vc.shape[1]
    comp = lax.broadcasted_iota(jnp.int32, (ROWS, 256), 0) % 4
    place = lax.broadcasted_iota(jnp.int32, (ROWS, 256), 1)
    for c in range(4):
        live = (comp == c) & (place < lens_ref[c])
        bias[:, pl.ds(c * 256, 256)] = jnp.where(live, 0.0, FLOOR)
    row = lax.broadcasted_iota(jnp.int32, (ROWS, BLK), 0)
    col = lax.broadcasted_iota(jnp.int32, (ROWS, BLK), 1)
    fresh = col - (row % 4) * 3
    bias[:, pl.ds(1024, BLK)] = jnp.where((fresh >= 0) & (fresh < 3) & (fresh <= row // 64), 0.0, FLOOR)
    for n in range(2):
        vc[n, :, pl.ds(HD, HD)] = jnp.ones((tokens, HD), BF)
        tmp[n, pl.ds(2048, 256), :] = jnp.zeros((256, HD), F32)

    def scores(k, q_ref, kv_ref):
        held = tmp.at[k % 2]
        held[pl.ds(0, 2048), :] = kv_ref[...].astype(F32)
        held[pl.ds(2048, 24), :] = new_ref[k].astype(F32)
        key = held[pl.ds(0, tokens, stride=2), :].astype(BF)
        vc[k % 2, :, pl.ds(0, HD)] = held[pl.ds(1, tokens, stride=2), :].astype(BF)
        s = lax.dot_general(q_ref[pl.ds(0, ROWS), :], key, NT, preferred_element_type=F32)
        return s + bias[...]

    def finish(k, s):
        m = jnp.max(s, axis=1, keepdims=True)
        w = jnp.exp2((s - m) * SCALE2).astype(BF)
        acc = jnp.dot(w, vc[k % 2], preferred_element_type=F32)
        total = acc[:, HD:]
        o_ref[k] = acc[:, :HD] / total
        lse_ref[k, pl.ds(0, 2), :] = flatten_rows(m * SCALE2 + jnp.log2(total))

    q_refs, kv_refs = (q0, q1, q2, q3), (s0, s1, s2, s3)
    s = scores(0, q0, s0)
    for k in range(KVH):
        following = scores(k + 1, q_refs[k + 1], kv_refs[k + 1]) if k + 1 < KVH else None
        finish(k, s)
        s = following


def combine_kernel(c0, c1, c2, c3, o0, o1, o2, o3):
    parts = (c0, c1, c2, c3)
    weights = []
    for k, out in enumerate((o0, o1, o2, o3)):
        group, lse = weigh([unpack_flat(ref[k, pl.ds(ROWS, 16), :]) for ref in parts])
        weights.append(group)
        out[pl.ds(ROWS, 16), :] = pack_flat(lse)
    outs = [[ref[k, pl.ds(0, ROWS), :].astype(F32) for ref in parts] for k in range(SIDE)]
    for out, mixed in zip((o0, o1, o2, o3), mix_all(weights, outs)):
        out[pl.ds(0, ROWS), :] = mixed.astype(BF)


def final_kernel(meta_ref, r0, r1, r2, r3, own_ref, lse_ref, out_ref):
    refs = (r0, r1, r2, r3)
    weights = [
        weigh([unpack_flat(ref[pl.ds(ROWS, 16), :]), lse_ref[k, pl.ds(0, 2), :]])[0] for k, ref in enumerate(refs)
    ]
    outs = [[ref[pl.ds(0, ROWS), :].astype(F32), own_ref[k]] for k, ref in enumerate(refs)]
    for k, mixed in enumerate(mix_all(weights, outs)):
        head = turned(meta_ref, k)
        for t in range(3):
            out_ref[t, head] = mixed[t * 64 : (t + 1) * 64].astype(BF)


def cost(flops, size, exps=0):
    return pl.CostEstimate(flops=flops, bytes_accessed=size, transcendentals=exps)


def shaped(shape, dtype=BF):
    return jax.ShapeDtypeStruct(shape, dtype)


def whole(array):
    return pl.BlockSpec(array.shape, lambda *_: (0,) * array.ndim)


def body(queries, new_kv, suffix_kv, suffix_len, pool_kv, sys_kv, block_slot, block_list, prefix_blocks):
    prompts = lax.axis_size("prompt")
    me_p = lax.axis_index("prompt")
    me_c = lax.axis_index("comp")
    y, x = me_c // SIDE, me_c % SIDE
    core = me_p % 2
    even = core == 0
    a = jnp.where(even, x, y)

    def send(array, role, step):
        return lax.ppermute(array, AXES, ring_pairs(prompts, role, step % SIDE))

    def source(k):
        return jnp.where(even, y * SIDE + (x - k + SIDE) % SIDE, ((y - k + SIDE) % SIDE) * SIDE + x) * 8

    zero = jnp.int32(0)
    meta = jnp.stack([y, x, a, source(0), source(1), source(2), source(3), core, zero]).astype(jnp.int32)

    far_sys = lax.ppermute(sys_kv, AXES, prompt_pairs(prompts, 1))
    places = jnp.arange(128, dtype=jnp.int32)
    listed = jnp.where(places[None, :64] < prefix_blocks[:1, None], block_list[:1], -1)
    far_listed = lax.ppermute(listed, AXES, row_pairs(prompts, 2))

    def one_head(array, k):
        return lax.dynamic_slice_in_dim(array, ((a + k) % SIDE) * HD, HD, array.ndim - 1).reshape(-1, HD)

    pieces = [one_head(pool_kv, 0)] + [send(one_head(pool_kv, k), "a", k) for k in (1, 2, 3)]

    q_msgs = pl.pallas_call(
        query_kernel,
        in_specs=[SMEM, VMEM, VMEM, VMEM],
        out_specs=[VMEM] * 4,
        out_shape=[shaped((ROWS + 2 * SYS_PART, HD))] * 4,
        scratch_shapes=[pltpu.VMEM((ROWS, HD), F32), pltpu.VMEM((2 * SYS_PART, HD), F32)],
        compiler_params=PARAMS,
        cost_estimate=cost(0, 2**19),
        name="query_messages",
    )(meta, queries.transpose(1, 0, 2), sys_kv, far_sys)
    q_got = [q_msgs[0]] + [send(q_msgs[k], "a", k) for k in (1, 2, 3)]
    stage, sys_one = pl.pallas_call(
        stage_kernel,
        in_specs=[VMEM] * 4,
        out_specs=[VMEM] * 2,
        out_shape=[shaped((SIDE, ROWS, HD)), shaped((1, 2, BLK, HD))],
        compiler_params=PARAMS,
        cost_estimate=cost(0, 2**19),
        name="stage",
    )(*q_got)
    columns = [stage] + [send(stage, "b", j) for j in (1, 2, 3)]
    sys_two = jnp.concatenate([sys_one, lax.ppermute(sys_one, AXES, prompt_pairs(prompts, 2))])
    sys_far = lax.ppermute(sys_two, AXES, prompt_pairs(prompts, 4))

    at_slot = block_slot[0][:, None] == places
    mine_first = y < 2
    both = jnp.where(
        mine_first, jnp.concatenate([listed, far_listed], axis=1), jnp.concatenate([far_listed, listed], axis=1)
    )
    used = jnp.any(both[0][:, None] == places, axis=0)
    mark = jnp.where(used, 1, 0) + jnp.where(places >= 64, 2, 0)
    code = jnp.sum(jnp.where(at_slot, mark[:, None], 0), axis=0)

    new_heads = jnp.stack([one_head(new_kv, k) for k in range(KVH)])
    own_out, own_lse = pl.pallas_call(
        own_kernel,
        in_specs=[SMEM] + [VMEM] * 9,
        out_specs=[VMEM] * 2,
        out_shape=[shaped((KVH, ROWS, HD), F32), shaped((KVH, 8, HD), F32)],
        scratch_shapes=[
            pltpu.VMEM((ROWS, 1024 + BLK), F32),
            pltpu.VMEM((2, 2048 + 2 * BLK, HD), F32),
            pltpu.VMEM((2, 1024 + BLK, 2 * HD), BF),
        ],
        compiler_params=PARAMS,
        cost_estimate=cost(2**30, 2**22, 2**20),
        name="own_tokens",
    )(suffix_len, *q_msgs, *[one_head(suffix_kv, k) for k in range(KVH)], new_heads)
    code, own_lse = lax.optimization_barrier((code, own_lse))

    operands = [*columns, *pieces, sys_two, sys_far]
    parts = pl.pallas_call(
        main_kernel,
        grid_spec=pltpu.PrefetchScalarGridSpec(
            num_scalar_prefetch=2,
            grid=(SIDE,),
            in_specs=[whole(one) for one in operands],
            out_specs=[pl.BlockSpec((SIDE, MSG, HD), lambda *_: (0, 0, 0))] * SIDE,
            scratch_shapes=[
                pltpu.VMEM((2, ALL_TOK, HD), BF),
                pltpu.VMEM((2, ALL_TOK, 2 * HD), BF),
                pltpu.VMEM((2, 20, 8, HD), F32),
                pltpu.VMEM((SIDE, SIDE, ROWS, HD), BF),
                pltpu.VMEM((SIDE, MSG, HD), BF),
                pltpu.VMEM((2, 2048, HD), F32),
            ],
        ),
        out_shape=[shaped((SIDE, MSG, HD))] * SIDE,
        compiler_params=PARAMS,
        cost_estimate=cost(2**33, 2**22, 2**23),
        name="attend",
    )(meta, code, *operands)
    parts = [parts[0]] + [send(parts[j], "b", -j) for j in (1, 2, 3)]
    back = pl.pallas_call(
        combine_kernel,
        in_specs=[VMEM] * 4,
        out_specs=[VMEM] * 4,
        out_shape=[shaped((MSG, HD))] * 4,
        compiler_params=PARAMS,
        cost_estimate=cost(0, 2**20),
        name="combine",
    )(*parts)
    heads = [back[0]] + [send(back[k], "a", -k) for k in (1, 2, 3)]
    out = pl.pallas_call(
        final_kernel,
        in_specs=[SMEM] + [VMEM] * 6,
        out_specs=VMEM,
        out_shape=shaped((3, KVH, 64, HD)),
        compiler_params=PARAMS,
        name="final",
    )(meta, *heads, own_out, own_lse)
    return out.reshape(3, KVH, GQ, 4, HD).transpose(3, 0, 1, 2, 4).reshape(4, 3, QH * HD)


def solution(mesh):
    both = P(AXES)
    in_specs = (both,) * 6 + (P("prompt"), both, both)
    return jax.shard_map(body, mesh=mesh, in_specs=in_specs, out_specs=both, check_vma=False)
```

time: 440 us -> 93 us (0.21)
  waiting for transfers between devices: 223 us -> 20.5 us
  matrix products: 92.5 us -> 0 us
  local copies, waits for them, and re-layouts: 63.5 us -> 12.5 us
  other arithmetic: 39.9 us -> 3.45 us
  Pallas kernels: 0 us -> 28.1 us
  starting transfers between devices: 0.04 us -> 27.6 us
  between operations: 13.7 us -> 0.14 us
    all_gather x2 -> x0, waiting for transfers between devices: 223 us -> none  [the longest x1 178 us: body(): portion = lax.all_gather(pool_kv, 'comp', axis=0, tiled=True)]
    dot_general x304 -> x0, matrix products: 92.5 us -> none  [the longest x144 45.1 us: attend_shared(): jnp.einsum('qd,nd->qn', head_rows[head], key_rows, preferred_element_type...]
    squeeze x36 -> x0, local copies, waits for them, and re-layouts: 47.1 us -> none  [the longest x32 41.7 us: blockwise(): running, unused = lax.scan(advance_masked, running, (blocks, mask_rows))]
    reduce_sum x153 -> x1, other arithmetic: 33.1 us -> 0.62 us  [body(): code = jnp.sum(jnp.where(at_slot, mark[:, None], 0), axis=0)]
    pallas_call x0 -> x6, Pallas kernels: none -> 28.1 us  [the longest x1 15.3 us: body(): pl.pallas_call(main_kernel, grid_spec=pltpu.PrefetchScalarGridSpec(num_sc...]
    ppermute x0 -> x19, starting transfers between devices: none -> 27.6 us  [the longest x15 18.4 us: send(): return lax.ppermute(array, AXES, ring_pairs(prompts, role, step % SIDE))]
    ppermute x0 -> x19, waiting for transfers between devices: none -> 20.5 us  [the longest x15 16.9 us: send(): return lax.ppermute(array, AXES, ring_pairs(prompts, role, step % SIDE))]
    dynamic_slice x0 -> x3, local copies, waits for them, and re-layouts: none -> 7.61 us  [one_head(): lax.dynamic_slice_in_dim(array, (a + k) % SIDE * HD, HD, array.ndim - 1)]
  transfers between devices with their start and end apart: 2 -> 19, of which waited for: 2 -> 11; matrix products, arithmetic and copies ran while one was open for 10% -> 12% of each run, Pallas kernels for 0% -> 9%
where the time goes in v1:
time: 93 us; the launch traced here: 92.3 us
  Pallas kernels  28.1 us (30%)
  starting transfers between devices  27.6 us (30%)
  waiting for transfers between devices  20.5 us (22%)
  local copies, waits for them, and re-layouts  12.5 us (13%)
  other arithmetic  3.45 us (4%)
    ppermute x15, starting transfers between devices, send(): return lax.ppermute(array, AXES, ring_pairs(prompts, role, step % SIDE))  18.4 us
    ppermute x15, waiting for transfers between devices, send(): return lax.ppermute(array, AXES, ring_pairs(prompts, role, step % SIDE))  16.9 us
    pallas_call x1, Pallas kernels, body(): pl.pallas_call(main_kernel, grid_spec=pltpu.PrefetchScalarGridSpec(num_sc...  15.3 us
    dynamic_slice x3, local copies, waits for them, and re-layouts, one_head(): lax.dynamic_slice_in_dim(array, (a + k) % SIDE * HD, HD, array.ndim - 1)  7.61 us
    pallas_call x1, Pallas kernels, body(): pl.pallas_call(own_kernel, in_specs=[SMEM] + [VMEM] * 9, out_specs=[VMEM]...  4.64 us
    unnamed x41, local copies, waits for them, and re-layouts  4.25 us
    ppermute x1, starting transfers between devices, body(): sys_far = lax.ppermute(sys_two, AXES, prompt_pairs(prompts, 4))  3.96 us
    ppermute x1, starting transfers between devices, body(): far_listed = lax.ppermute(listed, AXES, row_pairs(prompts, 2))  3.28 us
  transfers between devices with their start and end apart: 19, of which 11 were waited for; matrix products, arithmetic and copies ran while one was open for 12% of the time, Pallas kernels for 9%

profile of v1, /device:TPU:0, one launch (start us, length us, event | category | flops | bytes accessed | tf_op | source)
XLA Modules:
  0.0 92.3 jit_solution(8123123241587534326)
XLA Ops:
  0.0 1.3 %bitcast_select_fusion = s32[1,64]{1,0:T(1,128)S(1)} fusion(s32[4,64]{1,0:T(4,128)} %param.16, s32[128]{0:T(128)S(1)} %iota.10, s32[]{:T(128)} %bitcast.48), kind=kLoop, calls=%fused_computation.19 | loop fusion | flops 128 | bytes 772 | tf_op jit(solution)/shard_map/jit(_where)/select_n | solution.py:284
  1.3 3.3 %collective-permute-start = (s32[1,64]{1,0:T(1,128)S(1)}, s32[1,64]{1,0:T(1,128)S(1)}, u32[]{:S(2)}, u32[]{:S(2)}) collective-permute-start(s32[1,64]{1,0:T(1,128)S(1)} %bitcast_select_fusion), channel_id=1, source_target_pairs={{0,8},{1,9},{2,10},{3,11},{4,12},{5,13},{6,14},{7,15},{8,0},{9,1},... | collective-permute-start | bytes 776 | tf_op jit(solution)/shard_map/ppermute | solution.py:285
  4.6 4.7 %constant_dynamic-slice_fusion = (bf16[8,128,2,128]{3,2,1,0:T(2,128)(2,1)S(1)}, bf16[8,128,2,128]{3,2,1,0:T(2,128)(2,1)}, bf16[8,128,2,128]{3,2,1,0:T(2,128)(2,1)}, bf16[8,128,2,128]{3,2,1,0:T(2,128)(2,1)S(1)}) fusion(bf16[8,128,2,512]{3,2,1,0:T(2,128)(2,1)} %param.13, s32[]{:T(128)S(6)} %select_n.180, s32[]{:T(128)S(6)} %select_n.176, s32[]{:T(128)S(6)} %select_n.174, ...), kind=kLoop, calls=%fused_computation.7 | loop fusion | bytes 4194320 | tf_op jit(solution)/shard_map/dynamic_slice | solution.py:288
  9.3 1.5 %collective-permute-start.8 = (bf16[2048,128]{1,0:T(8,128)(2,1)}, bf16[2048,128]{1,0:T(8,128)(2,1)}, u32[]{:S(2)}, u32[]{:S(2)}) collective-permute-start(bf16[2048,128]{1,0:T(8,128)(2,1)} %bitcast.23), channel_id=1, source_target_pairs={{0,1},{1,2},{2,3},{3,0},{4,5},{5,6},{6,7},{7,4},{8,9},{9,10},{10,1... | collective-permute-start | bytes 1572872 | tf_op jit(solution)/shard_map/ppermute | solution.py:274
  10.8 1.7 %collective-permute-start.10 = (bf16[2048,128]{1,0:T(8,128)(2,1)S(1)}, bf16[2048,128]{1,0:T(8,128)(2,1)}, u32[]{:S(2)}, u32[]{:S(2)}) collective-permute-start(bf16[2048,128]{1,0:T(8,128)(2,1)S(1)} %bitcast.38), channel_id=1, source_target_pairs={{0,3},{1,0},{2,1},{3,2},{4,7},{5,4},{6,5},{7,6},{8,11},{9,8},{10,9... | collective-permute-start | bytes 1572872 | tf_op jit(solution)/shard_map/ppermute | solution.py:274
  13.3 2.9 %constant_dynamic-slice_fusion.8 = (bf16[4,256,2,128]{3,2,1,0:T(2,128)(2,1)}, bf16[4,256,2,128]{3,2,1,0:T(2,128)(2,1)}, bf16[4,256,2,128]{3,2,1,0:T(2,128)(2,1)}, bf16[4,256,2,128]{3,2,1,0:T(2,128)(2,1)}) fusion(bf16[4,256,2,512]{3,2,1,0:T(2,128)(2,1)S(1)} %copy-done, s32[]{:T(128)S(6)} %select_n.180, s32[]{:T(128)S(6)} %select_n.176, s32[]{:T(128)S(6)} %select_n.174, ...), kind=kLoop, calls=%fused_computation.15 | loop fusion | bytes 4194320 | tf_op jit(solution)/shard_map/dynamic_slice | solution.py:288
  18.2 1.8 %query_messages.1 = (bf16[256,128]{1,0:T(8,128)(2,1)}, bf16[256,128]{1,0:T(8,128)(2,1)}, bf16[256,128]{1,0:T(8,128)(2,1)}, bf16[256,128]{1,0:T(8,128)(2,1)}) custom-call(s32[9]{0:T(128)} %stack.38.meta_ref, bf16[3,4,8192]{2,1,0:T(4,128)(2,1)} %bitcast.43, bf16[16,2,512]{2,1,0:T(2,128)(2,1)} %sys_ref.1, bf16[16,2,512]{2,1,0:T(2,128)(2,1)} %copy-done.11), custom_call_target="tpu_custom_call" | custom-call | bytes 524288 | tf_op jit(solution)/shard_map/query_messages/pallas_call | solution.py:292
  20.2 2.7 %collective-permute-start.3 = (bf16[256,128]{1,0:T(8,128)(2,1)}, bf16[256,128]{1,0:T(8,128)(2,1)S(1)}, u32[]{:S(2)}, u32[]{:S(2)}) collective-permute-start(bf16[256,128]{1,0:T(8,128)(2,1)} %get-tuple-element.25.q2), channel_id=1, source_target_pairs={{0,2},{1,3},{2,0},{3,1},{4,6},{5,7},{6,4},{7,5},{8,10},{9,11},{10,... | collective-permute-start | bytes 196616 | tf_op jit(solution)/shard_map/ppermute | solution.py:274
  23.0 1.4 %collective-permute-start.4 = (bf16[256,128]{1,0:T(8,128)(2,1)}, bf16[256,128]{1,0:T(8,128)(2,1)S(1)}, u32[]{:S(2)}, u32[]{:S(2)}) collective-permute-start(bf16[256,128]{1,0:T(8,128)(2,1)} %get-tuple-element.26.q3), channel_id=1, source_target_pairs={{0,3},{1,0},{2,1},{3,2},{4,7},{5,4},{6,5},{7,6},{8,11},{9,8},{10,9... | collective-permute-start | bytes 196616 | tf_op jit(solution)/shard_map/ppermute | solution.py:274
  24.5 1.8 %collective-permute-done.2.m1 = bf16[256,128]{1,0:T(8,128)(2,1)S(1)} collective-permute-done((bf16[256,128]{1,0:T(8,128)(2,1)}, bf16[256,128]{1,0:T(8,128)(2,1)S(1)}, u32[]{:S(2)}, u32[]{:S(2)}) %collective-permute-start.2) | collective-permute-done | bytes 65568 | tf_op jit(solution)/shard_map/ppermute | solution.py:274
  26.4 1.1 %collective-permute-done.4.m3 = bf16[256,128]{1,0:T(8,128)(2,1)S(1)} collective-permute-done((bf16[256,128]{1,0:T(8,128)(2,1)}, bf16[256,128]{1,0:T(8,128)(2,1)S(1)}, u32[]{:S(2)}, u32[]{:S(2)}) %collective-permute-start.4) | collective-permute-done | bytes 65568 | tf_op jit(solution)/shard_map/ppermute | solution.py:274
  28.1 1.6 %stage.1 = (bf16[4,192,128]{2,1,0:T(8,128)(2,1)}, bf16[1,2,128,128]{3,2,1,0:T(8,128)(2,1)}) custom-call(bf16[256,128]{1,0:T(8,128)(2,1)} %get-tuple-element.23.q0.m0, bf16[256,128]{1,0:T(8,128)(2,1)} %copy-done.4, bf16[256,128]{1,0:T(8,128)(2,1)} %copy-done.5, bf16[256,128]{1,0:T(8,128)(2,1)} %copy-done.6), custom_call_target="tpu_custom_call" | custom-call | bytes 524288 | tf_op jit(solution)/shard_map/stage/pallas_call | solution.py:303
  29.7 1.9 %collective-permute-start.11 = (bf16[1,2,128,128]{3,2,1,0:T(8,128)(2,1)}, bf16[1,2,128,128]{3,2,1,0:T(8,128)(2,1)S(1)}, u32[]{:S(2)}, u32[]{:S(2)}) collective-permute-start(bf16[1,2,128,128]{3,2,1,0:T(8,128)(2,1)} %get-tuple-element.30), channel_id=1, source_target_pairs={{0,32},{1,33},{2,34},{3,35},{4,36},{5,37},{6,38},{7,39},{8,40},{9,... | collective-permute-start | bytes 196616 | tf_op jit(solution)/shard_map/ppermute | solution.py:313
  31.6 1.1 %collective-permute-start.7 = (bf16[4,192,128]{2,1,0:T(8,128)(2,1)}, bf16[4,192,128]{2,1,0:T(8,128)(2,1)S(1)}, u32[]{:S(2)}, u32[]{:S(2)}) collective-permute-start(bf16[4,192,128]{2,1,0:T(8,128)(2,1)} %get-tuple-element.29.refs_0_), channel_id=1, source_target_pairs={{0,12},{1,13},{2,14},{3,15},{4,0},{5,1},{6,2},{7,3},{8,4},{9,5},{1... | collective-permute-start | bytes 589832 | tf_op jit(solution)/shard_map/ppermute | solution.py:274
  32.7 0.8 constant_dynamic-update-slice_fusion.1
  34.2 4.0 %collective-permute-start.12 = (bf16[2,2,128,128]{3,2,1,0:T(8,128)(2,1)S(1)}, bf16[2,2,128,128]{3,2,1,0:T(8,128)(2,1)S(1)}, u32[]{:S(2)}, u32[]{:S(2)}) collective-permute-start(bf16[2,2,128,128]{3,2,1,0:T(8,128)(2,1)S(1)} %constant_dynamic-update-slice_fusion.refs_8_), channel_id=1, source_target_pairs={{0,64},{1,65},{2,66},{3,67},{4,68},{5,69},{6,70},{7,71},{8,72},{9,... | collective-permute-start | bytes 393224 | tf_op jit(solution)/shard_map/ppermute | solution.py:314
  38.2 2.9 %collective-permute-done.12.refs_9_ = bf16[2,2,128,128]{3,2,1,0:T(8,128)(2,1)S(1)} collective-permute-done((bf16[2,2,128,128]{3,2,1,0:T(8,128)(2,1)S(1)}, bf16[2,2,128,128]{3,2,1,0:T(8,128)(2,1)S(1)}, u32[]{:S(2)}, u32[]{:S(2)}) %collective-permute-start.12) | collective-permute-done | bytes 131104 | tf_op jit(solution)/shard_map/ppermute | solution.py:314
  41.1 1.9 %collective-permute-start.6 = (bf16[4,192,128]{2,1,0:T(8,128)(2,1)}, bf16[4,192,128]{2,1,0:T(8,128)(2,1)S(1)}, u32[]{:S(2)}, u32[]{:S(2)}) collective-permute-start(bf16[4,192,128]{2,1,0:T(8,128)(2,1)} %get-tuple-element.29.refs_0_), channel_id=1, source_target_pairs={{0,8},{1,9},{2,10},{3,11},{4,12},{5,13},{6,14},{7,15},{8,0},{9,1},... | collective-permute-start | bytes 589832 | tf_op jit(solution)/shard_map/ppermute | solution.py:274
  43.0 0.8 collective-permute-start.5
  44.4 4.6 %own_tokens.1 = (f32[4,192,128]{2,1,0:T(8,128)}, f32[4,8,128]{2,1,0:T(8,128)}) custom-call(s32[4]{0:T(128)} %lens_ref.1, bf16[256,128]{1,0:T(8,128)(2,1)} %get-tuple-element.23.q0.m0, bf16[256,128]{1,0:T(8,128)(2,1)} %get-tuple-element.24.q1, bf16[256,128]{1,0:T(8,128)(2,1)} %get-tuple-element.25.q2, bf16[256,128]{1,0:T(8,128)(2,1)} %get-tuple-element.26.q3, ...), custom_call_target="tpu_custom_call" | custom-call | flops 1073741824 | bytes 4194304 | tf_op jit(solution)/shard_map/own_tokens/pallas_call | solution.py:326
  49.1 1.5 %collective-permute-done.5.refs_1_ = bf16[4,192,128]{2,1,0:T(8,128)(2,1)S(1)} collective-permute-done((bf16[4,192,128]{2,1,0:T(8,128)(2,1)}, bf16[4,192,128]{2,1,0:T(8,128)(2,1)S(1)}, u32[]{:S(2)}, u32[]{:S(2)}) %collective-permute-start.5) | collective-permute-done | bytes 196640 | tf_op jit(solution)/shard_map/ppermute | solution.py:274
  51.5 15.3 %attend.1 = (bf16[4,208,128]{2,1,0:T(8,128)(2,1)}, bf16[4,208,128]{2,1,0:T(8,128)(2,1)}, bf16[4,208,128]{2,1,0:T(8,128)(2,1)}, bf16[4,208,128]{2,1,0:T(8,128)(2,1)}) custom-call(s32[9]{0:T(128)} %stack.38.meta_ref, s32[128]{0:T(128)} %select_reduce_fusion.code_ref, bf16[4,192,128]{2,1,0:T(8,128)(2,1)} %get-tuple-element.29.refs_0_, ...), custom_call_target="tpu_custom_call" | custom-call | flops 8589934592 | bytes 4194304 | tf_op jit(solution)/shard_map/attend/pallas_call | solution.py:343
  66.8 1.0 %collective-permute-start.13 = (bf16[4,208,128]{2,1,0:T(8,128)(2,1)}, bf16[4,208,128]{2,1,0:T(8,128)(2,1)S(1)}, u32[]{:S(2)}, u32[]{:S(2)}) collective-permute-start(bf16[4,208,128]{2,1,0:T(8,128)(2,1)} %get-tuple-element.32), channel_id=1, source_target_pairs={{0,12},{1,13},{2,14},{3,15},{4,0},{5,1},{6,2},{7,3},{8,4},{9,5},{1... | collective-permute-start | bytes 638984 | tf_op jit(solution)/shard_map/ppermute | solution.py:274
  67.7 1.5 %collective-permute-start.14 = (bf16[4,208,128]{2,1,0:T(8,128)(2,1)}, bf16[4,208,128]{2,1,0:T(8,128)(2,1)S(1)}, u32[]{:S(2)}, u32[]{:S(2)}) collective-permute-start(bf16[4,208,128]{2,1,0:T(8,128)(2,1)} %get-tuple-element.33), channel_id=1, source_target_pairs={{0,8},{1,9},{2,10},{3,11},{4,12},{5,13},{6,14},{7,15},{8,0},{9,1},... | collective-permute-start | bytes 638984 | tf_op jit(solution)/shard_map/ppermute | solution.py:274
  69.2 0.8 collective-permute-start.15
  70.1 2.7 %collective-permute-done.13.c1 = bf16[4,208,128]{2,1,0:T(8,128)(2,1)S(1)} collective-permute-done((bf16[4,208,128]{2,1,0:T(8,128)(2,1)}, bf16[4,208,128]{2,1,0:T(8,128)(2,1)S(1)}, u32[]{:S(2)}, u32[]{:S(2)}) %collective-permute-start.13) | collective-permute-done | bytes 213024 | tf_op jit(solution)/shard_map/ppermute | solution.py:274
  72.8 2.6 %collective-permute-done.14.c2 = bf16[4,208,128]{2,1,0:T(8,128)(2,1)S(1)} collective-permute-done((bf16[4,208,128]{2,1,0:T(8,128)(2,1)}, bf16[4,208,128]{2,1,0:T(8,128)(2,1)S(1)}, u32[]{:S(2)}, u32[]{:S(2)}) %collective-permute-start.14) | collective-permute-done | bytes 213024 | tf_op jit(solution)/shard_map/ppermute | solution.py:274
  75.4 2.2 %collective-permute-done.15.c3 = bf16[4,208,128]{2,1,0:T(8,128)(2,1)S(1)} collective-permute-done((bf16[4,208,128]{2,1,0:T(8,128)(2,1)}, bf16[4,208,128]{2,1,0:T(8,128)(2,1)S(1)}, u32[]{:S(2)}, u32[]{:S(2)}) %collective-permute-start.15) | collective-permute-done | bytes 213024 | tf_op jit(solution)/shard_map/ppermute | solution.py:274
  78.3 2.5 %combine.1 = (bf16[208,128]{1,0:T(8,128)(2,1)}, bf16[208,128]{1,0:T(8,128)(2,1)}, bf16[208,128]{1,0:T(8,128)(2,1)}, bf16[208,128]{1,0:T(8,128)(2,1)}) custom-call(bf16[4,208,128]{2,1,0:T(8,128)(2,1)} %get-tuple-element.31.c0, bf16[4,208,128]{2,1,0:T(8,128)(2,1)} %copy-done.1, bf16[4,208,128]{2,1,0:T(8,128)(2,1)} %copy-done.2, bf16[4,208,128]{2,1,0:T(8,128)(2,1)} %copy-done.3), custom_call_target="tpu_custom_call" | custom-call | bytes 1048576 | tf_op jit(solution)/shard_map/combine/pallas_call | solution.py:365
  80.8 2.2 %collective-permute-start.16 = (bf16[208,128]{1,0:T(8,128)(2,1)}, bf16[208,128]{1,0:T(8,128)(2,1)S(1)}, u32[]{:S(2)}, u32[]{:S(2)}) collective-permute-start(bf16[208,128]{1,0:T(8,128)(2,1)} %get-tuple-element.36), channel_id=1, source_target_pairs={{0,3},{1,0},{2,1},{3,2},{4,7},{5,4},{6,5},{7,6},{8,11},{9,8},{10,9... | collective-permute-start | bytes 159752 | tf_op jit(solution)/shard_map/ppermute | solution.py:274
  85.2 3.7 %collective-permute-done.17.r2 = bf16[208,128]{1,0:T(8,128)(2,1)S(1)} collective-permute-done((bf16[208,128]{1,0:T(8,128)(2,1)}, bf16[208,128]{1,0:T(8,128)(2,1)S(1)}, u32[]{:S(2)}, u32[]{:S(2)}) %collective-permute-start.17) | collective-permute-done | bytes 53280 | tf_op jit(solution)/shard_map/ppermute | solution.py:274
  90.1 2.2 %final.1 = bf16[3,4,64,128]{3,2,1,0:T(8,128)(2,1)} custom-call(s32[9]{0:T(128)} %stack.38.meta_ref, bf16[208,128]{1,0:T(8,128)(2,1)} %get-tuple-element.35.r0, bf16[208,128]{1,0:T(8,128)(2,1)} %copy-done.7, bf16[208,128]{1,0:T(8,128)(2,1)} %copy-done.8, bf16[208,128]{1,0:T(8,128)(2,1)} %copy-done.9, f32[4,192,128]{2,1,0:T(8,128)} %get-tuple-element.39.own_ref, ...), custom_call_target="tpu_custom_call" | custom-call | tf_op jit(solution)/shard_map/final/pallas_call | solution.py:375
  (66 shorter events, 9.8 us)
Async XLA Ops:
  1.3 16.1 %collective-permute-start = (s32[1,64]{1,0:T(1,128)S(1)}, s32[1,64]{1,0:T(1,128)S(1)}, u32[]{:S(2)}, u32[]{:S(2)}) collective-permute-start(s32[1,64]{1,0:T(1,128)S(1)} %bitcast_select_fusion), channel_id=1, source_target_pairs={{0,8},{1,9},{2,10},{3,11},{4,12},{5,13},{6,14},{7,15},{8,0},{9,1},... | collective-permute-start | bytes 776 | tf_op jit(solution)/shard_map/ppermute | solution.py:285
  4.6 12.9 %collective-permute-start.1 = (bf16[16,2,512]{2,1,0:T(2,128)(2,1)}, bf16[16,2,512]{2,1,0:T(2,128)(2,1)S(1)}, u32[]{:S(2)}, u32[]{:S(2)}) collective-permute-start(bf16[16,2,512]{2,1,0:T(2,128)(2,1)} %sys_ref.1), channel_id=1, source_target_pairs={{0,16},{1,17},{2,18},{3,19},{4,20},{5,21},{6,22},{7,23},{8,24},{9,... | collective-permute-start | bytes 98312 | tf_op jit(solution)/shard_map/ppermute | solution.py:282
  4.6 8.0 %copy-start.13 = (s32[4]{0:T(128)S(1)}, s32[4]{0:T(128)}, u32[]{:S(2)}) copy-start(s32[4]{0:T(128)} %param.17) | copy-start | bytes 52
  4.6 8.7 %copy-start.12 = (bf16[4,3,2,512]{3,2,1,0:T(2,128)(2,1)S(1)}, bf16[4,3,2,512]{3,2,1,0:T(2,128)(2,1)}, u32[]{:S(2)}) copy-start(bf16[4,3,2,512]{3,2,1,0:T(2,128)(2,1)} %param.10) | copy-start | bytes 73732
  4.6 8.7 %copy-start = (bf16[4,256,2,512]{3,2,1,0:T(2,128)(2,1)S(1)}, bf16[4,256,2,512]{3,2,1,0:T(2,128)(2,1)}, u32[]{:S(2)}) copy-start(bf16[4,256,2,512]{3,2,1,0:T(2,128)(2,1)} %param.11) | copy-start | bytes 6291460
  9.3 41.3 %collective-permute-start.8 = (bf16[2048,128]{1,0:T(8,128)(2,1)}, bf16[2048,128]{1,0:T(8,128)(2,1)}, u32[]{:S(2)}, u32[]{:S(2)}) collective-permute-start(bf16[2048,128]{1,0:T(8,128)(2,1)} %bitcast.23), channel_id=1, source_target_pairs={{0,1},{1,2},{2,3},{3,0},{4,5},{5,6},{6,7},{7,4},{8,9},{9,10},{10,1... | collective-permute-start | bytes 1572872 | tf_op jit(solution)/shard_map/ppermute | solution.py:274
  10.8 39.8 %collective-permute-start.10 = (bf16[2048,128]{1,0:T(8,128)(2,1)S(1)}, bf16[2048,128]{1,0:T(8,128)(2,1)}, u32[]{:S(2)}, u32[]{:S(2)}) collective-permute-start(bf16[2048,128]{1,0:T(8,128)(2,1)S(1)} %bitcast.38), channel_id=1, source_target_pairs={{0,3},{1,0},{2,1},{3,2},{4,7},{5,4},{6,5},{7,6},{8,11},{9,8},{10,9... | collective-permute-start | bytes 1572872 | tf_op jit(solution)/shard_map/ppermute | solution.py:274
  13.3 30.5 %copy-start.19 = (s32[1,128]{1,0:T(1,128)S(1)}, s32[1,128]{1,0:T(1,128)}, u32[]{:S(2)}) copy-start(s32[1,128]{1,0:T(1,128)} %param.15) | copy-start | bytes 1540
  20.0 6.4 %collective-permute-start.2 = (bf16[256,128]{1,0:T(8,128)(2,1)}, bf16[256,128]{1,0:T(8,128)(2,1)S(1)}, u32[]{:S(2)}, u32[]{:S(2)}) collective-permute-start(bf16[256,128]{1,0:T(8,128)(2,1)} %get-tuple-element.24.q1), channel_id=1, source_target_pairs={{0,1},{1,2},{2,3},{3,0},{4,5},{5,6},{6,7},{7,4},{8,9},{9,10},{10,1... | collective-permute-start | bytes 196616 | tf_op jit(solution)/shard_map/ppermute | solution.py:274
  20.2 6.1 %collective-permute-start.3 = (bf16[256,128]{1,0:T(8,128)(2,1)}, bf16[256,128]{1,0:T(8,128)(2,1)S(1)}, u32[]{:S(2)}, u32[]{:S(2)}) collective-permute-start(bf16[256,128]{1,0:T(8,128)(2,1)} %get-tuple-element.25.q2), channel_id=1, source_target_pairs={{0,2},{1,3},{2,0},{3,1},{4,6},{5,7},{6,4},{7,5},{8,10},{9,11},{10,... | collective-permute-start | bytes 196616 | tf_op jit(solution)/shard_map/ppermute | solution.py:274
  23.0 4.5 %collective-permute-start.4 = (bf16[256,128]{1,0:T(8,128)(2,1)}, bf16[256,128]{1,0:T(8,128)(2,1)S(1)}, u32[]{:S(2)}, u32[]{:S(2)}) collective-permute-start(bf16[256,128]{1,0:T(8,128)(2,1)} %get-tuple-element.26.q3), channel_id=1, source_target_pairs={{0,3},{1,0},{2,1},{3,2},{4,7},{5,4},{6,5},{7,6},{8,11},{9,8},{10,9... | collective-permute-start | bytes 196616 | tf_op jit(solution)/shard_map/ppermute | solution.py:274
  26.4 1.1 %copy-start.4 = (bf16[256,128]{1,0:T(8,128)(2,1)}, bf16[256,128]{1,0:T(8,128)(2,1)S(1)}, u32[]{:S(2)}) copy-start(bf16[256,128]{1,0:T(8,128)(2,1)S(1)} %collective-permute-done.2.m1) | copy-start | bytes 196612
  26.4 24.3 %collective-permute-start.9 = (bf16[2048,128]{1,0:T(8,128)(2,1)S(1)}, bf16[2048,128]{1,0:T(8,128)(2,1)S(1)}, u32[]{:S(2)}, u32[]{:S(2)}) collective-permute-start(bf16[2048,128]{1,0:T(8,128)(2,1)S(1)} %bitcast.37), channel_id=1, source_target_pairs={{0,2},{1,3},{2,0},{3,1},{4,6},{5,7},{6,4},{7,5},{8,10},{9,11},{10,... | collective-permute-start | bytes 1572872 | tf_op jit(solution)/shard_map/ppermute | solution.py:274
  26.4 1.1 %copy-start.5 = (bf16[256,128]{1,0:T(8,128)(2,1)}, bf16[256,128]{1,0:T(8,128)(2,1)S(1)}, u32[]{:S(2)}) copy-start(bf16[256,128]{1,0:T(8,128)(2,1)S(1)} %collective-permute-done.3.m2) | copy-start | bytes 196612
  29.7 4.5 %collective-permute-start.11 = (bf16[1,2,128,128]{3,2,1,0:T(8,128)(2,1)}, bf16[1,2,128,128]{3,2,1,0:T(8,128)(2,1)S(1)}, u32[]{:S(2)}, u32[]{:S(2)}) collective-permute-start(bf16[1,2,128,128]{3,2,1,0:T(8,128)(2,1)} %get-tuple-element.30), channel_id=1, source_target_pairs={{0,32},{1,33},{2,34},{3,35},{4,36},{5,37},{6,38},{7,39},{8,40},{9,... | collective-permute-start | bytes 196616 | tf_op jit(solution)/shard_map/ppermute | solution.py:313
  31.6 11.4 %collective-permute-start.7 = (bf16[4,192,128]{2,1,0:T(8,128)(2,1)}, bf16[4,192,128]{2,1,0:T(8,128)(2,1)S(1)}, u32[]{:S(2)}, u32[]{:S(2)}) collective-permute-start(bf16[4,192,128]{2,1,0:T(8,128)(2,1)} %get-tuple-element.29.refs_0_), channel_id=1, source_target_pairs={{0,12},{1,13},{2,14},{3,15},{4,0},{5,1},{6,2},{7,3},{8,4},{9,5},{1... | collective-permute-start | bytes 589832 | tf_op jit(solution)/shard_map/ppermute | solution.py:274
  34.2 16.4 %copy-start.10 = (bf16[2,2,128,128]{3,2,1,0:T(8,128)(2,1)}, bf16[2,2,128,128]{3,2,1,0:T(8,128)(2,1)S(1)}, u32[]{:S(2)}) copy-start(bf16[2,2,128,128]{3,2,1,0:T(8,128)(2,1)S(1)} %constant_dynamic-update-slice_fusion.refs_8_) | copy-start | bytes 393220
  34.2 6.9 %collective-permute-start.12 = (bf16[2,2,128,128]{3,2,1,0:T(8,128)(2,1)S(1)}, bf16[2,2,128,128]{3,2,1,0:T(8,128)(2,1)S(1)}, u32[]{:S(2)}, u32[]{:S(2)}) collective-permute-start(bf16[2,2,128,128]{3,2,1,0:T(8,128)(2,1)S(1)} %constant_dynamic-update-slice_fusion.refs_8_), channel_id=1, source_target_pairs={{0,64},{1,65},{2,66},{3,67},{4,68},{5,69},{6,70},{7,71},{8,72},{9,... | collective-permute-start | bytes 393224 | tf_op jit(solution)/shard_map/ppermute | solution.py:314
  41.1 9.5 %copy-start.18 = (bf16[2,2,128,128]{3,2,1,0:T(8,128)(2,1)}, bf16[2,2,128,128]{3,2,1,0:T(8,128)(2,1)S(1)}, u32[]{:S(2)}) copy-start(bf16[2,2,128,128]{3,2,1,0:T(8,128)(2,1)S(1)} %collective-permute-done.12.refs_9_) | copy-start | bytes 393220
  41.1 8.0 %collective-permute-start.6 = (bf16[4,192,128]{2,1,0:T(8,128)(2,1)}, bf16[4,192,128]{2,1,0:T(8,128)(2,1)S(1)}, u32[]{:S(2)}, u32[]{:S(2)}) collective-permute-start(bf16[4,192,128]{2,1,0:T(8,128)(2,1)} %get-tuple-element.29.refs_0_), channel_id=1, source_target_pairs={{0,8},{1,9},{2,10},{3,11},{4,12},{5,13},{6,14},{7,15},{8,0},{9,1},... | collective-permute-start | bytes 589832 | tf_op jit(solution)/shard_map/ppermute | solution.py:274
  43.0 7.7 %copy-start.15 = (bf16[4,192,128]{2,1,0:T(8,128)(2,1)}, bf16[4,192,128]{2,1,0:T(8,128)(2,1)S(1)}, u32[]{:S(2)}) copy-start(bf16[4,192,128]{2,1,0:T(8,128)(2,1)S(1)} %collective-permute-done.7.refs_3_) | copy-start | bytes 589828
  43.0 7.6 %collective-permute-start.5 = (bf16[4,192,128]{2,1,0:T(8,128)(2,1)}, bf16[4,192,128]{2,1,0:T(8,128)(2,1)S(1)}, u32[]{:S(2)}, u32[]{:S(2)}) collective-permute-start(bf16[4,192,128]{2,1,0:T(8,128)(2,1)} %get-tuple-element.29.refs_0_), channel_id=1, source_target_pairs={{0,4},{1,5},{2,6},{3,7},{4,8},{5,9},{6,10},{7,11},{8,12},{9,13},{1... | collective-permute-start | bytes 589832 | tf_op jit(solution)/shard_map/ppermute | solution.py:274
  49.1 1.6 %copy-start.16 = (bf16[4,192,128]{2,1,0:T(8,128)(2,1)}, bf16[4,192,128]{2,1,0:T(8,128)(2,1)S(1)}, u32[]{:S(2)}) copy-start(bf16[4,192,128]{2,1,0:T(8,128)(2,1)S(1)} %collective-permute-done.6.refs_2_) | copy-start | bytes 589828
  66.8 6.1 %collective-permute-start.13 = (bf16[4,208,128]{2,1,0:T(8,128)(2,1)}, bf16[4,208,128]{2,1,0:T(8,128)(2,1)S(1)}, u32[]{:S(2)}, u32[]{:S(2)}) collective-permute-start(bf16[4,208,128]{2,1,0:T(8,128)(2,1)} %get-tuple-element.32), channel_id=1, source_target_pairs={{0,12},{1,13},{2,14},{3,15},{4,0},{5,1},{6,2},{7,3},{8,4},{9,5},{1... | collective-permute-start | bytes 638984 | tf_op jit(solution)/shard_map/ppermute | solution.py:274
  67.7 7.7 %collective-permute-start.14 = (bf16[4,208,128]{2,1,0:T(8,128)(2,1)}, bf16[4,208,128]{2,1,0:T(8,128)(2,1)S(1)}, u32[]{:S(2)}, u32[]{:S(2)}) collective-permute-start(bf16[4,208,128]{2,1,0:T(8,128)(2,1)} %get-tuple-element.33), channel_id=1, source_target_pairs={{0,8},{1,9},{2,10},{3,11},{4,12},{5,13},{6,14},{7,15},{8,0},{9,1},... | collective-permute-start | bytes 638984 | tf_op jit(solution)/shard_map/ppermute | solution.py:274
  69.2 8.3 %collective-permute-start.15 = (bf16[4,208,128]{2,1,0:T(8,128)(2,1)}, bf16[4,208,128]{2,1,0:T(8,128)(2,1)S(1)}, u32[]{:S(2)}, u32[]{:S(2)}) collective-permute-start(bf16[4,208,128]{2,1,0:T(8,128)(2,1)} %get-tuple-element.34), channel_id=1, source_target_pairs={{0,4},{1,5},{2,6},{3,7},{4,8},{5,9},{6,10},{7,11},{8,12},{9,13},{1... | collective-permute-start | bytes 638984 | tf_op jit(solution)/shard_map/ppermute | solution.py:274
  72.8 4.8 %copy-start.1 = (bf16[4,208,128]{2,1,0:T(8,128)(2,1)}, bf16[4,208,128]{2,1,0:T(8,128)(2,1)S(1)}, u32[]{:S(2)}) copy-start(bf16[4,208,128]{2,1,0:T(8,128)(2,1)S(1)} %collective-permute-done.13.c1) | copy-start | bytes 638980
  75.4 2.2 %copy-start.2 = (bf16[4,208,128]{2,1,0:T(8,128)(2,1)}, bf16[4,208,128]{2,1,0:T(8,128)(2,1)S(1)}, u32[]{:S(2)}) copy-start(bf16[4,208,128]{2,1,0:T(8,128)(2,1)S(1)} %collective-permute-done.14.c2) | copy-start | bytes 638980
  80.8 4.3 %collective-permute-start.16 = (bf16[208,128]{1,0:T(8,128)(2,1)}, bf16[208,128]{1,0:T(8,128)(2,1)S(1)}, u32[]{:S(2)}, u32[]{:S(2)}) collective-permute-start(bf16[208,128]{1,0:T(8,128)(2,1)} %get-tuple-element.36), channel_id=1, source_target_pairs={{0,3},{1,0},{2,1},{3,2},{4,7},{5,4},{6,5},{7,6},{8,11},{9,8},{10,9... | collective-permute-start | bytes 159752 | tf_op jit(solution)/shard_map/ppermute | solution.py:274
  83.1 5.8 %collective-permute-start.17 = (bf16[208,128]{1,0:T(8,128)(2,1)}, bf16[208,128]{1,0:T(8,128)(2,1)S(1)}, u32[]{:S(2)}, u32[]{:S(2)}) collective-permute-start(bf16[208,128]{1,0:T(8,128)(2,1)} %get-tuple-element.37), channel_id=1, source_target_pairs={{0,2},{1,3},{2,0},{3,1},{4,6},{5,7},{6,4},{7,5},{8,10},{9,11},{10,... | collective-permute-start | bytes 159752 | tf_op jit(solution)/shard_map/ppermute | solution.py:274
  83.9 5.6 %collective-permute-start.18 = (bf16[208,128]{1,0:T(8,128)(2,1)}, bf16[208,128]{1,0:T(8,128)(2,1)S(1)}, u32[]{:S(2)}, u32[]{:S(2)}) collective-permute-start(bf16[208,128]{1,0:T(8,128)(2,1)} %get-tuple-element.38), channel_id=1, source_target_pairs={{0,1},{1,2},{2,3},{3,0},{4,5},{5,6},{6,7},{7,4},{8,9},{9,10},{10,1... | collective-permute-start | bytes 159752 | tf_op jit(solution)/shard_map/ppermute | solution.py:274
  85.2 4.3 %copy-start.7 = (bf16[208,128]{1,0:T(8,128)(2,1)}, bf16[208,128]{1,0:T(8,128)(2,1)S(1)}, u32[]{:S(2)}) copy-start(bf16[208,128]{1,0:T(8,128)(2,1)S(1)} %collective-permute-done.16.r1) | copy-start | bytes 159748
  (7 other events, 4.7 us)

commit v2 on v1

--- a/solution.py
+++ b/solution.py
@@ -42,6 +42,20 @@
     return pairs
 
 
+def ring_groups(prompts, role):
+    step = ring_pairs(prompts, role, 1)
+    follow = dict(step)
+    groups = []
+    for p in range(prompts):
+        along_x = (p % 2 == 0) == (role == "a")
+        for n in range(SIDE):
+            group = [p * SIDE * SIDE + (n * SIDE if along_x else n)]
+            while len(group) < SIDE:
+                group.append(follow[group[-1]])
+            groups.append(group)
+    return groups
+
+
 def row_pairs(prompts, step):
     count = SIDE * SIDE
     return [(p * count + c, p * count + (c + step * SIDE) % count) for p in range(prompts) for c in range(count)]
@@ -71,9 +85,9 @@
         out[pl.ds(ROWS + SYS_PART, SYS_PART), :] = sys_tmp[pl.ds(1, SYS_PART, stride=2), :].astype(BF)
 
 
-def stage_kernel(m0, m1, m2, m3, stage_ref, sys_ref):
+def stage_kernel(meta_ref, m0, m1, m2, m3, stage_ref, sys_ref):
     for k, msg in enumerate((m0, m1, m2, m3)):
-        stage_ref[k] = msg[pl.ds(0, ROWS), :]
+        stage_ref[turned(meta_ref, SIDE - k)] = msg[pl.ds(0, ROWS), :]
         for side in range(2):
             at = pl.ds(k * SYS_PART, SYS_PART)
             sys_ref[0, side, at, :] = msg[pl.ds(ROWS + side * SYS_PART, SYS_PART), :]
@@ -124,15 +138,13 @@
     return mixed
 
 
-def main_kernel(meta_ref, code_ref, *refs):
-    q_refs, pieces, sys_refs, o_refs, refs = refs[:4], refs[4:8], refs[8:10], refs[10:14], refs[14:]
-    kc, vc, bias, q_all, o_all, tmp = refs
-    j = pl.program_id(0)
-
-    @pl.when(j == 0)
-    def _():
-        for n, ref in enumerate(q_refs):
-            q_all[n] = ref[...]
+def main_kernel(cols, meta_ref, code_ref, *refs):
+    count = len(cols)
+    q_refs, pool_ref, sys_refs, refs = refs[:count], refs[count], refs[count + 1 : count + 3], refs[count + 3 :]
+    o_refs, (kc, vc, bias, tmp) = refs[:count], refs[count:]
+    pair = 2 * ROWS
+
+    def fill():
         for p in range(2):
             vc[p, :, pl.ds(HD, HD)] = jnp.ones((ALL_TOK, HD), BF)
             for n in range(4):
@@ -140,9 +152,9 @@
                 kc[p, at, :] = sys_refs[n // 2][n % 2, 0]
                 vc[p, at, pl.ds(0, HD)] = sys_refs[n // 2][n % 2, 1]
                 bias[p, 16 + n] = jnp.zeros((8, HD), F32)
-        for k, ref in enumerate(pieces):
+        for k in range(SIDE):
             held = tmp.at[k % 2]
-            held[...] = ref[...].astype(F32)
+            held[...] = pool_ref[k].astype(F32)
             n0, n1 = jnp.int32(0), jnp.int32(0)
             for blk in range(8):
                 code = code_ref[meta_ref[3 + k] + blk]
@@ -156,33 +168,35 @@
                 n0 = n0 + 1 - prompt
                 n1 = n1 + prompt
 
-    def prompt_of(k):
-        shift = jnp.where(meta_ref[7] == 0, j, k)
-        return lax.rem(meta_ref[0] - shift + SIDE, SIDE) // 2
-
-    def scores(k):
-        p = prompt_of(k)
-        s = lax.dot_general(q_all[j, k], kc[p], NT, preferred_element_type=F32)
-        return s + jnp.concatenate([bias[p, n, :1, :] for n in range(20)], axis=1)
-
-    def finish(k, s):
+    def prompt_of(i, n):
+        row = lax.rem(meta_ref[0] - cols[i] + SIDE, SIDE)
+        return jnp.where(meta_ref[7] == 0, row // 2, n)
+
+    def scores(i, n):
+        p = prompt_of(i, n)
+        q = q_refs[i][2 * n : 2 * n + 2].reshape(pair, HD)
+        s = lax.dot_general(q, kc[p], NT, preferred_element_type=F32)
+        return s + jnp.concatenate([bias[p, t, :1, :] for t in range(20)], axis=1)
+
+    def finish(i, n, s):
         m = jnp.max(s, axis=1, keepdims=True)
         w = jnp.exp2((s - m) * SCALE2).astype(BF)
-        acc = jnp.dot(w, vc[prompt_of(k)], preferred_element_type=F32)
+        acc = jnp.dot(w, vc[prompt_of(i, n)], preferred_element_type=F32)
         total = acc[:, HD:]
-        o_all[k, pl.ds(0, ROWS), :] = (acc[:, :HD] / total).astype(BF)
-        o_all[k, pl.ds(ROWS, 16), :] = pack_flat(flatten_rows(m * SCALE2 + jnp.log2(total)))
-
-    s = scores(0)
-    for k in range(SIDE):
-        following = scores(k + 1) if k + 1 < SIDE else None
-        finish(k, s)
+        out = (acc[:, :HD] / total).astype(BF)
+        lse = m * SCALE2 + jnp.log2(total)
+        for half in range(2):
+            part = slice(half * ROWS, (half + 1) * ROWS)
+            o_refs[i][2 * n + half, pl.ds(0, ROWS), :] = out[part]
+            o_refs[i][2 * n + half, pl.ds(ROWS, 16), :] = pack_flat(flatten_rows(lse[part]))
+
+    fill()
+    jobs = [(i, n) for i in range(count) for n in range(2)]
+    s = scores(*jobs[0])
+    for t, job in enumerate(jobs):
+        following = scores(*jobs[t + 1]) if t + 1 < len(jobs) else None
+        finish(*job, s)
         s = following
-    for n, ref in enumerate(o_refs):
-
-        @pl.when(j == n)
-        def _():
-            ref[...] = o_all[...]
 
 
 def own_kernel(lens_ref, q0, q1, q2, q3, s0, s1, s2, s3, new_ref, o_ref, lse_ref, bias, tmp, vc):
@@ -225,14 +239,15 @@
         s = following
 
 
-def combine_kernel(c0, c1, c2, c3, o0, o1, o2, o3):
+def combine_kernel(meta_ref, c0, c1, c2, c3, o0, o1, o2, o3):
     parts = (c0, c1, c2, c3)
-    weights = []
+    weights, outs = [], []
     for k, out in enumerate((o0, o1, o2, o3)):
-        group, lse = weigh([unpack_flat(ref[k, pl.ds(ROWS, 16), :]) for ref in parts])
+        n = turned(meta_ref, SIDE - k)
+        group, lse = weigh([unpack_flat(ref[n, pl.ds(ROWS, 16), :]) for ref in parts])
         weights.append(group)
+        outs.append([ref[n, pl.ds(0, ROWS), :].astype(F32) for ref in parts])
         out[pl.ds(ROWS, 16), :] = pack_flat(lse)
-    outs = [[ref[k, pl.ds(0, ROWS), :].astype(F32) for ref in parts] for k in range(SIDE)]
     for out, mixed in zip((o0, o1, o2, o3), mix_all(weights, outs)):
         out[pl.ds(0, ROWS), :] = mixed.astype(BF)
 
@@ -273,21 +288,17 @@
     def send(array, role, step):
         return lax.ppermute(array, AXES, ring_pairs(prompts, role, step % SIDE))
 
-    def source(k):
-        return jnp.where(even, y * SIDE + (x - k + SIDE) % SIDE, ((y - k + SIDE) % SIDE) * SIDE + x) * 8
+    def source(n):
+        return jnp.where(even, y * SIDE + n, n * SIDE + x) * 8
 
     zero = jnp.int32(0)
     meta = jnp.stack([y, x, a, source(0), source(1), source(2), source(3), core, zero]).astype(jnp.int32)
 
     far_sys = lax.ppermute(sys_kv, AXES, prompt_pairs(prompts, 1))
-    places = jnp.arange(128, dtype=jnp.int32)
-    listed = jnp.where(places[None, :64] < prefix_blocks[:1, None], block_list[:1], -1)
-    far_listed = lax.ppermute(listed, AXES, row_pairs(prompts, 2))
-
     def one_head(array, k):
         return lax.dynamic_slice_in_dim(array, ((a + k) % SIDE) * HD, HD, array.ndim - 1).reshape(-1, HD)
 
-    pieces = [one_head(pool_kv, 0)] + [send(one_head(pool_kv, k), "a", k) for k in (1, 2, 3)]
+    by_head = jnp.stack([pool_kv[..., h * HD : (h + 1) * HD].reshape(-1, HD) for h in range(KVH)])
 
     q_msgs = pl.pallas_call(
         query_kernel,
@@ -299,21 +310,29 @@
         cost_estimate=cost(0, 2**19),
         name="query_messages",
     )(meta, queries.transpose(1, 0, 2), sys_kv, far_sys)
+    q_msgs = list(q_msgs)
+    places = jnp.arange(128, dtype=jnp.int32)
+    block_list, q_msgs[0] = lax.optimization_barrier((block_list, q_msgs[0]))
+    listed = jnp.where(places[None, :64] < prefix_blocks[:1, None], block_list[:1], -1)
+    far_listed = lax.ppermute(listed, AXES, row_pairs(prompts, 2))
     q_got = [q_msgs[0]] + [send(q_msgs[k], "a", k) for k in (1, 2, 3)]
+    by_head, *q_got = lax.optimization_barrier((by_head, *q_got))
+    pool = lax.all_to_all(by_head, AXES, 0, 0, axis_index_groups=ring_groups(prompts, "a"), tiled=True)
     stage, sys_one = pl.pallas_call(
         stage_kernel,
-        in_specs=[VMEM] * 4,
+        in_specs=[SMEM] + [VMEM] * 4,
         out_specs=[VMEM] * 2,
         out_shape=[shaped((SIDE, ROWS, HD)), shaped((1, 2, BLK, HD))],
         compiler_params=PARAMS,
         cost_estimate=cost(0, 2**19),
         name="stage",
-    )(*q_got)
+    )(meta, *q_got)
     columns = [stage] + [send(stage, "b", j) for j in (1, 2, 3)]
     sys_two = jnp.concatenate([sys_one, lax.ppermute(sys_one, AXES, prompt_pairs(prompts, 2))])
     sys_far = lax.ppermute(sys_two, AXES, prompt_pairs(prompts, 4))
 
     at_slot = block_slot[0][:, None] == places
+    far_listed, *columns = lax.optimization_barrier((far_listed, *columns))
     mine_first = y < 2
     both = jnp.where(
         mine_first, jnp.concatenate([listed, far_listed], axis=1), jnp.concatenate([far_listed, listed], axis=1)
@@ -322,6 +341,31 @@
     mark = jnp.where(used, 1, 0) + jnp.where(places >= 64, 2, 0)
     code = jnp.sum(jnp.where(at_slot, mark[:, None], 0), axis=0)
 
+    def attend(cols):
+        operands = [columns[j] for j in cols] + [pool, sys_two, sys_far]
+        return pl.pallas_call(
+            functools.partial(main_kernel, cols),
+            grid_spec=pltpu.PrefetchScalarGridSpec(
+                num_scalar_prefetch=2,
+                grid=(1,),
+                in_specs=[whole(one) for one in operands],
+                out_specs=[pl.BlockSpec((SIDE, MSG, HD), lambda *_: (0, 0, 0))] * len(cols),
+                scratch_shapes=[
+                    pltpu.VMEM((2, ALL_TOK, HD), BF),
+                    pltpu.VMEM((2, ALL_TOK, 2 * HD), BF),
+                    pltpu.VMEM((2, 20, 8, HD), F32),
+                    pltpu.VMEM((2, 2048, HD), F32),
+                ],
+            ),
+            out_shape=[shaped((SIDE, MSG, HD))] * len(cols),
+            compiler_params=PARAMS,
+            cost_estimate=cost(len(cols) * 2**31, 2**22, len(cols) * 2**21),
+            name="attend_%d" % len(cols),
+        )(meta, code, *operands)
+
+    parts = list(attend((0, 1, 2, 3)))
+    parts = [parts[0]] + [send(parts[j], "b", -j) for j in (1, 2, 3)]
+    suffix_len, suffix_kv, parts[0] = lax.optimization_barrier((suffix_len, suffix_kv, parts[0]))
     new_heads = jnp.stack([one_head(new_kv, k) for k in range(KVH)])
     own_out, own_lse = pl.pallas_call(
         own_kernel,
@@ -337,40 +381,15 @@
         cost_estimate=cost(2**30, 2**22, 2**20),
         name="own_tokens",
     )(suffix_len, *q_msgs, *[one_head(suffix_kv, k) for k in range(KVH)], new_heads)
-    code, own_lse = lax.optimization_barrier((code, own_lse))
-
-    operands = [*columns, *pieces, sys_two, sys_far]
-    parts = pl.pallas_call(
-        main_kernel,
-        grid_spec=pltpu.PrefetchScalarGridSpec(
-            num_scalar_prefetch=2,
-            grid=(SIDE,),
-            in_specs=[whole(one) for one in operands],
-            out_specs=[pl.BlockSpec((SIDE, MSG, HD), lambda *_: (0, 0, 0))] * SIDE,
-            scratch_shapes=[
-                pltpu.VMEM((2, ALL_TOK, HD), BF),
-                pltpu.VMEM((2, ALL_TOK, 2 * HD), BF),
-                pltpu.VMEM((2, 20, 8, HD), F32),
-                pltpu.VMEM((SIDE, SIDE, ROWS, HD), BF),
-                pltpu.VMEM((SIDE, MSG, HD), BF),
-                pltpu.VMEM((2, 2048, HD), F32),
-            ],
-        ),
-        out_shape=[shaped((SIDE, MSG, HD))] * SIDE,
-        compiler_params=PARAMS,
-        cost_estimate=cost(2**33, 2**22, 2**23),
-        name="attend",
-    )(meta, code, *operands)
-    parts = [parts[0]] + [send(parts[j], "b", -j) for j in (1, 2, 3)]
     back = pl.pallas_call(
         combine_kernel,
-        in_specs=[VMEM] * 4,
+        in_specs=[SMEM] + [VMEM] * 4,
         out_specs=[VMEM] * 4,
         out_shape=[shaped((MSG, HD))] * 4,
         compiler_params=PARAMS,
         cost_estimate=cost(0, 2**20),
         name="combine",
-    )(*parts)
+    )(meta, *parts)
     heads = [back[0]] + [send(back[k], "a", -k) for k in (1, 2, 3)]
     out = pl.pallas_call(
         final_kernel,

time: 93 us -> 84.7 us (0.911)
  waiting for transfers between devices: 20.5 us -> 11.4 us
  starting transfers between devices: 27.6 us -> 31.4 us
  local copies, waits for them, and re-layouts: 12.5 us -> 10.5 us
    ppermute x15 -> x12, waiting for transfers between devices: 16.9 us -> 8.53 us  [send(): return lax.ppermute(array, AXES, ring_pairs(prompts, role, step % SIDE))]
    dynamic_slice x3 -> x2, local copies, waits for them, and re-layouts: 7.61 us -> 2.88 us  [one_head(): lax.dynamic_slice_in_dim(array, (a + k) % SIDE * HD, HD, array.ndim - 1)]
    all_to_all x0 -> x1, starting transfers between devices: none -> 3.91 us  [body(): lax.all_to_all(by_head, AXES, 0, 0, axis_index_groups=ring_groups(prompts...]
    ppermute x1, waiting for transfers between devices: 2.94 us -> 0.01 us  [body(): sys_far = lax.ppermute(sys_two, AXES, prompt_pairs(prompts, 4))]
    slice x0 -> x1, local copies, waits for them, and re-layouts: none -> 2.77 us  [body(): pool_kv[..., h * HD:(h + 1) * HD].reshape(-1, HD)]
    another operation x0 -> x1, other arithmetic: none -> 1.61 us  [body(): jnp.stack([pool_kv[..., h * HD:(h + 1) * HD].reshape(-1, HD) for h in ran...]
    select_n x1, other arithmetic: 1.33 us -> 0.04 us  [body(): jnp.where(places[None, :64] < prefix_blocks[:1, None], block_list[:1], -1)]
    all_to_all x0 -> x1, waiting for transfers between devices: none -> 1.19 us  [body(): lax.all_to_all(by_head, AXES, 0, 0, axis_index_groups=ring_groups(prompts...]
  transfers between devices with their start and end apart: 19 -> 17, of which waited for: 11 -> 9; matrix products, arithmetic and copies ran while one was open for 12% -> 12% of each run, Pallas kernels for 9% -> 7%
where the time goes in v2:
time: 84.7 us; the launch traced here: 84.1 us
  starting transfers between devices  31.4 us (37%)
  Pallas kernels  27.3 us (32%)
  waiting for transfers between devices  11.4 us (13%)
  local copies, waits for them, and re-layouts  10.5 us (12%)
  other arithmetic  3.1 us (4%)
    ppermute x12, starting transfers between devices, send(): return lax.ppermute(array, AXES, ring_pairs(prompts, role, step % SIDE))  18.1 us
    pallas_call x1, Pallas kernels, attend(): pl.pallas_call(functools.partial(main_kernel, cols), grid_spec=pltpu.Pref...  14.4 us
    ppermute x12, waiting for transfers between devices, send(): return lax.ppermute(array, AXES, ring_pairs(prompts, role, step % SIDE))  8.53 us
    pallas_call x1, Pallas kernels, body(): pl.pallas_call(own_kernel, in_specs=[SMEM] + [VMEM] * 9, out_specs=[VMEM]...  4.63 us
    unnamed x43, local copies, waits for them, and re-layouts  4.22 us
    ppermute x1, starting transfers between devices, body(): sys_far = lax.ppermute(sys_two, AXES, prompt_pairs(prompts, 4))  4.14 us
    all_to_all x1, starting transfers between devices, body(): lax.all_to_all(by_head, AXES, 0, 0, axis_index_groups=ring_groups(prompts...  3.91 us
    ppermute x1, starting transfers between devices, body(): far_listed = lax.ppermute(listed, AXES, row_pairs(prompts, 2))  3.27 us
  transfers between devices with their start and end apart: 17, of which 9 were waited for; matrix products, arithmetic and copies ran while one was open for 12% of the time, Pallas kernels for 7%

profile of v2, /device:TPU:0, one launch (start us, length us, event | category | flops | bytes accessed | tf_op | source)
XLA Modules:
  0.0 84.1 jit_solution(3675648661149673687)
XLA Ops:
  0.0 2.8 %fusion.2 = (bf16[8,128,2,128]{3,2,1,0:T(2,128)(2,1)S(1)}, bf16[8,128,2,128]{3,2,1,0:T(2,128)(2,1)S(1)}, bf16[8,128,2,128]{3,2,1,0:T(2,128)(2,1)S(1)}, bf16[8,128,2,128]{3,2,1,0:T(2,128)(2,1)S(1)}) fusion(bf16[8,128,2,512]{3,2,1,0:T(2,128)(2,1)} %param.13), kind=kLoop, calls=%fused_computation.20 | loop fusion | bytes 4194304 | tf_op jit(solution)/shard_map/slice | solution.py:301
  4.1 1.8 %query_messages.1 = (bf16[256,128]{1,0:T(8,128)(2,1)}, bf16[256,128]{1,0:T(8,128)(2,1)}, bf16[256,128]{1,0:T(8,128)(2,1)}, bf16[256,128]{1,0:T(8,128)(2,1)}) custom-call(s32[9]{0:T(128)} %stack.41.meta_ref, bf16[3,4,8192]{2,1,0:T(4,128)(2,1)} %bitcast.44, bf16[16,2,512]{2,1,0:T(2,128)(2,1)} %sys_ref.1, bf16[16,2,512]{2,1,0:T(2,128)(2,1)} %copy-done.12), custom_call_target="tpu_custom_call" | custom-call | bytes 524288 | tf_op jit(solution)/shard_map/query_messages/pallas_call | solution.py:303
  5.9 1.6 %collective-permute-start.2 = (bf16[256,128]{1,0:T(8,128)(2,1)}, bf16[256,128]{1,0:T(8,128)(2,1)S(1)}, u32[]{:S(2)}, u32[]{:S(2)}) collective-permute-start(bf16[256,128]{1,0:T(8,128)(2,1)} %get-tuple-element.39.q1), channel_id=1, source_target_pairs={{0,1},{1,2},{2,3},{3,0},{4,5},{5,6},{6,7},{7,4},{8,9},{9,10},{10,1... | collective-permute-start | bytes 196616 | tf_op jit(solution)/shard_map/ppermute | solution.py:289
  7.5 2.7 %collective-permute-start.3 = (bf16[256,128]{1,0:T(8,128)(2,1)}, bf16[256,128]{1,0:T(8,128)(2,1)S(1)}, u32[]{:S(2)}, u32[]{:S(2)}) collective-permute-start(bf16[256,128]{1,0:T(8,128)(2,1)} %get-tuple-element.40.q2), channel_id=1, source_target_pairs={{0,2},{1,3},{2,0},{3,1},{4,6},{5,7},{6,4},{7,5},{8,10},{9,11},{10,... | collective-permute-start | bytes 196616 | tf_op jit(solution)/shard_map/ppermute | solution.py:289
  10.2 1.4 %collective-permute-start.4 = (bf16[256,128]{1,0:T(8,128)(2,1)}, bf16[256,128]{1,0:T(8,128)(2,1)S(1)}, u32[]{:S(2)}, u32[]{:S(2)}) collective-permute-start(bf16[256,128]{1,0:T(8,128)(2,1)} %get-tuple-element.41.q3), channel_id=1, source_target_pairs={{0,3},{1,0},{2,1},{3,2},{4,7},{5,4},{6,5},{7,6},{8,11},{9,8},{10,9... | collective-permute-start | bytes 196616 | tf_op jit(solution)/shard_map/ppermute | solution.py:289
  11.7 1.6 %pad_maximum_fusion = bf16[4,2048,128]{2,1,0:T(8,128)(2,1)} fusion(bf16[1,2048,128]{2,1,0:T(8,128)(2,1)S(1)} %bitcast.38, bf16[1,2048,128]{2,1,0:T(8,128)(2,1)S(1)} %bitcast.39, bf16[1,2048,128]{2,1,0:T(8,128)(2,1)S(1)} %bitcast.37, bf16[1,2048,128]{2,1,0:T(8,128)(2,1)S(1)} %bitcast.36), kind=kLoop, calls=%fused_computation | loop fusion | flops 3145728 | bytes 4194304 | tf_op jit(solution)/shard_map/stack | solution.py:301
  13.5 1.2 %collective-permute-done.4.m3 = bf16[256,128]{1,0:T(8,128)(2,1)S(1)} collective-permute-done((bf16[256,128]{1,0:T(8,128)(2,1)}, bf16[256,128]{1,0:T(8,128)(2,1)S(1)}, u32[]{:S(2)}, u32[]{:S(2)}) %collective-permute-start.4) | collective-permute-done | bytes 65568 | tf_op jit(solution)/shard_map/ppermute | solution.py:289
  14.7 3.9 %all-to-all-start = ((bf16[4,2048,128]{2,1,0:T(8,128)(2,1)}), bf16[4,2048,128]{2,1,0:T(8,128)(2,1)S(1)}, u32[]{:S(2)}, u32[]{:S(2)}) async-start(bf16[4,2048,128]{2,1,0:T(8,128)(2,1)} %pad_maximum_fusion), calls=%async_computation | async-start | bytes 4194304 | tf_op jit(solution)/shard_map/all_to_all | solution.py:320
  18.8 3.3 %collective-permute-start.1 = (s32[1,64]{1,0:T(1,128)S(1)}, s32[1,64]{1,0:T(1,128)S(1)}, u32[]{:S(2)}, u32[]{:S(2)}) collective-permute-start(s32[1,64]{1,0:T(1,128)S(1)} %bitcast_select_fusion), channel_id=1, source_target_pairs={{0,8},{1,9},{2,10},{3,11},{4,12},{5,13},{6,14},{7,15},{8,0},{9,1},... | collective-permute-start | bytes 776 | tf_op jit(solution)/shard_map/ppermute | solution.py:317
  22.2 1.7 %stage.1 = (bf16[4,192,128]{2,1,0:T(8,128)(2,1)}, bf16[1,2,128,128]{3,2,1,0:T(8,128)(2,1)}) custom-call(s32[9]{0:T(128)} %stack.41.meta_ref, bf16[256,128]{1,0:T(8,128)(2,1)} %get-tuple-element.42.m0.q0, bf16[256,128]{1,0:T(8,128)(2,1)} %copy-done.5, bf16[256,128]{1,0:T(8,128)(2,1)} %copy-done.6, bf16[256,128]{1,0:T(8,128)(2,1)} %copy-done.7), custom_call_target="tpu_custom_call" | custom-call | bytes 524288 | tf_op jit(solution)/shard_map/stage/pallas_call | solution.py:321
  23.8 1.1 %collective-permute-start.7 = (bf16[4,192,128]{2,1,0:T(8,128)(2,1)}, bf16[4,192,128]{2,1,0:T(8,128)(2,1)S(1)}, u32[]{:S(2)}, u32[]{:S(2)}) collective-permute-start(bf16[4,192,128]{2,1,0:T(8,128)(2,1)} %get-tuple-element.48.refs_0_), channel_id=1, source_target_pairs={{0,12},{1,13},{2,14},{3,15},{4,0},{5,1},{6,2},{7,3},{8,4},{9,5},{1... | collective-permute-start | bytes 589832 | tf_op jit(solution)/shard_map/ppermute | solution.py:289
  24.9 1.7 %collective-permute-start.6 = (bf16[4,192,128]{2,1,0:T(8,128)(2,1)}, bf16[4,192,128]{2,1,0:T(8,128)(2,1)S(1)}, u32[]{:S(2)}, u32[]{:S(2)}) collective-permute-start(bf16[4,192,128]{2,1,0:T(8,128)(2,1)} %get-tuple-element.48.refs_0_), channel_id=1, source_target_pairs={{0,8},{1,9},{2,10},{3,11},{4,12},{5,13},{6,14},{7,15},{8,0},{9,1},... | collective-permute-start | bytes 589832 | tf_op jit(solution)/shard_map/ppermute | solution.py:289
  26.6 1.9 %collective-permute-start.8 = (bf16[1,2,128,128]{3,2,1,0:T(8,128)(2,1)}, bf16[1,2,128,128]{3,2,1,0:T(8,128)(2,1)S(1)}, u32[]{:S(2)}, u32[]{:S(2)}) collective-permute-start(bf16[1,2,128,128]{3,2,1,0:T(8,128)(2,1)} %get-tuple-element.53), channel_id=1, source_target_pairs={{0,32},{1,33},{2,34},{3,35},{4,36},{5,37},{6,38},{7,39},{8,40},{9,... | collective-permute-start | bytes 196616 | tf_op jit(solution)/shard_map/ppermute | solution.py:331
  28.5 0.9 %constant_dynamic-update-slice_fusion.1 = bf16[2,2,128,128]{3,2,1,0:T(8,128)(2,1)S(1)} fusion(bf16[1,2,128,128]{3,2,1,0:T(8,128)(2,1)} %get-tuple-element.53), kind=kLoop, calls=%fused_computation.7 | loop fusion | bytes 131072
  29.4 1.7 %collective-permute-done.8 = bf16[1,2,128,128]{3,2,1,0:T(8,128)(2,1)S(1)} collective-permute-done((bf16[1,2,128,128]{3,2,1,0:T(8,128)(2,1)}, bf16[1,2,128,128]{3,2,1,0:T(8,128)(2,1)S(1)}, u32[]{:S(2)}, u32[]{:S(2)}) %collective-permute-start.8) | collective-permute-done | bytes 65568 | tf_op jit(solution)/shard_map/ppermute | solution.py:331
  31.1 4.1 %collective-permute-start.9 = (bf16[2,2,128,128]{3,2,1,0:T(8,128)(2,1)S(1)}, bf16[2,2,128,128]{3,2,1,0:T(8,128)(2,1)S(1)}, u32[]{:S(2)}, u32[]{:S(2)}) collective-permute-start(bf16[2,2,128,128]{3,2,1,0:T(8,128)(2,1)S(1)} %constant_dynamic-update-slice_fusion.refs_5_), channel_id=1, source_target_pairs={{0,64},{1,65},{2,66},{3,67},{4,68},{5,69},{6,70},{7,71},{8,72},{9,... | collective-permute-start | bytes 393224 | tf_op jit(solution)/shard_map/ppermute | solution.py:332
  35.2 2.1 %collective-permute-done.5.refs_1_ = bf16[4,192,128]{2,1,0:T(8,128)(2,1)S(1)} collective-permute-done((bf16[4,192,128]{2,1,0:T(8,128)(2,1)}, bf16[4,192,128]{2,1,0:T(8,128)(2,1)S(1)}, u32[]{:S(2)}, u32[]{:S(2)}) %collective-permute-start.5) | collective-permute-done | bytes 196640 | tf_op jit(solution)/shard_map/ppermute | solution.py:289
  38.2 1.2 %all-to-all-done.refs_4_ = bf16[4,2048,128]{2,1,0:T(8,128)(2,1)S(1)} async-done(((bf16[4,2048,128]{2,1,0:T(8,128)(2,1)}), bf16[4,2048,128]{2,1,0:T(8,128)(2,1)S(1)}, u32[]{:S(2)}, u32[]{:S(2)}) %all-to-all-start) | async-done | bytes 2097184 | tf_op jit(solution)/shard_map/all_to_all | solution.py:320
  39.4 1.3 %copy-done = bf16[4,2048,128]{2,1,0:T(8,128)(2,1)} copy-done((bf16[4,2048,128]{2,1,0:T(8,128)(2,1)}, bf16[4,2048,128]{2,1,0:T(8,128)(2,1)S(1)}, u32[]{:S(2)}) %copy-start) | copy-done | bytes 2097176
  40.8 14.4 %attend_4.1 = (bf16[4,208,128]{2,1,0:T(8,128)(2,1)}, bf16[4,208,128]{2,1,0:T(8,128)(2,1)}, bf16[4,208,128]{2,1,0:T(8,128)(2,1)}, bf16[4,208,128]{2,1,0:T(8,128)(2,1)}) custom-call(s32[9]{0:T(128)} %stack.41.meta_ref, s32[128]{0:T(128)} %select_reduce_fusion.code_ref, bf16[4,192,128]{2,1,0:T(8,128)(2,1)} %get-tuple-element.48.refs_0_, ...), custom_call_target="tpu_custom_call" | custom-call | flops 8589934592 | bytes 4194304 | tf_op jit(solution)/shard_map/attend_4/pallas_call | solution.py:346
  55.2 3.2 %collective-permute-start.10 = (bf16[4,208,128]{2,1,0:T(8,128)(2,1)}, bf16[4,208,128]{2,1,0:T(8,128)(2,1)S(1)}, u32[]{:S(2)}, u32[]{:S(2)}) collective-permute-start(bf16[4,208,128]{2,1,0:T(8,128)(2,1)} %get-tuple-element.56), channel_id=1, source_target_pairs={{0,12},{1,13},{2,14},{3,15},{4,0},{5,1},{6,2},{7,3},{8,4},{9,5},{1... | collective-permute-start | bytes 638984 | tf_op jit(solution)/shard_map/ppermute | solution.py:289
  58.8 1.1 %collective-permute-start.12 = (bf16[4,208,128]{2,1,0:T(8,128)(2,1)}, bf16[4,208,128]{2,1,0:T(8,128)(2,1)S(1)}, u32[]{:S(2)}, u32[]{:S(2)}) collective-permute-start(bf16[4,208,128]{2,1,0:T(8,128)(2,1)} %get-tuple-element.58), channel_id=1, source_target_pairs={{0,4},{1,5},{2,6},{3,7},{4,8},{5,9},{6,10},{7,11},{8,12},{9,13},{1... | collective-permute-start | bytes 638984 | tf_op jit(solution)/shard_map/ppermute | solution.py:289
  60.6 2.8 %constant_dynamic-slice_fusion.4 = (bf16[4,256,2,128]{3,2,1,0:T(2,128)(2,1)}, bf16[4,256,2,128]{3,2,1,0:T(2,128)(2,1)}, bf16[4,256,2,128]{3,2,1,0:T(2,128)(2,1)}, bf16[4,256,2,128]{3,2,1,0:T(2,128)(2,1)}) fusion(bf16[4,256,2,512]{3,2,1,0:T(2,128)(2,1)S(1)} %copy-done.1, s32[]{:T(128)S(6)} %select_n.128, s32[]{:T(128)S(6)} %select_n.126, s32[]{:T(128)S(6)} %select_n.124, ...), kind=kLoop, calls=%fused_computation.12 | loop fusion | bytes 4194320 | tf_op jit(solution)/shard_map/dynamic_slice | solution.py:299
  63.4 0.9 %collective-permute-done.10.c1 = bf16[4,208,128]{2,1,0:T(8,128)(2,1)S(1)} collective-permute-done((bf16[4,208,128]{2,1,0:T(8,128)(2,1)}, bf16[4,208,128]{2,1,0:T(8,128)(2,1)S(1)}, u32[]{:S(2)}, u32[]{:S(2)}) %collective-permute-start.10) | collective-permute-done | bytes 213024 | tf_op jit(solution)/shard_map/ppermute | solution.py:289
  64.4 1.7 %collective-permute-done.11.c2 = bf16[4,208,128]{2,1,0:T(8,128)(2,1)S(1)} collective-permute-done((bf16[4,208,128]{2,1,0:T(8,128)(2,1)}, bf16[4,208,128]{2,1,0:T(8,128)(2,1)S(1)}, u32[]{:S(2)}, u32[]{:S(2)}) %collective-permute-start.11) | collective-permute-done | bytes 213024 | tf_op jit(solution)/shard_map/ppermute | solution.py:289
  66.0 2.2 %collective-permute-done.12.c3 = bf16[4,208,128]{2,1,0:T(8,128)(2,1)S(1)} collective-permute-done((bf16[4,208,128]{2,1,0:T(8,128)(2,1)}, bf16[4,208,128]{2,1,0:T(8,128)(2,1)S(1)}, u32[]{:S(2)}, u32[]{:S(2)}) %collective-permute-start.12) | collective-permute-done | bytes 213024 | tf_op jit(solution)/shard_map/ppermute | solution.py:289
  68.2 0.7 copy-done.4
  68.9 2.6 %combine.1 = (bf16[208,128]{1,0:T(8,128)(2,1)}, bf16[208,128]{1,0:T(8,128)(2,1)}, bf16[208,128]{1,0:T(8,128)(2,1)}, bf16[208,128]{1,0:T(8,128)(2,1)}) custom-call(s32[9]{0:T(128)} %stack.41.meta_ref, bf16[4,208,128]{2,1,0:T(8,128)(2,1)} %get-tuple-element.55.c0, bf16[4,208,128]{2,1,0:T(8,128)(2,1)} %copy-done.2, bf16[4,208,128]{2,1,0:T(8,128)(2,1)} %copy-done.3, ...), custom_call_target="tpu_custom_call" | custom-call | bytes 1048576 | tf_op jit(solution)/shard_map/combine/pallas_call | solution.py:384
  71.5 3.3 %collective-permute-start.13 = (bf16[208,128]{1,0:T(8,128)(2,1)}, bf16[208,128]{1,0:T(8,128)(2,1)S(1)}, u32[]{:S(2)}, u32[]{:S(2)}) collective-permute-start(bf16[208,128]{1,0:T(8,128)(2,1)} %get-tuple-element.60), channel_id=1, source_target_pairs={{0,3},{1,0},{2,1},{3,2},{4,7},{5,4},{6,5},{7,6},{8,11},{9,8},{10,9... | collective-permute-start | bytes 159752 | tf_op jit(solution)/shard_map/ppermute | solution.py:289
  75.5 0.8 collective-permute-start.15
  76.3 4.6 %own_tokens.1 = (f32[4,192,128]{2,1,0:T(8,128)}, f32[4,8,128]{2,1,0:T(8,128)}) custom-call(s32[4]{0:T(128)} %lens_ref, bf16[256,128]{1,0:T(8,128)(2,1)} %get-tuple-element.42.m0.q0, bf16[256,128]{1,0:T(8,128)(2,1)} %get-tuple-element.39.q1, bf16[256,128]{1,0:T(8,128)(2,1)} %get-tuple-element.40.q2, bf16[256,128]{1,0:T(8,128)(2,1)} %get-tuple-element.41.q3, ...), custom_call_target="tpu_custom_call" | custom-call | flops 1073741824 | bytes 4194304 | tf_op jit(solution)/shard_map/own_tokens/pallas_call | solution.py:370
  81.9 2.2 %final.1 = bf16[3,4,64,128]{3,2,1,0:T(8,128)(2,1)} custom-call(s32[9]{0:T(128)} %stack.41.meta_ref, bf16[208,128]{1,0:T(8,128)(2,1)} %get-tuple-element.59.r0, bf16[208,128]{1,0:T(8,128)(2,1)} %copy-done.8, bf16[208,128]{1,0:T(8,128)(2,1)} %copy-done.9, bf16[208,128]{1,0:T(8,128)(2,1)} %copy-done.10, f32[4,192,128]{2,1,0:T(8,128)} %get-tuple-element.65.own_ref, ...), custom_call_target="tpu_custom_call" | custom-call | tf_op jit(solution)/shard_map/final/pallas_call | solution.py:394
  (65 shorter events, 5.1 us)
Async XLA Ops:
  0.0 3.5 %collective-permute-start = (bf16[16,2,512]{2,1,0:T(2,128)(2,1)}, bf16[16,2,512]{2,1,0:T(2,128)(2,1)S(1)}, u32[]{:S(2)}, u32[]{:S(2)}) collective-permute-start(bf16[16,2,512]{2,1,0:T(2,128)(2,1)} %sys_ref.1), channel_id=1, source_target_pairs={{0,16},{1,17},{2,18},{3,19},{4,20},{5,21},{6,22},{7,23},{8,24},{9,... | collective-permute-start | bytes 98312 | tf_op jit(solution)/shard_map/ppermute | solution.py:297
  5.9 7.4 %collective-permute-start.2 = (bf16[256,128]{1,0:T(8,128)(2,1)}, bf16[256,128]{1,0:T(8,128)(2,1)S(1)}, u32[]{:S(2)}, u32[]{:S(2)}) collective-permute-start(bf16[256,128]{1,0:T(8,128)(2,1)} %get-tuple-element.39.q1), channel_id=1, source_target_pairs={{0,1},{1,2},{2,3},{3,0},{4,5},{5,6},{6,7},{7,4},{8,9},{9,10},{10,1... | collective-permute-start | bytes 196616 | tf_op jit(solution)/shard_map/ppermute | solution.py:289
  7.5 6.0 %collective-permute-start.3 = (bf16[256,128]{1,0:T(8,128)(2,1)}, bf16[256,128]{1,0:T(8,128)(2,1)S(1)}, u32[]{:S(2)}, u32[]{:S(2)}) collective-permute-start(bf16[256,128]{1,0:T(8,128)(2,1)} %get-tuple-element.40.q2), channel_id=1, source_target_pairs={{0,2},{1,3},{2,0},{3,1},{4,6},{5,7},{6,4},{7,5},{8,10},{9,11},{10,... | collective-permute-start | bytes 196616 | tf_op jit(solution)/shard_map/ppermute | solution.py:289
  10.2 4.5 %collective-permute-start.4 = (bf16[256,128]{1,0:T(8,128)(2,1)}, bf16[256,128]{1,0:T(8,128)(2,1)S(1)}, u32[]{:S(2)}, u32[]{:S(2)}) collective-permute-start(bf16[256,128]{1,0:T(8,128)(2,1)} %get-tuple-element.41.q3), channel_id=1, source_target_pairs={{0,3},{1,0},{2,1},{3,2},{4,7},{5,4},{6,5},{7,6},{8,11},{9,8},{10,9... | collective-permute-start | bytes 196616 | tf_op jit(solution)/shard_map/ppermute | solution.py:289
  13.3 5.4 %copy-start.13 = (bf16[4,3,2,512]{3,2,1,0:T(2,128)(2,1)S(1)}, bf16[4,3,2,512]{3,2,1,0:T(2,128)(2,1)}, u32[]{:S(2)}) copy-start(bf16[4,3,2,512]{3,2,1,0:T(2,128)(2,1)} %param.10) | copy-start | bytes 73732
  13.3 5.5 %copy-start.14 = (s32[4]{0:T(128)S(1)}, s32[4]{0:T(128)}, u32[]{:S(2)}) copy-start(s32[4]{0:T(128)} %param.17) | copy-start | bytes 52
  13.3 5.5 %copy-start.15 = (s32[4,64]{1,0:T(4,128)S(1)}, s32[4,64]{1,0:T(4,128)}, u32[]{:S(2)}) copy-start(s32[4,64]{1,0:T(4,128)} %param.16) | copy-start | bytes 3076
  13.3 24.3 %copy-start.20 = (s32[1,128]{1,0:T(1,128)S(1)}, s32[1,128]{1,0:T(1,128)}, u32[]{:S(2)}) copy-start(s32[1,128]{1,0:T(1,128)} %param.15) | copy-start | bytes 1540
  13.3 5.3 %copy-start.5 = (bf16[256,128]{1,0:T(8,128)(2,1)}, bf16[256,128]{1,0:T(8,128)(2,1)S(1)}, u32[]{:S(2)}) copy-start(bf16[256,128]{1,0:T(8,128)(2,1)S(1)} %collective-permute-done.2.m1) | copy-start | bytes 196612
  13.5 5.1 %copy-start.6 = (bf16[256,128]{1,0:T(8,128)(2,1)}, bf16[256,128]{1,0:T(8,128)(2,1)S(1)}, u32[]{:S(2)}) copy-start(bf16[256,128]{1,0:T(8,128)(2,1)S(1)} %collective-permute-done.3.m2) | copy-start | bytes 196612
  14.7 3.9 %copy-start.7 = (bf16[256,128]{1,0:T(8,128)(2,1)}, bf16[256,128]{1,0:T(8,128)(2,1)S(1)}, u32[]{:S(2)}) copy-start(bf16[256,128]{1,0:T(8,128)(2,1)S(1)} %collective-permute-done.4.m3) | copy-start | bytes 196612
  14.7 24.7 %all-to-all-start = ((bf16[4,2048,128]{2,1,0:T(8,128)(2,1)}), bf16[4,2048,128]{2,1,0:T(8,128)(2,1)S(1)}, u32[]{:S(2)}, u32[]{:S(2)}) async-start(bf16[4,2048,128]{2,1,0:T(8,128)(2,1)} %pad_maximum_fusion), calls=%async_computation | async-start | bytes 4194304 | tf_op jit(solution)/shard_map/all_to_all | solution.py:320
  18.8 16.4 %collective-permute-start.1 = (s32[1,64]{1,0:T(1,128)S(1)}, s32[1,64]{1,0:T(1,128)S(1)}, u32[]{:S(2)}, u32[]{:S(2)}) collective-permute-start(s32[1,64]{1,0:T(1,128)S(1)} %bitcast_select_fusion), channel_id=1, source_target_pairs={{0,8},{1,9},{2,10},{3,11},{4,12},{5,13},{6,14},{7,15},{8,0},{9,1},... | collective-permute-start | bytes 776 | tf_op jit(solution)/shard_map/ppermute | solution.py:317
  23.8 11.4 %collective-permute-start.7 = (bf16[4,192,128]{2,1,0:T(8,128)(2,1)}, bf16[4,192,128]{2,1,0:T(8,128)(2,1)S(1)}, u32[]{:S(2)}, u32[]{:S(2)}) collective-permute-start(bf16[4,192,128]{2,1,0:T(8,128)(2,1)} %get-tuple-element.48.refs_0_), channel_id=1, source_target_pairs={{0,12},{1,13},{2,14},{3,15},{4,0},{5,1},{6,2},{7,3},{8,4},{9,5},{1... | collective-permute-start | bytes 589832 | tf_op jit(solution)/shard_map/ppermute | solution.py:289
  24.9 10.3 %collective-permute-start.6 = (bf16[4,192,128]{2,1,0:T(8,128)(2,1)}, bf16[4,192,128]{2,1,0:T(8,128)(2,1)S(1)}, u32[]{:S(2)}, u32[]{:S(2)}) collective-permute-start(bf16[4,192,128]{2,1,0:T(8,128)(2,1)} %get-tuple-element.48.refs_0_), channel_id=1, source_target_pairs={{0,8},{1,9},{2,10},{3,11},{4,12},{5,13},{6,14},{7,15},{8,0},{9,1},... | collective-permute-start | bytes 589832 | tf_op jit(solution)/shard_map/ppermute | solution.py:289
  26.6 10.8 %collective-permute-start.5 = (bf16[4,192,128]{2,1,0:T(8,128)(2,1)}, bf16[4,192,128]{2,1,0:T(8,128)(2,1)S(1)}, u32[]{:S(2)}, u32[]{:S(2)}) collective-permute-start(bf16[4,192,128]{2,1,0:T(8,128)(2,1)} %get-tuple-element.48.refs_0_), channel_id=1, source_target_pairs={{0,4},{1,5},{2,6},{3,7},{4,8},{5,9},{6,10},{7,11},{8,12},{9,13},{1... | collective-permute-start | bytes 589832 | tf_op jit(solution)/shard_map/ppermute | solution.py:289
  26.6 4.5 %collective-permute-start.8 = (bf16[1,2,128,128]{3,2,1,0:T(8,128)(2,1)}, bf16[1,2,128,128]{3,2,1,0:T(8,128)(2,1)S(1)}, u32[]{:S(2)}, u32[]{:S(2)}) collective-permute-start(bf16[1,2,128,128]{3,2,1,0:T(8,128)(2,1)} %get-tuple-element.53), channel_id=1, source_target_pairs={{0,32},{1,33},{2,34},{3,35},{4,36},{5,37},{6,38},{7,39},{8,40},{9,... | collective-permute-start | bytes 196616 | tf_op jit(solution)/shard_map/ppermute | solution.py:331
  31.1 8.3 %copy-start.11 = (bf16[2,2,128,128]{3,2,1,0:T(8,128)(2,1)}, bf16[2,2,128,128]{3,2,1,0:T(8,128)(2,1)S(1)}, u32[]{:S(2)}) copy-start(bf16[2,2,128,128]{3,2,1,0:T(8,128)(2,1)S(1)} %constant_dynamic-update-slice_fusion.refs_5_) | copy-start | bytes 393220
  31.1 7.1 %collective-permute-start.9 = (bf16[2,2,128,128]{3,2,1,0:T(8,128)(2,1)S(1)}, bf16[2,2,128,128]{3,2,1,0:T(8,128)(2,1)S(1)}, u32[]{:S(2)}, u32[]{:S(2)}) collective-permute-start(bf16[2,2,128,128]{3,2,1,0:T(8,128)(2,1)S(1)} %constant_dynamic-update-slice_fusion.refs_5_), channel_id=1, source_target_pairs={{0,64},{1,65},{2,66},{3,67},{4,68},{5,69},{6,70},{7,71},{8,72},{9,... | collective-permute-start | bytes 393224 | tf_op jit(solution)/shard_map/ppermute | solution.py:332
  35.2 4.2 %copy-start.16 = (bf16[4,192,128]{2,1,0:T(8,128)(2,1)}, bf16[4,192,128]{2,1,0:T(8,128)(2,1)S(1)}, u32[]{:S(2)}) copy-start(bf16[4,192,128]{2,1,0:T(8,128)(2,1)S(1)} %collective-permute-done.7.refs_3_) | copy-start | bytes 589828
  35.2 4.2 %copy-start.17 = (bf16[4,192,128]{2,1,0:T(8,128)(2,1)}, bf16[4,192,128]{2,1,0:T(8,128)(2,1)S(1)}, u32[]{:S(2)}) copy-start(bf16[4,192,128]{2,1,0:T(8,128)(2,1)S(1)} %collective-permute-done.6.refs_2_) | copy-start | bytes 589828
  37.4 2.0 %copy-start.18 = (bf16[4,192,128]{2,1,0:T(8,128)(2,1)}, bf16[4,192,128]{2,1,0:T(8,128)(2,1)S(1)}, u32[]{:S(2)}) copy-start(bf16[4,192,128]{2,1,0:T(8,128)(2,1)S(1)} %collective-permute-done.5.refs_1_) | copy-start | bytes 589828
  39.4 1.4 %copy-start = (bf16[4,2048,128]{2,1,0:T(8,128)(2,1)}, bf16[4,2048,128]{2,1,0:T(8,128)(2,1)S(1)}, u32[]{:S(2)}) copy-start(bf16[4,2048,128]{2,1,0:T(8,128)(2,1)S(1)} %all-to-all-done.refs_4_) | copy-start | bytes 6291460
  40.8 19.8 %copy-start.1 = (bf16[4,256,2,512]{3,2,1,0:T(2,128)(2,1)S(1)}, bf16[4,256,2,512]{3,2,1,0:T(2,128)(2,1)}, u32[]{:S(2)}) copy-start(bf16[4,256,2,512]{3,2,1,0:T(2,128)(2,1)} %param.11) | copy-start | bytes 6291460
  55.2 9.2 %collective-permute-start.10 = (bf16[4,208,128]{2,1,0:T(8,128)(2,1)}, bf16[4,208,128]{2,1,0:T(8,128)(2,1)S(1)}, u32[]{:S(2)}, u32[]{:S(2)}) collective-permute-start(bf16[4,208,128]{2,1,0:T(8,128)(2,1)} %get-tuple-element.56), channel_id=1, source_target_pairs={{0,12},{1,13},{2,14},{3,15},{4,0},{5,1},{6,2},{7,3},{8,4},{9,5},{1... | collective-permute-start | bytes 638984 | tf_op jit(solution)/shard_map/ppermute | solution.py:289
  58.4 7.7 %collective-permute-start.11 = (bf16[4,208,128]{2,1,0:T(8,128)(2,1)}, bf16[4,208,128]{2,1,0:T(8,128)(2,1)S(1)}, u32[]{:S(2)}, u32[]{:S(2)}) collective-permute-start(bf16[4,208,128]{2,1,0:T(8,128)(2,1)} %get-tuple-element.57), channel_id=1, source_target_pairs={{0,8},{1,9},{2,10},{3,11},{4,12},{5,13},{6,14},{7,15},{8,0},{9,1},... | collective-permute-start | bytes 638984 | tf_op jit(solution)/shard_map/ppermute | solution.py:289
  58.8 9.4 %collective-permute-start.12 = (bf16[4,208,128]{2,1,0:T(8,128)(2,1)}, bf16[4,208,128]{2,1,0:T(8,128)(2,1)S(1)}, u32[]{:S(2)}, u32[]{:S(2)}) collective-permute-start(bf16[4,208,128]{2,1,0:T(8,128)(2,1)} %get-tuple-element.58), channel_id=1, source_target_pairs={{0,4},{1,5},{2,6},{3,7},{4,8},{5,9},{6,10},{7,11},{8,12},{9,13},{1... | collective-permute-start | bytes 638984 | tf_op jit(solution)/shard_map/ppermute | solution.py:289
  64.4 3.9 %copy-start.2 = (bf16[4,208,128]{2,1,0:T(8,128)(2,1)}, bf16[4,208,128]{2,1,0:T(8,128)(2,1)S(1)}, u32[]{:S(2)}) copy-start(bf16[4,208,128]{2,1,0:T(8,128)(2,1)S(1)} %collective-permute-done.10.c1) | copy-start | bytes 638980
  66.0 2.2 %copy-start.3 = (bf16[4,208,128]{2,1,0:T(8,128)(2,1)}, bf16[4,208,128]{2,1,0:T(8,128)(2,1)S(1)}, u32[]{:S(2)}) copy-start(bf16[4,208,128]{2,1,0:T(8,128)(2,1)S(1)} %collective-permute-done.11.c2) | copy-start | bytes 638980
  71.5 9.5 %collective-permute-start.13 = (bf16[208,128]{1,0:T(8,128)(2,1)}, bf16[208,128]{1,0:T(8,128)(2,1)S(1)}, u32[]{:S(2)}, u32[]{:S(2)}) collective-permute-start(bf16[208,128]{1,0:T(8,128)(2,1)} %get-tuple-element.60), channel_id=1, source_target_pairs={{0,3},{1,0},{2,1},{3,2},{4,7},{5,4},{6,5},{7,6},{8,11},{9,8},{10,9... | collective-permute-start | bytes 159752 | tf_op jit(solution)/shard_map/ppermute | solution.py:289
  74.8 6.2 %collective-permute-start.14 = (bf16[208,128]{1,0:T(8,128)(2,1)}, bf16[208,128]{1,0:T(8,128)(2,1)S(1)}, u32[]{:S(2)}, u32[]{:S(2)}) collective-permute-start(bf16[208,128]{1,0:T(8,128)(2,1)} %get-tuple-element.61), channel_id=1, source_target_pairs={{0,2},{1,3},{2,0},{3,1},{4,6},{5,7},{6,4},{7,5},{8,10},{9,11},{10,... | collective-permute-start | bytes 159752 | tf_op jit(solution)/shard_map/ppermute | solution.py:289
  75.5 5.7 %collective-permute-start.15 = (bf16[208,128]{1,0:T(8,128)(2,1)}, bf16[208,128]{1,0:T(8,128)(2,1)S(1)}, u32[]{:S(2)}, u32[]{:S(2)}) collective-permute-start(bf16[208,128]{1,0:T(8,128)(2,1)} %get-tuple-element.62), channel_id=1, source_target_pairs={{0,1},{1,2},{2,3},{3,0},{4,5},{5,6},{6,7},{7,4},{8,9},{9,10},{10,1... | collective-permute-start | bytes 159752 | tf_op jit(solution)/shard_map/ppermute | solution.py:289
  (6 other events, 4.4 us)

commit v3 on v2

--- a/solution.py
+++ b/solution.py
@@ -24,7 +24,12 @@
 BF = jnp.bfloat16
 F32 = jnp.float32
 NT = (((1,), (1,)), ((), ()))
-PARAMS = pltpu.CompilerParams(vmem_limit_bytes=56 * 2**20)
+
+
+def room(mib):
+    return pltpu.CompilerParams(vmem_limit_bytes=mib * 2**20)
+
+
 SMEM = pl.BlockSpec(memory_space=pltpu.SMEM)
 VMEM = pl.BlockSpec(memory_space=pltpu.VMEM)
 
@@ -56,21 +61,26 @@
     return groups
 
 
-def row_pairs(prompts, step):
+def core_pairs(prompts):
     count = SIDE * SIDE
-    return [(p * count + c, p * count + (c + step * SIDE) % count) for p in range(prompts) for c in range(count)]
-
-
-def prompt_pairs(prompts, bit):
+    return [(p * count + c, (p ^ 1) * count + c) for p in range(prompts) for c in range(count)]
+
+
+def plane_pairs(prompts, step):
     count = SIDE * SIDE
-    return [(p * count + c, (p ^ bit) * count + c) for p in range(prompts) for c in range(count)]
+    return [(p * count + c, (p + 2 * step) % prompts * count + c) for p in range(prompts) for c in range(count)]
 
 
 def turned(meta_ref, k):
     return lax.rem(meta_ref[2] + k, SIDE)
 
 
-def query_kernel(meta_ref, q_ref, sys_ref, far_ref, o0, o1, o2, o3, tmp, sys_tmp):
+def query_kernel(meta_ref, slot_ref, list_ref, used_ref, q_ref, sys_ref, far_ref, o0, o1, o2, o3, tmp, sys_tmp):
+    lane = lax.broadcasted_iota(jnp.int32, (16, HD), 1)
+    flags = jnp.zeros((16, HD), F32)
+    for n in range(64):
+        slot = jnp.where(n < used_ref[0], slot_ref[0, list_ref[0, n]], -1)
+        flags = jnp.where(lane == slot, 1.0, flags)
     for k, out in enumerate((o0, o1, o2, o3)):
         head = turned(meta_ref, k)
         for t in range(3):
@@ -81,16 +91,17 @@
         lanes = pl.ds(pl.multiple_of(head * HD, HD), HD)
         sys_tmp[pl.ds(0, SYS_PART), :] = sys_ref[:, :, lanes].reshape(SYS_PART, HD).astype(F32)
         sys_tmp[pl.ds(SYS_PART, SYS_PART), :] = far_ref[:, :, lanes].reshape(SYS_PART, HD).astype(F32)
-        out[pl.ds(ROWS, SYS_PART), :] = sys_tmp[pl.ds(0, SYS_PART, stride=2), :].astype(BF)
-        out[pl.ds(ROWS + SYS_PART, SYS_PART), :] = sys_tmp[pl.ds(1, SYS_PART, stride=2), :].astype(BF)
+        out[pl.ds(MSG, SYS_PART), :] = sys_tmp[pl.ds(0, SYS_PART, stride=2), :].astype(BF)
+        out[pl.ds(MSG + SYS_PART, SYS_PART), :] = sys_tmp[pl.ds(1, SYS_PART, stride=2), :].astype(BF)
+        out[pl.ds(ROWS, 16), :] = flags.astype(BF)
 
 
 def stage_kernel(meta_ref, m0, m1, m2, m3, stage_ref, sys_ref):
     for k, msg in enumerate((m0, m1, m2, m3)):
-        stage_ref[turned(meta_ref, SIDE - k)] = msg[pl.ds(0, ROWS), :]
+        stage_ref[turned(meta_ref, SIDE - k)] = msg[pl.ds(0, MSG), :]
         for side in range(2):
             at = pl.ds(k * SYS_PART, SYS_PART)
-            sys_ref[0, side, at, :] = msg[pl.ds(ROWS + side * SYS_PART, SYS_PART), :]
+            sys_ref[side, at, :] = msg[pl.ds(MSG + side * SYS_PART, SYS_PART), :]
 
 
 def flatten_rows(lse):
@@ -138,43 +149,57 @@
     return mixed
 
 
-def main_kernel(cols, meta_ref, code_ref, *refs):
-    count = len(cols)
-    q_refs, pool_ref, sys_refs, refs = refs[:count], refs[count], refs[count + 1 : count + 3], refs[count + 3 :]
-    o_refs, (kc, vc, bias, tmp) = refs[:count], refs[count:]
+def main_kernel(meta_ref, owner_ref, *refs):
+    q_refs, pool_ref, sys_refs, o_refs, refs = refs[:4], refs[4], refs[5:9], refs[9:13], refs[13:]
+    kc, vc, bias, tmp, raw, sems = refs
     pair = 2 * ROWS
-
-    def fill():
-        for p in range(2):
-            vc[p, :, pl.ds(HD, HD)] = jnp.ones((ALL_TOK, HD), BF)
-            for n in range(4):
-                at = pl.ds(4 * POOL_TOK + n * BLK, BLK)
-                kc[p, at, :] = sys_refs[n // 2][n % 2, 0]
-                vc[p, at, pl.ds(0, HD)] = sys_refs[n // 2][n % 2, 1]
-                bias[p, 16 + n] = jnp.zeros((8, HD), F32)
-        for k in range(SIDE):
-            held = tmp.at[k % 2]
-            held[...] = pool_ref[k].astype(F32)
-            n0, n1 = jnp.int32(0), jnp.int32(0)
-            for blk in range(8):
-                code = code_ref[meta_ref[3 + k] + blk]
-                prompt = code // 2
-                rank = k * 4 + jnp.minimum(jnp.where(prompt == 0, n0, n1), 3)
-                at = pl.ds(pl.multiple_of(rank * BLK, BLK), BLK)
-                kc[prompt, at, :] = held[pl.ds(blk * 2 * BLK, BLK, stride=2), :].astype(BF)
-                vc[prompt, at, pl.ds(0, HD)] = held[pl.ds(blk * 2 * BLK + 1, BLK, stride=2), :].astype(BF)
-                dead = jnp.where(code % 2 == 1, 0.0, FLOOR)
-                bias[prompt, rank] = jnp.full((8, HD), dead, F32)
-                n0 = n0 + 1 - prompt
-                n1 = n1 + prompt
+    copies = [pltpu.make_async_copy(pool_ref.at[k], raw.at[k], sems.at[k]) for k in range(SIDE)]
+    for copy in copies:
+        copy.start()
+
+    def used_slots(prompt):
+        column = lax.rem(meta_ref[0] - 2 * prompt + SIDE, SIDE)
+        row = pl.ds(ROWS, 1)
+        flags = q_refs[0][2 * prompt, row, :].astype(F32)
+        for j in range(SIDE):
+            chosen = (meta_ref[7] == 0) & (column == j)
+            flags = jnp.where(chosen, q_refs[j][0, row, :].astype(F32), flags)
+        return flags
+
+    flags = [used_slots(0), used_slots(1)]
+    lane = lax.broadcasted_iota(jnp.int32, (1, HD), 1)
+    for p in range(2):
+        vc[p, :, pl.ds(HD, HD)] = jnp.ones((ALL_TOK, HD), BF)
+        for n in range(4):
+            at = pl.ds(4 * POOL_TOK + n * BLK, BLK)
+            kc[p, at, :] = sys_refs[n][0]
+            vc[p, at, pl.ds(0, HD)] = sys_refs[n][1]
+            bias[p, 16 + n] = jnp.zeros((8, HD), F32)
+    for k in range(SIDE):
+        copies[k].wait()
+        held = tmp.at[k % 2]
+        held[...] = raw[k].astype(F32)
+        n0, n1 = jnp.int32(0), jnp.int32(0)
+        for blk in range(8):
+            slot = meta_ref[3 + k] + blk
+            prompt = owner_ref[slot]
+            rank = k * 4 + jnp.minimum(jnp.where(prompt == 0, n0, n1), 3)
+            at = pl.ds(pl.multiple_of(rank * BLK, BLK), BLK)
+            kc[prompt, at, :] = held[pl.ds(blk * 2 * BLK, BLK, stride=2), :].astype(BF)
+            vc[prompt, at, pl.ds(0, HD)] = held[pl.ds(blk * 2 * BLK + 1, BLK, stride=2), :].astype(BF)
+            live = jnp.where(prompt == 0, flags[0], flags[1])
+            live = jnp.sum(jnp.where(lane == slot, live, 0.0), axis=1, keepdims=True)
+            bias[prompt, rank] = jnp.broadcast_to((1.0 - live) * FLOOR, (8, HD))
+            n0 = n0 + 1 - prompt
+            n1 = n1 + prompt
 
     def prompt_of(i, n):
-        row = lax.rem(meta_ref[0] - cols[i] + SIDE, SIDE)
+        row = lax.rem(meta_ref[0] - i + SIDE, SIDE)
         return jnp.where(meta_ref[7] == 0, row // 2, n)
 
     def scores(i, n):
         p = prompt_of(i, n)
-        q = q_refs[i][2 * n : 2 * n + 2].reshape(pair, HD)
+        q = q_refs[i][2 * n : 2 * n + 2, :ROWS].reshape(pair, HD)
         s = lax.dot_general(q, kc[p], NT, preferred_element_type=F32)
         return s + jnp.concatenate([bias[p, t, :1, :] for t in range(20)], axis=1)
 
@@ -190,8 +215,7 @@
             o_refs[i][2 * n + half, pl.ds(0, ROWS), :] = out[part]
             o_refs[i][2 * n + half, pl.ds(ROWS, 16), :] = pack_flat(flatten_rows(lse[part]))
 
-    fill()
-    jobs = [(i, n) for i in range(count) for n in range(2)]
+    jobs = [(i, n) for i in range(SIDE) for n in range(2)]
     s = scores(*jobs[0])
     for t, job in enumerate(jobs):
         following = scores(*jobs[t + 1]) if t + 1 < len(jobs) else None
@@ -291,10 +315,10 @@
     def source(n):
         return jnp.where(even, y * SIDE + n, n * SIDE + x) * 8
 
-    zero = jnp.int32(0)
-    meta = jnp.stack([y, x, a, source(0), source(1), source(2), source(3), core, zero]).astype(jnp.int32)
-
-    far_sys = lax.ppermute(sys_kv, AXES, prompt_pairs(prompts, 1))
+    meta = jnp.stack([y, x, a, source(0), source(1), source(2), source(3), core]).astype(jnp.int32)
+
+    far_sys = lax.ppermute(sys_kv, AXES, core_pairs(prompts))
+
     def one_head(array, k):
         return lax.dynamic_slice_in_dim(array, ((a + k) % SIDE) * HD, HD, array.ndim - 1).reshape(-1, HD)
 
@@ -302,19 +326,14 @@
 
     q_msgs = pl.pallas_call(
         query_kernel,
-        in_specs=[SMEM, VMEM, VMEM, VMEM],
+        in_specs=[SMEM] * 4 + [VMEM] * 3,
         out_specs=[VMEM] * 4,
-        out_shape=[shaped((ROWS + 2 * SYS_PART, HD))] * 4,
+        out_shape=[shaped((MSG + 2 * SYS_PART, HD))] * 4,
         scratch_shapes=[pltpu.VMEM((ROWS, HD), F32), pltpu.VMEM((2 * SYS_PART, HD), F32)],
-        compiler_params=PARAMS,
+        compiler_params=room(10),
         cost_estimate=cost(0, 2**19),
         name="query_messages",
-    )(meta, queries.transpose(1, 0, 2), sys_kv, far_sys)
-    q_msgs = list(q_msgs)
-    places = jnp.arange(128, dtype=jnp.int32)
-    block_list, q_msgs[0] = lax.optimization_barrier((block_list, q_msgs[0]))
-    listed = jnp.where(places[None, :64] < prefix_blocks[:1, None], block_list[:1], -1)
-    far_listed = lax.ppermute(listed, AXES, row_pairs(prompts, 2))
+    )(meta, block_slot, block_list, prefix_blocks, queries.transpose(1, 0, 2), sys_kv, far_sys)
     q_got = [q_msgs[0]] + [send(q_msgs[k], "a", k) for k in (1, 2, 3)]
     by_head, *q_got = lax.optimization_barrier((by_head, *q_got))
     pool = lax.all_to_all(by_head, AXES, 0, 0, axis_index_groups=ring_groups(prompts, "a"), tiled=True)
@@ -322,50 +341,41 @@
         stage_kernel,
         in_specs=[SMEM] + [VMEM] * 4,
         out_specs=[VMEM] * 2,
-        out_shape=[shaped((SIDE, ROWS, HD)), shaped((1, 2, BLK, HD))],
-        compiler_params=PARAMS,
+        out_shape=[shaped((SIDE, MSG, HD)), shaped((2, BLK, HD))],
+        compiler_params=room(8),
         cost_estimate=cost(0, 2**19),
         name="stage",
     )(meta, *q_got)
     columns = [stage] + [send(stage, "b", j) for j in (1, 2, 3)]
-    sys_two = jnp.concatenate([sys_one, lax.ppermute(sys_one, AXES, prompt_pairs(prompts, 2))])
-    sys_far = lax.ppermute(sys_two, AXES, prompt_pairs(prompts, 4))
-
-    at_slot = block_slot[0][:, None] == places
-    far_listed, *columns = lax.optimization_barrier((far_listed, *columns))
-    mine_first = y < 2
-    both = jnp.where(
-        mine_first, jnp.concatenate([listed, far_listed], axis=1), jnp.concatenate([far_listed, listed], axis=1)
-    )
-    used = jnp.any(both[0][:, None] == places, axis=0)
-    mark = jnp.where(used, 1, 0) + jnp.where(places >= 64, 2, 0)
-    code = jnp.sum(jnp.where(at_slot, mark[:, None], 0), axis=0)
-
-    def attend(cols):
-        operands = [columns[j] for j in cols] + [pool, sys_two, sys_far]
-        return pl.pallas_call(
-            functools.partial(main_kernel, cols),
-            grid_spec=pltpu.PrefetchScalarGridSpec(
-                num_scalar_prefetch=2,
-                grid=(1,),
-                in_specs=[whole(one) for one in operands],
-                out_specs=[pl.BlockSpec((SIDE, MSG, HD), lambda *_: (0, 0, 0))] * len(cols),
-                scratch_shapes=[
-                    pltpu.VMEM((2, ALL_TOK, HD), BF),
-                    pltpu.VMEM((2, ALL_TOK, 2 * HD), BF),
-                    pltpu.VMEM((2, 20, 8, HD), F32),
-                    pltpu.VMEM((2, 2048, HD), F32),
-                ],
-            ),
-            out_shape=[shaped((SIDE, MSG, HD))] * len(cols),
-            compiler_params=PARAMS,
-            cost_estimate=cost(len(cols) * 2**31, 2**22, len(cols) * 2**21),
-            name="attend_%d" % len(cols),
-        )(meta, code, *operands)
-
-    parts = list(attend((0, 1, 2, 3)))
+    system = [sys_one] + [lax.ppermute(sys_one, AXES, plane_pairs(prompts, k)) for k in (1, 2, 3)]
+
+    places = jnp.arange(128, dtype=jnp.int32)
+    owner = jnp.sum(jnp.where((block_slot[0][:, None] == places) & (places[:, None] >= 64), 1, 0), axis=0)
+
+    parts = pl.pallas_call(
+        main_kernel,
+        grid_spec=pltpu.PrefetchScalarGridSpec(
+            num_scalar_prefetch=2,
+            grid=(1,),
+            in_specs=[whole(one) for one in columns] + [pl.BlockSpec(memory_space=pl.ANY)] + [whole(sys_one)] * 4,
+            out_specs=[pl.BlockSpec((SIDE, MSG, HD), lambda *_: (0, 0, 0))] * SIDE,
+            scratch_shapes=[
+                pltpu.VMEM((2, ALL_TOK, HD), BF),
+                pltpu.VMEM((2, ALL_TOK, 2 * HD), BF),
+                pltpu.VMEM((2, 20, 8, HD), F32),
+                pltpu.VMEM((2, 2048, HD), F32),
+                pltpu.VMEM((SIDE, 2048, HD), BF),
+                pltpu.SemaphoreType.DMA((SIDE,)),
+            ],
+        ),
+        out_shape=[shaped((SIDE, MSG, HD))] * SIDE,
+        compiler_params=room(38),
+        cost_estimate=cost(2**33, 2**22, 2**23),
+        name="attend",
+    )(meta, owner, *columns, pool, *system)
+    parts = list(parts)
     parts = [parts[0]] + [send(parts[j], "b", -j) for j in (1, 2, 3)]
-    suffix_len, suffix_kv, parts[0] = lax.optimization_barrier((suffix_len, suffix_kv, parts[0]))
+    suffix_len, parts[0] = lax.optimization_barrier((suffix_len, parts[0]))
     new_heads = jnp.stack([one_head(new_kv, k) for k in range(KVH)])
     own_out, own_lse = pl.pallas_call(
         own_kernel,
@@ -377,7 +387,7 @@
             pltpu.VMEM((2, 2048 + 2 * BLK, HD), F32),
             pltpu.VMEM((2, 1024 + BLK, 2 * HD), BF),
         ],
-        compiler_params=PARAMS,
+        compiler_params=room(20),
         cost_estimate=cost(2**30, 2**22, 2**20),
         name="own_tokens",
     )(suffix_len, *q_msgs, *[one_head(suffix_kv, k) for k in range(KVH)], new_heads)
@@ -386,7 +396,7 @@
         in_specs=[SMEM] + [VMEM] * 4,
         out_specs=[VMEM] * 4,
         out_shape=[shaped((MSG, HD))] * 4,
-        compiler_params=PARAMS,
+        compiler_params=room(10),
         cost_estimate=cost(0, 2**20),
         name="combine",
     )(meta, *parts)
@@ -396,7 +406,7 @@
         in_specs=[SMEM] + [VMEM] * 6,
         out_specs=VMEM,
         out_shape=shaped((3, KVH, 64, HD)),
-        compiler_params=PARAMS,
+        compiler_params=room(10),
         name="final",
     )(meta, *heads, own_out, own_lse)
     return out.reshape(3, KVH, GQ, 4, HD).transpose(3, 0, 1, 2, 4).reshape(4, 3, QH * HD)

time: 84.7 us -> 74 us (0.87)
  Pallas kernels: 27.3 us -> 19.6 us
  local copies, waits for them, and re-layouts: 10.5 us -> 5.49 us
  waiting for transfers between devices: 11.4 us -> 15.1 us
  other arithmetic: 3.1 us -> 1.74 us
    unnamed x43 -> x14, local copies, waits for them, and re-layouts: 4.22 us -> 0.03 us
    pallas_call x2, Pallas kernels: 16.2 us -> 13.4 us  [the longest x1 12.5 us: body(): pl.pallas_call(main_kernel, grid_spec=pltpu.PrefetchScalarGridSpec(num_sc...]
    all_to_all x1, waiting for transfers between devices: 1.19 us -> 3.3 us  [body(): lax.all_to_all(by_head, AXES, 0, 0, axis_index_groups=ring_groups(prompts...]
    ppermute x12, starting transfers between devices: 18.1 us -> 20 us  [send(): return lax.ppermute(array, AXES, ring_pairs(prompts, role, step % SIDE))]
    pallas_call x1, Pallas kernels: 4.63 us -> 2.81 us  [body(): pl.pallas_call(own_kernel, in_specs=[SMEM] + [VMEM] * 9, out_specs=[VMEM]...]
    ppermute x4, starting transfers between devices: 9.33 us -> 7.68 us  [the longest x3 7.6 us: body(): lax.ppermute(sys_one, AXES, plane_pairs(prompts, k))]
    pallas_call x1, Pallas kernels: 2.57 us -> 1.23 us  [body(): pl.pallas_call(combine_kernel, in_specs=[SMEM] + [VMEM] * 4, out_specs=[V...]
    ppermute x12, waiting for transfers between devices: 8.53 us -> 9.78 us  [send(): return lax.ppermute(array, AXES, ring_pairs(prompts, role, step % SIDE))]
  transfers between devices with their start and end apart: 17 -> 17, of which waited for: 9 -> 9; matrix products, arithmetic and copies ran while one was open for 12% -> 10% of each run, Pallas kernels for 7% -> 5%
where the time goes in v3:
time: 74 us; the launch traced here: 73.7 us
  starting transfers between devices  31.5 us (43%)
  Pallas kernels  19.6 us (26%)
  waiting for transfers between devices  15.1 us (20%)
  local copies, waits for them, and re-layouts  5.49 us (7%)
  other arithmetic  1.74 us (2%)
    ppermute x12, starting transfers between devices, send(): return lax.ppermute(array, AXES, ring_pairs(prompts, role, step % SIDE))  20 us
    pallas_call x1, Pallas kernels, body(): pl.pallas_call(main_kernel, grid_spec=pltpu.PrefetchScalarGridSpec(num_sc...  12.5 us
    ppermute x12, waiting for transfers between devices, send(): return lax.ppermute(array, AXES, ring_pairs(prompts, role, step % SIDE))  9.78 us
    ppermute x3, starting transfers between devices, body(): lax.ppermute(sys_one, AXES, plane_pairs(prompts, k))  7.6 us
    all_to_all x1, starting transfers between devices, body(): lax.all_to_all(by_head, AXES, 0, 0, axis_index_groups=ring_groups(prompts...  3.91 us
    all_to_all x1, waiting for transfers between devices, body(): lax.all_to_all(by_head, AXES, 0, 0, axis_index_groups=ring_groups(prompts...  3.3 us
    pallas_call x1, Pallas kernels, body(): pl.pallas_call(own_kernel, in_specs=[SMEM] + [VMEM] * 9, out_specs=[VMEM]...  2.81 us
    slice x1, local copies, waits for them, and re-layouts, body(): pool_kv[..., h * HD:(h + 1) * HD].reshape(-1, HD)  2.72 us
  transfers between devices with their start and end apart: 17, of which 9 were waited for; matrix products, arithmetic and copies ran while one was open for 10% of the time, Pallas kernels for 5%

profile of v3, /device:TPU:0, one launch (start us, length us, event | category | flops | bytes accessed | tf_op | source)
XLA Modules:
  0.0 73.7 jit_solution(15743723567900051172)
XLA Ops:
  0.1 2.7 %fusion.1 = (bf16[8,128,2,128]{3,2,1,0:T(2,128)(2,1)S(1)}, bf16[8,128,2,128]{3,2,1,0:T(2,128)(2,1)S(1)}, bf16[8,128,2,128]{3,2,1,0:T(2,128)(2,1)S(1)}, bf16[8,128,2,128]{3,2,1,0:T(2,128)(2,1)S(1)}) fusion(bf16[8,128,2,512]{3,2,1,0:T(2,128)(2,1)} %param.13), kind=kLoop, calls=%fused_computation.14 | loop fusion | bytes 4194304 | tf_op jit(solution)/shard_map/slice | solution.py:325
  3.0 0.9 %query_messages.1 = (bf16[272,128]{1,0:T(8,128)(2,1)S(1)}, bf16[272,128]{1,0:T(8,128)(2,1)S(1)}, bf16[272,128]{1,0:T(8,128)(2,1)S(1)}, bf16[272,128]{1,0:T(8,128)(2,1)S(1)}) custom-call(s32[8]{0:T(128)S(1)} %stack.41.meta_ref, s32[1,128]{1,0:T(1,128)S(1)} %copy-done.4, s32[4,64]{1,0:T(4,128)S(1)} %copy-done.2, s32[4]{0:T(128)S(1)} %copy-done.3, ...), custom_call_target="tpu_custom_call" | custom-call | bytes 524288 | tf_op jit(solution)/shard_map/query_messages/pallas_call | solution.py:327
  3.9 1.6 %collective-permute-start.1 = (bf16[272,128]{1,0:T(8,128)(2,1)S(1)}, bf16[272,128]{1,0:T(8,128)(2,1)S(1)}, u32[]{:S(2)}, u32[]{:S(2)}) collective-permute-start(bf16[272,128]{1,0:T(8,128)(2,1)S(1)} %get-tuple-element.29.q1), channel_id=1, source_target_pairs={{0,1},{1,2},{2,3},{3,0},{4,5},{5,6},{6,7},{7,4},{8,9},{9,10},{10,1... | collective-permute-start | bytes 208904 | tf_op jit(solution)/shard_map/ppermute | solution.py:313
  5.5 2.7 %collective-permute-start.2 = (bf16[272,128]{1,0:T(8,128)(2,1)S(1)}, bf16[272,128]{1,0:T(8,128)(2,1)S(1)}, u32[]{:S(2)}, u32[]{:S(2)}) collective-permute-start(bf16[272,128]{1,0:T(8,128)(2,1)S(1)} %get-tuple-element.30.q2), channel_id=1, source_target_pairs={{0,2},{1,3},{2,0},{3,1},{4,6},{5,7},{6,4},{7,5},{8,10},{9,11},{10,... | collective-permute-start | bytes 208904 | tf_op jit(solution)/shard_map/ppermute | solution.py:313
  8.3 1.4 %collective-permute-start.3 = (bf16[272,128]{1,0:T(8,128)(2,1)S(1)}, bf16[272,128]{1,0:T(8,128)(2,1)S(1)}, u32[]{:S(2)}, u32[]{:S(2)}) collective-permute-start(bf16[272,128]{1,0:T(8,128)(2,1)S(1)} %get-tuple-element.31.q3), channel_id=1, source_target_pairs={{0,3},{1,0},{2,1},{3,2},{4,7},{5,4},{6,5},{7,6},{8,11},{9,8},{10,9... | collective-permute-start | bytes 208904 | tf_op jit(solution)/shard_map/ppermute | solution.py:313
  9.7 1.6 %pad_maximum_fusion = bf16[4,2048,128]{2,1,0:T(8,128)(2,1)} fusion(bf16[1,2048,128]{2,1,0:T(8,128)(2,1)S(1)} %bitcast.35, bf16[1,2048,128]{2,1,0:T(8,128)(2,1)S(1)} %bitcast.36, bf16[1,2048,128]{2,1,0:T(8,128)(2,1)S(1)} %bitcast.34, bf16[1,2048,128]{2,1,0:T(8,128)(2,1)S(1)} %bitcast.33), kind=kLoop, calls=%fused_computation | loop fusion | flops 3145728 | bytes 4194304 | tf_op jit(solution)/shard_map/stack | solution.py:325
  11.3 1.2 %collective-permute-done.3.m3 = bf16[272,128]{1,0:T(8,128)(2,1)S(1)} collective-permute-done((bf16[272,128]{1,0:T(8,128)(2,1)S(1)}, bf16[272,128]{1,0:T(8,128)(2,1)S(1)}, u32[]{:S(2)}, u32[]{:S(2)}) %collective-permute-start.3) | collective-permute-done | bytes 69664 | tf_op jit(solution)/shard_map/ppermute | solution.py:313
  12.6 3.9 %all-to-all-start = ((bf16[4,2048,128]{2,1,0:T(8,128)(2,1)}), bf16[4,2048,128]{2,1,0:T(8,128)(2,1)S(1)}, u32[]{:S(2)}, u32[]{:S(2)}) async-start(bf16[4,2048,128]{2,1,0:T(8,128)(2,1)} %pad_maximum_fusion), calls=%async_computation | async-start | bytes 4194304 | tf_op jit(solution)/shard_map/all_to_all | solution.py:339
  17.1 1.6 %collective-permute-start.4 = (bf16[4,208,128]{2,1,0:T(8,128)(2,1)S(1)}, bf16[4,208,128]{2,1,0:T(8,128)(2,1)S(1)}, u32[]{:S(2)}, u32[]{:S(2)}) collective-permute-start(bf16[4,208,128]{2,1,0:T(8,128)(2,1)S(1)} %get-tuple-element.36.refs_0_), channel_id=1, source_target_pairs={{0,4},{1,5},{2,6},{3,7},{4,8},{5,9},{6,10},{7,11},{8,12},{9,13},{1... | collective-permute-start | bytes 638984 | tf_op jit(solution)/shard_map/ppermute | solution.py:313
  18.7 2.9 %collective-permute-start.5 = (bf16[4,208,128]{2,1,0:T(8,128)(2,1)S(1)}, bf16[4,208,128]{2,1,0:T(8,128)(2,1)S(1)}, u32[]{:S(2)}, u32[]{:S(2)}) collective-permute-start(bf16[4,208,128]{2,1,0:T(8,128)(2,1)S(1)} %get-tuple-element.36.refs_0_), channel_id=1, source_target_pairs={{0,8},{1,9},{2,10},{3,11},{4,12},{5,13},{6,14},{7,15},{8,0},{9,1},... | collective-permute-start | bytes 638984 | tf_op jit(solution)/shard_map/ppermute | solution.py:313
  21.6 1.3 %collective-permute-start.6 = (bf16[4,208,128]{2,1,0:T(8,128)(2,1)S(1)}, bf16[4,208,128]{2,1,0:T(8,128)(2,1)S(1)}, u32[]{:S(2)}, u32[]{:S(2)}) collective-permute-start(bf16[4,208,128]{2,1,0:T(8,128)(2,1)S(1)} %get-tuple-element.36.refs_0_), channel_id=1, source_target_pairs={{0,12},{1,13},{2,14},{3,15},{4,0},{5,1},{6,2},{7,3},{8,4},{9,5},{1... | collective-permute-start | bytes 638984 | tf_op jit(solution)/shard_map/ppermute | solution.py:313
  23.0 1.9 %collective-permute-start.7 = (bf16[2,128,128]{2,1,0:T(8,128)(2,1)S(1)}, bf16[2,128,128]{2,1,0:T(8,128)(2,1)S(1)}, u32[]{:S(2)}, u32[]{:S(2)}) collective-permute-start(bf16[2,128,128]{2,1,0:T(8,128)(2,1)S(1)} %get-tuple-element.38.refs_5_), channel_id=1, source_target_pairs={{0,32},{1,33},{2,34},{3,35},{4,36},{5,37},{6,38},{7,39},{8,40},{9,... | collective-permute-start | bytes 196616 | tf_op jit(solution)/shard_map/ppermute | solution.py:350
  25.0 3.7 %collective-permute-start.8 = (bf16[2,128,128]{2,1,0:T(8,128)(2,1)S(1)}, bf16[2,128,128]{2,1,0:T(8,128)(2,1)S(1)}, u32[]{:S(2)}, u32[]{:S(2)}) collective-permute-start(bf16[2,128,128]{2,1,0:T(8,128)(2,1)S(1)} %get-tuple-element.38.refs_5_), channel_id=1, source_target_pairs={{0,64},{1,65},{2,66},{3,67},{4,68},{5,69},{6,70},{7,71},{8,72},{9,... | collective-permute-start | bytes 196616 | tf_op jit(solution)/shard_map/ppermute | solution.py:350
  29.2 2.0 %collective-permute-start.9 = (bf16[2,128,128]{2,1,0:T(8,128)(2,1)S(1)}, bf16[2,128,128]{2,1,0:T(8,128)(2,1)S(1)}, u32[]{:S(2)}, u32[]{:S(2)}) collective-permute-start(bf16[2,128,128]{2,1,0:T(8,128)(2,1)S(1)} %get-tuple-element.38.refs_5_), channel_id=1, source_target_pairs={{0,96},{1,97},{2,98},{3,99},{4,100},{5,101},{6,102},{7,103},{8,104... | collective-permute-start | bytes 196616 | tf_op jit(solution)/shard_map/ppermute | solution.py:350
  31.3 0.8 %constant_dynamic-slice_fusion.2 = (bf16[4,3,2,128]{3,2,1,0:T(2,128)(2,1)S(1)}, bf16[4,3,2,128]{3,2,1,0:T(2,128)(2,1)S(1)}, bf16[4,3,2,128]{3,2,1,0:T(2,128)(2,1)S(1)}, bf16[4,3,2,128]{3,2,1,0:T(2,128)(2,1)S(1)}) fusion(bf16[4,3,2,512]{3,2,1,0:T(2,128)(2,1)} %param.10, s32[]{:T(128)S(6)} %select_n.84, s32[]{:T(128)S(6)} %select_n.86, s32[]{:T(128)S(6)} %select_n.90, ...), kind=kLoop, calls=%fused_computation.7 | loop fusion | bytes 49168 | tf_op jit(solution)/shard_map/dynamic_slice | solution.py:323
  32.0 1.5 %collective-permute-done.9.refs_8_ = bf16[2,128,128]{2,1,0:T(8,128)(2,1)S(1)} collective-permute-done((bf16[2,128,128]{2,1,0:T(8,128)(2,1)S(1)}, bf16[2,128,128]{2,1,0:T(8,128)(2,1)S(1)}, u32[]{:S(2)}, u32[]{:S(2)}) %collective-permute-start.9) | collective-permute-done | bytes 65568 | tf_op jit(solution)/shard_map/ppermute | solution.py:350
  33.5 3.3 %all-to-all-done.refs_4_ = bf16[4,2048,128]{2,1,0:T(8,128)(2,1)S(1)} async-done(((bf16[4,2048,128]{2,1,0:T(8,128)(2,1)}), bf16[4,2048,128]{2,1,0:T(8,128)(2,1)S(1)}, u32[]{:S(2)}, u32[]{:S(2)}) %all-to-all-start) | async-done | bytes 2097184 | tf_op jit(solution)/shard_map/all_to_all | solution.py:339
  36.8 12.5 %attend.1 = (bf16[4,208,128]{2,1,0:T(8,128)(2,1)S(1)}, bf16[4,208,128]{2,1,0:T(8,128)(2,1)S(1)}, bf16[4,208,128]{2,1,0:T(8,128)(2,1)S(1)}, bf16[4,208,128]{2,1,0:T(8,128)(2,1)S(1)}) custom-call(s32[8]{0:T(128)S(1)} %stack.41.meta_ref, s32[128]{0:T(128)S(1)} %select_reduce_fusion.owner_ref, bf16[4,208,128]{2,1,0:T(8,128)(2,1)S(1)} %get-tuple-element.36.refs_0_, ...), custom_call_target="tpu_custom_call" | custom-call | flops 8589934592 | bytes 4194304 | tf_op jit(solution)/shard_map/attend/pallas_call | solution.py:355
  49.3 2.9 %collective-permute-start.10 = (bf16[4,208,128]{2,1,0:T(8,128)(2,1)S(1)}, bf16[4,208,128]{2,1,0:T(8,128)(2,1)S(1)}, u32[]{:S(2)}, u32[]{:S(2)}) collective-permute-start(bf16[4,208,128]{2,1,0:T(8,128)(2,1)S(1)} %get-tuple-element.41), channel_id=1, source_target_pairs={{0,12},{1,13},{2,14},{3,15},{4,0},{5,1},{6,2},{7,3},{8,4},{9,5},{1... | collective-permute-start | bytes 638984 | tf_op jit(solution)/shard_map/ppermute | solution.py:313
  52.2 0.9 %collective-permute-start.11 = (bf16[4,208,128]{2,1,0:T(8,128)(2,1)S(1)}, bf16[4,208,128]{2,1,0:T(8,128)(2,1)S(1)}, u32[]{:S(2)}, u32[]{:S(2)}) collective-permute-start(bf16[4,208,128]{2,1,0:T(8,128)(2,1)S(1)} %get-tuple-element.42), channel_id=1, source_target_pairs={{0,8},{1,9},{2,10},{3,11},{4,12},{5,13},{6,14},{7,15},{8,0},{9,1},... | collective-permute-start | bytes 638984 | tf_op jit(solution)/shard_map/ppermute | solution.py:313
  53.1 0.9 %collective-permute-start.12 = (bf16[4,208,128]{2,1,0:T(8,128)(2,1)S(1)}, bf16[4,208,128]{2,1,0:T(8,128)(2,1)S(1)}, u32[]{:S(2)}, u32[]{:S(2)}) collective-permute-start(bf16[4,208,128]{2,1,0:T(8,128)(2,1)S(1)} %get-tuple-element.43), channel_id=1, source_target_pairs={{0,4},{1,5},{2,6},{3,7},{4,8},{5,9},{6,10},{7,11},{8,12},{9,13},{1... | collective-permute-start | bytes 638984 | tf_op jit(solution)/shard_map/ppermute | solution.py:313
  54.0 1.9 %constant_dynamic-slice_fusion.3 = (bf16[4,256,2,128]{3,2,1,0:T(2,128)(2,1)S(1)}, bf16[4,256,2,128]{3,2,1,0:T(2,128)(2,1)S(1)}, bf16[4,256,2,128]{3,2,1,0:T(2,128)(2,1)S(1)}, bf16[4,256,2,128]{3,2,1,0:T(2,128)(2,1)S(1)}) fusion(bf16[4,256,2,512]{3,2,1,0:T(2,128)(2,1)S(1)} %copy-done.6, s32[]{:T(128)S(6)} %select_n.90, s32[]{:T(128)S(6)} %select_n.86, ...), kind=kLoop, calls=%fused_computation.8 | loop fusion | bytes 4194320 | tf_op jit(solution)/shard_map/dynamic_slice | solution.py:323
  55.9 2.0 %collective-permute-done.10.c1 = bf16[4,208,128]{2,1,0:T(8,128)(2,1)S(1)} collective-permute-done((bf16[4,208,128]{2,1,0:T(8,128)(2,1)S(1)}, bf16[4,208,128]{2,1,0:T(8,128)(2,1)S(1)}, u32[]{:S(2)}, u32[]{:S(2)}) %collective-permute-start.10) | collective-permute-done | bytes 213024 | tf_op jit(solution)/shard_map/ppermute | solution.py:313
  57.9 1.8 %collective-permute-done.11.c2 = bf16[4,208,128]{2,1,0:T(8,128)(2,1)S(1)} collective-permute-done((bf16[4,208,128]{2,1,0:T(8,128)(2,1)S(1)}, bf16[4,208,128]{2,1,0:T(8,128)(2,1)S(1)}, u32[]{:S(2)}, u32[]{:S(2)}) %collective-permute-start.11) | collective-permute-done | bytes 213024 | tf_op jit(solution)/shard_map/ppermute | solution.py:313
  59.7 2.2 %collective-permute-done.12.c3 = bf16[4,208,128]{2,1,0:T(8,128)(2,1)S(1)} collective-permute-done((bf16[4,208,128]{2,1,0:T(8,128)(2,1)S(1)}, bf16[4,208,128]{2,1,0:T(8,128)(2,1)S(1)}, u32[]{:S(2)}, u32[]{:S(2)}) %collective-permute-start.12) | collective-permute-done | bytes 213024 | tf_op jit(solution)/shard_map/ppermute | solution.py:313
  61.9 1.2 %combine.1 = (bf16[208,128]{1,0:T(8,128)(2,1)S(1)}, bf16[208,128]{1,0:T(8,128)(2,1)S(1)}, bf16[208,128]{1,0:T(8,128)(2,1)S(1)}, bf16[208,128]{1,0:T(8,128)(2,1)S(1)}) custom-call(s32[8]{0:T(128)S(1)} %stack.41.meta_ref, bf16[4,208,128]{2,1,0:T(8,128)(2,1)S(1)} %get-tuple-element.40.c0, bf16[4,208,128]{2,1,0:T(8,128)(2,1)S(1)} %collective-permute-done.10.c1, ...), custom_call_target="tpu_custom_call" | custom-call | bytes 1048576 | tf_op jit(solution)/shard_map/combine/pallas_call | solution.py:394
  63.1 2.2 %collective-permute-start.13 = (bf16[208,128]{1,0:T(8,128)(2,1)S(1)}, bf16[208,128]{1,0:T(8,128)(2,1)S(1)}, u32[]{:S(2)}, u32[]{:S(2)}) collective-permute-start(bf16[208,128]{1,0:T(8,128)(2,1)S(1)} %get-tuple-element.45), channel_id=1, source_target_pairs={{0,3},{1,0},{2,1},{3,2},{4,7},{5,4},{6,5},{7,6},{8,11},{9,8},{10,9... | collective-permute-start | bytes 159752 | tf_op jit(solution)/shard_map/ppermute | solution.py:313
  65.3 1.5 %collective-permute-start.14 = (bf16[208,128]{1,0:T(8,128)(2,1)S(1)}, bf16[208,128]{1,0:T(8,128)(2,1)S(1)}, u32[]{:S(2)}, u32[]{:S(2)}) collective-permute-start(bf16[208,128]{1,0:T(8,128)(2,1)S(1)} %get-tuple-element.46), channel_id=1, source_target_pairs={{0,2},{1,3},{2,0},{3,1},{4,6},{5,7},{6,4},{7,5},{8,10},{9,11},{10,... | collective-permute-start | bytes 159752 | tf_op jit(solution)/shard_map/ppermute | solution.py:313
  66.7 2.8 %own_tokens.1 = (f32[4,192,128]{2,1,0:T(8,128)S(1)}, f32[4,8,128]{2,1,0:T(8,128)S(1)}) custom-call(s32[4]{0:T(128)S(1)} %copy-done.5, bf16[272,128]{1,0:T(8,128)(2,1)S(1)} %get-tuple-element.32.m0.q0, bf16[272,128]{1,0:T(8,128)(2,1)S(1)} %get-tuple-element.29.q1, bf16[272,128]{1,0:T(8,128)(2,1)S(1)} %get-tuple-element.30.q2, ...), custom_call_target="tpu_custom_call" | custom-call | flops 1073741824 | bytes 4194304 | tf_op jit(solution)/shard_map/own_tokens/pallas_call | solution.py:380
  69.6 1.3 %collective-permute-done.14.r2 = bf16[208,128]{1,0:T(8,128)(2,1)S(1)} collective-permute-done((bf16[208,128]{1,0:T(8,128)(2,1)S(1)}, bf16[208,128]{1,0:T(8,128)(2,1)S(1)}, u32[]{:S(2)}, u32[]{:S(2)}) %collective-permute-start.14) | collective-permute-done | bytes 53280 | tf_op jit(solution)/shard_map/ppermute | solution.py:313
  70.9 1.2 %collective-permute-done.15.r3 = bf16[208,128]{1,0:T(8,128)(2,1)S(1)} collective-permute-done((bf16[208,128]{1,0:T(8,128)(2,1)S(1)}, bf16[208,128]{1,0:T(8,128)(2,1)S(1)}, u32[]{:S(2)}, u32[]{:S(2)}) %collective-permute-start.15) | collective-permute-done | bytes 53280 | tf_op jit(solution)/shard_map/ppermute | solution.py:313
  72.1 1.7 %final.1 = bf16[3,4,64,128]{3,2,1,0:T(8,128)(2,1)} custom-call(s32[8]{0:T(128)S(1)} %stack.41.meta_ref, bf16[208,128]{1,0:T(8,128)(2,1)S(1)} %get-tuple-element.44.r0, bf16[208,128]{1,0:T(8,128)(2,1)S(1)} %collective-permute-done.13.r1, bf16[208,128]{1,0:T(8,128)(2,1)S(1)} %collective-permute-done.14.r2, bf16[208,128]{1,0:T(8,128)(2,1)S(1)} %collective-permute-done.15.r3, ...), custom_call_target="tpu_custom_call" | custom-call | tf_op jit(solution)/shard_map/final/pallas_call | solution.py:404
  (30 shorter events, 1.5 us)
Async XLA Ops:
  0.0 3.0 %copy-start.1 = (bf16[16,2,512]{2,1,0:T(2,128)(2,1)S(1)}, bf16[16,2,512]{2,1,0:T(2,128)(2,1)}, u32[]{:S(2)}) copy-start(bf16[16,2,512]{2,1,0:T(2,128)(2,1)} %sys_ref.1) | copy-start | bytes 98308
  0.0 3.0 %copy-start.4 = (s32[1,128]{1,0:T(1,128)S(1)}, s32[1,128]{1,0:T(1,128)}, u32[]{:S(2)}) copy-start(s32[1,128]{1,0:T(1,128)} %slot_ref.1) | copy-start | bytes 1540
  0.0 3.0 %copy-start.2 = (s32[4,64]{1,0:T(4,128)S(1)}, s32[4,64]{1,0:T(4,128)}, u32[]{:S(2)}) copy-start(s32[4,64]{1,0:T(4,128)} %list_ref.1) | copy-start | bytes 3076
  0.0 3.0 %copy-start.3 = (s32[4]{0:T(128)S(1)}, s32[4]{0:T(128)}, u32[]{:S(2)}) copy-start(s32[4]{0:T(128)} %used_ref.1) | copy-start | bytes 52
  0.0 3.0 %copy-start = (bf16[4,3,8192]{2,0,1:T(4,128)(2,1)S(1)}, bf16[4,3,8192]{2,0,1:T(4,128)(2,1)}, u32[]{:S(2)}) copy-start(bf16[4,3,8192]{2,0,1:T(4,128)(2,1)} %param.9) | copy-start | bytes 589828
  0.0 3.0 %collective-permute-start = (bf16[16,2,512]{2,1,0:T(2,128)(2,1)}, bf16[16,2,512]{2,1,0:T(2,128)(2,1)S(1)}, u32[]{:S(2)}, u32[]{:S(2)}) collective-permute-start(bf16[16,2,512]{2,1,0:T(2,128)(2,1)} %sys_ref.1), channel_id=1, source_target_pairs={{0,16},{1,17},{2,18},{3,19},{4,20},{5,21},{6,22},{7,23},{8,24},{9,... | collective-permute-start | bytes 98312 | tf_op jit(solution)/shard_map/ppermute | solution.py:320
  3.9 7.4 %collective-permute-start.1 = (bf16[272,128]{1,0:T(8,128)(2,1)S(1)}, bf16[272,128]{1,0:T(8,128)(2,1)S(1)}, u32[]{:S(2)}, u32[]{:S(2)}) collective-permute-start(bf16[272,128]{1,0:T(8,128)(2,1)S(1)} %get-tuple-element.29.q1), channel_id=1, source_target_pairs={{0,1},{1,2},{2,3},{3,0},{4,5},{5,6},{6,7},{7,4},{8,9},{9,10},{10,1... | collective-permute-start | bytes 208904 | tf_op jit(solution)/shard_map/ppermute | solution.py:313
  5.5 5.8 %collective-permute-start.2 = (bf16[272,128]{1,0:T(8,128)(2,1)S(1)}, bf16[272,128]{1,0:T(8,128)(2,1)S(1)}, u32[]{:S(2)}, u32[]{:S(2)}) collective-permute-start(bf16[272,128]{1,0:T(8,128)(2,1)S(1)} %get-tuple-element.30.q2), channel_id=1, source_target_pairs={{0,2},{1,3},{2,0},{3,1},{4,6},{5,7},{6,4},{7,5},{8,10},{9,11},{10,... | collective-permute-start | bytes 208904 | tf_op jit(solution)/shard_map/ppermute | solution.py:313
  8.3 4.3 %collective-permute-start.3 = (bf16[272,128]{1,0:T(8,128)(2,1)S(1)}, bf16[272,128]{1,0:T(8,128)(2,1)S(1)}, u32[]{:S(2)}, u32[]{:S(2)}) collective-permute-start(bf16[272,128]{1,0:T(8,128)(2,1)S(1)} %get-tuple-element.31.q3), channel_id=1, source_target_pairs={{0,3},{1,0},{2,1},{3,2},{4,7},{5,4},{6,5},{7,6},{8,11},{9,8},{10,9... | collective-permute-start | bytes 208904 | tf_op jit(solution)/shard_map/ppermute | solution.py:313
  12.6 24.2 %all-to-all-start = ((bf16[4,2048,128]{2,1,0:T(8,128)(2,1)}), bf16[4,2048,128]{2,1,0:T(8,128)(2,1)S(1)}, u32[]{:S(2)}, u32[]{:S(2)}) async-start(bf16[4,2048,128]{2,1,0:T(8,128)(2,1)} %pad_maximum_fusion), calls=%async_computation | async-start | bytes 4194304 | tf_op jit(solution)/shard_map/all_to_all | solution.py:339
  17.1 16.4 %collective-permute-start.4 = (bf16[4,208,128]{2,1,0:T(8,128)(2,1)S(1)}, bf16[4,208,128]{2,1,0:T(8,128)(2,1)S(1)}, u32[]{:S(2)}, u32[]{:S(2)}) collective-permute-start(bf16[4,208,128]{2,1,0:T(8,128)(2,1)S(1)} %get-tuple-element.36.refs_0_), channel_id=1, source_target_pairs={{0,4},{1,5},{2,6},{3,7},{4,8},{5,9},{6,10},{7,11},{8,12},{9,13},{1... | collective-permute-start | bytes 638984 | tf_op jit(solution)/shard_map/ppermute | solution.py:313
  18.7 14.8 %collective-permute-start.5 = (bf16[4,208,128]{2,1,0:T(8,128)(2,1)S(1)}, bf16[4,208,128]{2,1,0:T(8,128)(2,1)S(1)}, u32[]{:S(2)}, u32[]{:S(2)}) collective-permute-start(bf16[4,208,128]{2,1,0:T(8,128)(2,1)S(1)} %get-tuple-element.36.refs_0_), channel_id=1, source_target_pairs={{0,8},{1,9},{2,10},{3,11},{4,12},{5,13},{6,14},{7,15},{8,0},{9,1},... | collective-permute-start | bytes 638984 | tf_op jit(solution)/shard_map/ppermute | solution.py:313
  21.6 11.9 %collective-permute-start.6 = (bf16[4,208,128]{2,1,0:T(8,128)(2,1)S(1)}, bf16[4,208,128]{2,1,0:T(8,128)(2,1)S(1)}, u32[]{:S(2)}, u32[]{:S(2)}) collective-permute-start(bf16[4,208,128]{2,1,0:T(8,128)(2,1)S(1)} %get-tuple-element.36.refs_0_), channel_id=1, source_target_pairs={{0,12},{1,13},{2,14},{3,15},{4,0},{5,1},{6,2},{7,3},{8,4},{9,5},{1... | collective-permute-start | bytes 638984 | tf_op jit(solution)/shard_map/ppermute | solution.py:313
  23.0 6.3 %collective-permute-start.7 = (bf16[2,128,128]{2,1,0:T(8,128)(2,1)S(1)}, bf16[2,128,128]{2,1,0:T(8,128)(2,1)S(1)}, u32[]{:S(2)}, u32[]{:S(2)}) collective-permute-start(bf16[2,128,128]{2,1,0:T(8,128)(2,1)S(1)} %get-tuple-element.38.refs_5_), channel_id=1, source_target_pairs={{0,32},{1,33},{2,34},{3,35},{4,36},{5,37},{6,38},{7,39},{8,40},{9,... | collective-permute-start | bytes 196616 | tf_op jit(solution)/shard_map/ppermute | solution.py:350
  25.0 7.0 %collective-permute-start.8 = (bf16[2,128,128]{2,1,0:T(8,128)(2,1)S(1)}, bf16[2,128,128]{2,1,0:T(8,128)(2,1)S(1)}, u32[]{:S(2)}, u32[]{:S(2)}) collective-permute-start(bf16[2,128,128]{2,1,0:T(8,128)(2,1)S(1)} %get-tuple-element.38.refs_5_), channel_id=1, source_target_pairs={{0,64},{1,65},{2,66},{3,67},{4,68},{5,69},{6,70},{7,71},{8,72},{9,... | collective-permute-start | bytes 196616 | tf_op jit(solution)/shard_map/ppermute | solution.py:350
  29.2 4.3 %collective-permute-start.9 = (bf16[2,128,128]{2,1,0:T(8,128)(2,1)S(1)}, bf16[2,128,128]{2,1,0:T(8,128)(2,1)S(1)}, u32[]{:S(2)}, u32[]{:S(2)}) collective-permute-start(bf16[2,128,128]{2,1,0:T(8,128)(2,1)S(1)} %get-tuple-element.38.refs_5_), channel_id=1, source_target_pairs={{0,96},{1,97},{2,98},{3,99},{4,100},{5,101},{6,102},{7,103},{8,104... | collective-permute-start | bytes 196616 | tf_op jit(solution)/shard_map/ppermute | solution.py:350
  36.8 17.1 %copy-start.6 = (bf16[4,256,2,512]{3,2,1,0:T(2,128)(2,1)S(1)}, bf16[4,256,2,512]{3,2,1,0:T(2,128)(2,1)}, u32[]{:S(2)}) copy-start(bf16[4,256,2,512]{3,2,1,0:T(2,128)(2,1)} %param.11) | copy-start | bytes 6291460
  49.3 8.6 %collective-permute-start.10 = (bf16[4,208,128]{2,1,0:T(8,128)(2,1)S(1)}, bf16[4,208,128]{2,1,0:T(8,128)(2,1)S(1)}, u32[]{:S(2)}, u32[]{:S(2)}) collective-permute-start(bf16[4,208,128]{2,1,0:T(8,128)(2,1)S(1)} %get-tuple-element.41), channel_id=1, source_target_pairs={{0,12},{1,13},{2,14},{3,15},{4,0},{5,1},{6,2},{7,3},{8,4},{9,5},{1... | collective-permute-start | bytes 638984 | tf_op jit(solution)/shard_map/ppermute | solution.py:313
  52.2 7.5 %collective-permute-start.11 = (bf16[4,208,128]{2,1,0:T(8,128)(2,1)S(1)}, bf16[4,208,128]{2,1,0:T(8,128)(2,1)S(1)}, u32[]{:S(2)}, u32[]{:S(2)}) collective-permute-start(bf16[4,208,128]{2,1,0:T(8,128)(2,1)S(1)} %get-tuple-element.42), channel_id=1, source_target_pairs={{0,8},{1,9},{2,10},{3,11},{4,12},{5,13},{6,14},{7,15},{8,0},{9,1},... | collective-permute-start | bytes 638984 | tf_op jit(solution)/shard_map/ppermute | solution.py:313
  53.1 8.8 %collective-permute-start.12 = (bf16[4,208,128]{2,1,0:T(8,128)(2,1)S(1)}, bf16[4,208,128]{2,1,0:T(8,128)(2,1)S(1)}, u32[]{:S(2)}, u32[]{:S(2)}) collective-permute-start(bf16[4,208,128]{2,1,0:T(8,128)(2,1)S(1)} %get-tuple-element.43), channel_id=1, source_target_pairs={{0,4},{1,5},{2,6},{3,7},{4,8},{5,9},{6,10},{7,11},{8,12},{9,13},{1... | collective-permute-start | bytes 638984 | tf_op jit(solution)/shard_map/ppermute | solution.py:313
  54.0 12.8 %copy-start.5 = (s32[4]{0:T(128)S(1)}, s32[4]{0:T(128)}, u32[]{:S(2)}) copy-start(s32[4]{0:T(128)} %lens_ref) | copy-start | bytes 52
  63.1 6.5 %collective-permute-start.13 = (bf16[208,128]{1,0:T(8,128)(2,1)S(1)}, bf16[208,128]{1,0:T(8,128)(2,1)S(1)}, u32[]{:S(2)}, u32[]{:S(2)}) collective-permute-start(bf16[208,128]{1,0:T(8,128)(2,1)S(1)} %get-tuple-element.45), channel_id=1, source_target_pairs={{0,3},{1,0},{2,1},{3,2},{4,7},{5,4},{6,5},{7,6},{8,11},{9,8},{10,9... | collective-permute-start | bytes 159752 | tf_op jit(solution)/shard_map/ppermute | solution.py:313
  65.3 5.6 %collective-permute-start.14 = (bf16[208,128]{1,0:T(8,128)(2,1)S(1)}, bf16[208,128]{1,0:T(8,128)(2,1)S(1)}, u32[]{:S(2)}, u32[]{:S(2)}) collective-permute-start(bf16[208,128]{1,0:T(8,128)(2,1)S(1)} %get-tuple-element.46), channel_id=1, source_target_pairs={{0,2},{1,3},{2,0},{3,1},{4,6},{5,7},{6,4},{7,5},{8,10},{9,11},{10,... | collective-permute-start | bytes 159752 | tf_op jit(solution)/shard_map/ppermute | solution.py:313
  66.7 5.3 %collective-permute-start.15 = (bf16[208,128]{1,0:T(8,128)(2,1)S(1)}, bf16[208,128]{1,0:T(8,128)(2,1)S(1)}, u32[]{:S(2)}, u32[]{:S(2)}) collective-permute-start(bf16[208,128]{1,0:T(8,128)(2,1)S(1)} %get-tuple-element.47), channel_id=1, source_target_pairs={{0,1},{1,2},{2,3},{3,0},{4,5},{5,6},{6,7},{7,4},{8,9},{9,10},{10,1... | collective-permute-start | bytes 159752 | tf_op jit(solution)/shard_map/ppermute | solution.py:313

commit v4 on v3

--- a/solution.py
+++ b/solution.py
@@ -75,20 +75,20 @@
     return lax.rem(meta_ref[2] + k, SIDE)
 
 
-def query_kernel(meta_ref, slot_ref, list_ref, used_ref, q_ref, sys_ref, far_ref, o0, o1, o2, o3, tmp, sys_tmp):
+def query_kernel(slot_ref, list_ref, used_ref, q_ref, sys_ref, far_ref, out_ref, tmp, sys_tmp):
     lane = lax.broadcasted_iota(jnp.int32, (16, HD), 1)
     flags = jnp.zeros((16, HD), F32)
     for n in range(64):
         slot = jnp.where(n < used_ref[0], slot_ref[0, list_ref[0, n]], -1)
         flags = jnp.where(lane == slot, 1.0, flags)
-    for k, out in enumerate((o0, o1, o2, o3)):
-        head = turned(meta_ref, k)
+    for head in range(KVH):
+        out = out_ref.at[head]
         for t in range(3):
             for g in range(GQ):
-                at = pl.ds(pl.multiple_of((head * GQ + g) * HD, HD), HD)
+                at = pl.ds((head * GQ + g) * HD, HD)
                 tmp[pl.ds(t * 64 + g * 4, 4), :] = q_ref[t, :, at].astype(F32)
         out[pl.ds(0, ROWS), :] = tmp[...].astype(BF)
-        lanes = pl.ds(pl.multiple_of(head * HD, HD), HD)
+        lanes = pl.ds(head * HD, HD)
         sys_tmp[pl.ds(0, SYS_PART), :] = sys_ref[:, :, lanes].reshape(SYS_PART, HD).astype(F32)
         sys_tmp[pl.ds(SYS_PART, SYS_PART), :] = far_ref[:, :, lanes].reshape(SYS_PART, HD).astype(F32)
         out[pl.ds(MSG, SYS_PART), :] = sys_tmp[pl.ds(0, SYS_PART, stride=2), :].astype(BF)
@@ -96,12 +96,12 @@
         out[pl.ds(ROWS, 16), :] = flags.astype(BF)
 
 
-def stage_kernel(meta_ref, m0, m1, m2, m3, stage_ref, sys_ref):
-    for k, msg in enumerate((m0, m1, m2, m3)):
-        stage_ref[turned(meta_ref, SIDE - k)] = msg[pl.ds(0, MSG), :]
+def stage_kernel(got_ref, stage_ref, sys_ref):
+    for k in range(SIDE):
+        stage_ref[k] = got_ref[k, pl.ds(0, MSG), :]
         for side in range(2):
             at = pl.ds(k * SYS_PART, SYS_PART)
-            sys_ref[side, at, :] = msg[pl.ds(MSG + side * SYS_PART, SYS_PART), :]
+            sys_ref[side, at, :] = got_ref[k, pl.ds(MSG + side * SYS_PART, SYS_PART), :]
 
 
 def flatten_rows(lse):
@@ -223,7 +223,7 @@
         s = following
 
 
-def own_kernel(lens_ref, q0, q1, q2, q3, s0, s1, s2, s3, new_ref, o_ref, lse_ref, bias, tmp, vc):
+def own_kernel(lens_ref, q_ref, s0, s1, s2, s3, new_ref, o_ref, lse_ref, bias, tmp, vc):
     tokens = vc.shape[1]
     comp = lax.broadcasted_iota(jnp.int32, (ROWS, 256), 0) % 4
     place = lax.broadcasted_iota(jnp.int32, (ROWS, 256), 1)
@@ -238,13 +238,13 @@
         vc[n, :, pl.ds(HD, HD)] = jnp.ones((tokens, HD), BF)
         tmp[n, pl.ds(2048, 256), :] = jnp.zeros((256, HD), F32)
 
-    def scores(k, q_ref, kv_ref):
+    def scores(k, kv_ref):
         held = tmp.at[k % 2]
         held[pl.ds(0, 2048), :] = kv_ref[...].astype(F32)
         held[pl.ds(2048, 24), :] = new_ref[k].astype(F32)
         key = held[pl.ds(0, tokens, stride=2), :].astype(BF)
         vc[k % 2, :, pl.ds(0, HD)] = held[pl.ds(1, tokens, stride=2), :].astype(BF)
-        s = lax.dot_general(q_ref[pl.ds(0, ROWS), :], key, NT, preferred_element_type=F32)
+        s = lax.dot_general(q_ref[k, pl.ds(0, ROWS), :], key, NT, preferred_element_type=F32)
         return s + bias[...]
 
     def finish(k, s):
@@ -255,10 +255,10 @@
         o_ref[k] = acc[:, :HD] / total
         lse_ref[k, pl.ds(0, 2), :] = flatten_rows(m * SCALE2 + jnp.log2(total))
 
-    q_refs, kv_refs = (q0, q1, q2, q3), (s0, s1, s2, s3)
-    s = scores(0, q0, s0)
+    kv_refs = (s0, s1, s2, s3)
+    s = scores(0, s0)
     for k in range(KVH):
-        following = scores(k + 1, q_refs[k + 1], kv_refs[k + 1]) if k + 1 < KVH else None
+        following = scores(k + 1, kv_refs[k + 1]) if k + 1 < KVH else None
         finish(k, s)
         s = following
 
@@ -278,12 +278,13 @@
 
 def final_kernel(meta_ref, r0, r1, r2, r3, own_ref, lse_ref, out_ref):
     refs = (r0, r1, r2, r3)
+    heads = [turned(meta_ref, k) for k in range(KVH)]
     weights = [
-        weigh([unpack_flat(ref[pl.ds(ROWS, 16), :]), lse_ref[k, pl.ds(0, 2), :]])[0] for k, ref in enumerate(refs)
+        weigh([unpack_flat(ref[pl.ds(ROWS, 16), :]), lse_ref[head, pl.ds(0, 2), :]])[0]
+        for head, ref in zip(heads, refs)
     ]
-    outs = [[ref[pl.ds(0, ROWS), :].astype(F32), own_ref[k]] for k, ref in enumerate(refs)]
-    for k, mixed in enumerate(mix_all(weights, outs)):
-        head = turned(meta_ref, k)
+    outs = [[ref[pl.ds(0, ROWS), :].astype(F32), own_ref[head]] for head, ref in zip(heads, refs)]
+    for head, mixed in zip(heads, mix_all(weights, outs)):
         for t in range(3):
             out_ref[t, head] = mixed[t * 64 : (t + 1) * 64].astype(BF)
 
@@ -319,33 +320,36 @@
 
     far_sys = lax.ppermute(sys_kv, AXES, core_pairs(prompts))
 
-    def one_head(array, k):
-        return lax.dynamic_slice_in_dim(array, ((a + k) % SIDE) * HD, HD, array.ndim - 1).reshape(-1, HD)
-
-    by_head = jnp.stack([pool_kv[..., h * HD : (h + 1) * HD].reshape(-1, HD) for h in range(KVH)])
-
-    q_msgs = pl.pallas_call(
+    def split_heads(array):
+        return [array[..., h * HD : (h + 1) * HD].reshape(-1, HD) for h in range(KVH)]
+
+    def exchange(array):
+        return lax.all_to_all(array, AXES, 0, 0, axis_index_groups=ring_groups(prompts, "a"), tiled=True)
+
+    by_head = jnp.stack(split_heads(pool_kv))
+
+    q_msg = pl.pallas_call(
         query_kernel,
-        in_specs=[SMEM] * 4 + [VMEM] * 3,
-        out_specs=[VMEM] * 4,
-        out_shape=[shaped((MSG + 2 * SYS_PART, HD))] * 4,
+        in_specs=[SMEM] * 3 + [VMEM] * 3,
+        out_specs=VMEM,
+        out_shape=shaped((KVH, MSG + 2 * SYS_PART, HD)),
         scratch_shapes=[pltpu.VMEM((ROWS, HD), F32), pltpu.VMEM((2 * SYS_PART, HD), F32)],
         compiler_params=room(10),
         cost_estimate=cost(0, 2**19),
         name="query_messages",
-    )(meta, block_slot, block_list, prefix_blocks, queries.transpose(1, 0, 2), sys_kv, far_sys)
-    q_got = [q_msgs[0]] + [send(q_msgs[k], "a", k) for k in (1, 2, 3)]
-    by_head, *q_got = lax.optimization_barrier((by_head, *q_got))
-    pool = lax.all_to_all(by_head, AXES, 0, 0, axis_index_groups=ring_groups(prompts, "a"), tiled=True)
+    )(block_slot, block_list, prefix_blocks, queries.transpose(1, 0, 2), sys_kv, far_sys)
+    q_got = exchange(q_msg)
+    by_head, q_got = lax.optimization_barrier((by_head, q_got))
+    pool = exchange(by_head)
     stage, sys_one = pl.pallas_call(
         stage_kernel,
-        in_specs=[SMEM] + [VMEM] * 4,
+        in_specs=[VMEM],
         out_specs=[VMEM] * 2,
         out_shape=[shaped((SIDE, MSG, HD)), shaped((2, BLK, HD))],
         compiler_params=room(8),
         cost_estimate=cost(0, 2**19),
         name="stage",
-    )(meta, *q_got)
+    )(q_got)
     columns = [stage] + [send(stage, "b", j) for j in (1, 2, 3)]
     system = [sys_one] + [lax.ppermute(sys_one, AXES, plane_pairs(prompts, k)) for k in (1, 2, 3)]
 
@@ -376,10 +380,10 @@
     parts = list(parts)
     parts = [parts[0]] + [send(parts[j], "b", -j) for j in (1, 2, 3)]
     suffix_len, parts[0] = lax.optimization_barrier((suffix_len, parts[0]))
-    new_heads = jnp.stack([one_head(new_kv, k) for k in range(KVH)])
+    new_heads = jnp.stack(split_heads(new_kv))
     own_out, own_lse = pl.pallas_call(
         own_kernel,
-        in_specs=[SMEM] + [VMEM] * 9,
+        in_specs=[SMEM] + [VMEM] * 6,
         out_specs=[VMEM] * 2,
         out_shape=[shaped((KVH, ROWS, HD), F32), shaped((KVH, 8, HD), F32)],
         scratch_shapes=[
@@ -390,7 +394,7 @@
         compiler_params=room(20),
         cost_estimate=cost(2**30, 2**22, 2**20),
         name="own_tokens",
-    )(suffix_len, *q_msgs, *[one_head(suffix_kv, k) for k in range(KVH)], new_heads)
+    )(suffix_len, q_msg, *split_heads(suffix_kv), new_heads)
     back = pl.pallas_call(
         combine_kernel,
         in_specs=[SMEM] + [VMEM] * 4,

time: 74 us -> 76.4 us (1.032)
  waiting for transfers between devices: 15.1 us -> 20.1 us
  starting transfers between devices: 31.5 us -> 30 us
  local copies, waits for them, and re-layouts: 5.49 us -> 4.32 us
    ppermute x12 -> x9, starting transfers between devices: 20 us -> 14.4 us  [send(): return lax.ppermute(array, AXES, ring_pairs(prompts, role, step % SIDE))]
    all_to_all x1 -> x2, waiting for transfers between devices: 3.3 us -> 8.48 us  [exchange(): lax.all_to_all(array, AXES, 0, 0, axis_index_groups=ring_groups(prompts,...]
    all_to_all x1 -> x2, starting transfers between devices: 3.91 us -> 7.99 us  [exchange(): lax.all_to_all(array, AXES, 0, 0, axis_index_groups=ring_groups(prompts,...]
    dynamic_slice x2 -> x0, local copies, waits for them, and re-layouts: 2.65 us -> none  [one_head(): lax.dynamic_slice_in_dim(array, (a + k) % SIDE * HD, HD, array.ndim - 1)]
    slice x1 -> x3, local copies, waits for them, and re-layouts: 2.72 us -> 4.21 us  [split_heads(): return [array[..., h * HD:(h + 1) * HD].reshape(-1, HD) for h in range(KVH)]]
    ppermute x12 -> x9, waiting for transfers between devices: 9.78 us -> 8.58 us  [send(): return lax.ppermute(array, AXES, ring_pairs(prompts, role, step % SIDE))]
    ppermute x3, waiting for transfers between devices: 2.06 us -> 2.99 us  [body(): lax.ppermute(sys_one, AXES, plane_pairs(prompts, k))]
  transfers between devices with their start and end apart: 17 -> 15, of which waited for: 9 -> 10; matrix products, arithmetic and copies ran while one was open for 10% -> 8% of each run, Pallas kernels for 5% -> 4%
where the time goes in v4:
time: 76.4 us; the launch traced here: 76.1 us
  starting transfers between devices  30 us (39%)
  waiting for transfers between devices  20.1 us (26%)
  Pallas kernels  19.8 us (26%)
  local copies, waits for them, and re-layouts  4.32 us (6%)
  other arithmetic  1.73 us (2%)
    ppermute x9, starting transfers between devices, send(): return lax.ppermute(array, AXES, ring_pairs(prompts, role, step % SIDE))  14.4 us
    pallas_call x1, Pallas kernels, body(): pl.pallas_call(main_kernel, grid_spec=pltpu.PrefetchScalarGridSpec(num_sc...  12.3 us
    ppermute x9, waiting for transfers between devices, send(): return lax.ppermute(array, AXES, ring_pairs(prompts, role, step % SIDE))  8.58 us
    all_to_all x2, waiting for transfers between devices, exchange(): lax.all_to_all(array, AXES, 0, 0, axis_index_groups=ring_groups(prompts,...  8.48 us
    all_to_all x2, starting transfers between devices, exchange(): lax.all_to_all(array, AXES, 0, 0, axis_index_groups=ring_groups(prompts,...  7.99 us
    ppermute x3, starting transfers between devices, body(): lax.ppermute(sys_one, AXES, plane_pairs(prompts, k))  7.52 us
    slice x3, local copies, waits for them, and re-layouts, split_heads(): return [array[..., h * HD:(h + 1) * HD].reshape(-1, HD) for h in range(KVH)]  4.21 us
    pallas_call x1, Pallas kernels, body(): pl.pallas_call(own_kernel, in_specs=[SMEM] + [VMEM] * 6, out_specs=[VMEM]...  3.19 us
  transfers between devices with their start and end apart: 15, of which 10 were waited for; matrix products, arithmetic and copies ran while one was open for 8% of the time, Pallas kernels for 4%

profile of v4, /device:TPU:0, one launch (start us, length us, event | category | flops | bytes accessed | tf_op | source)
XLA Modules:
  0.0 76.1 jit_solution(11651696860676948673)
XLA Ops:
  0.1 2.7 %fusion.2 = (bf16[8,128,2,128]{3,2,1,0:T(2,128)(2,1)S(1)}, bf16[8,128,2,128]{3,2,1,0:T(2,128)(2,1)S(1)}, bf16[8,128,2,128]{3,2,1,0:T(2,128)(2,1)S(1)}, bf16[8,128,2,128]{3,2,1,0:T(2,128)(2,1)S(1)}) fusion(bf16[8,128,2,512]{3,2,1,0:T(2,128)(2,1)} %param.13), kind=kLoop, calls=%fused_computation.7 | loop fusion | bytes 4194304 | tf_op jit(solution)/shard_map/slice | solution.py:324
  2.9 1.4 %query_messages.1.q_ref = bf16[4,272,128]{2,1,0:T(8,128)(2,1)} custom-call(s32[1,128]{1,0:T(1,128)S(1)} %copy-done.4, s32[4,64]{1,0:T(4,128)S(1)} %copy-done.2, s32[4]{0:T(128)S(1)} %copy-done.3, bf16[3,4,8192]{2,1,0:T(4,128)(2,1)S(1)} %bitcast.31, bf16[16,2,512]{2,1,0:T(2,128)(2,1)S(1)} %copy-done.1, bf16[16,2,512]{2,1,0:T(2,128)(2,1)S(1)} %collective-permute-done.far_ref), custom_call_target="tpu_custom_call" | custom-call | bytes 524288 | tf_op jit(solution)/shard_map/query_messages/pallas_call | solution.py:331
  4.3 4.4 %all-to-all-start = ((bf16[4,272,128]{2,1,0:T(8,128)(2,1)}), bf16[4,272,128]{2,1,0:T(8,128)(2,1)S(1)}, u32[]{:S(2)}, u32[]{:S(2)}) async-start(bf16[4,272,128]{2,1,0:T(8,128)(2,1)} %query_messages.1.q_ref), calls=%async_computation | async-start | bytes 557056 | tf_op jit(solution)/shard_map/all_to_all | solution.py:327
  8.7 1.6 %pad_maximum_fusion = bf16[4,2048,128]{2,1,0:T(8,128)(2,1)} fusion(bf16[1,2048,128]{2,1,0:T(8,128)(2,1)S(1)} %bitcast.35, bf16[1,2048,128]{2,1,0:T(8,128)(2,1)S(1)} %bitcast.36, bf16[1,2048,128]{2,1,0:T(8,128)(2,1)S(1)} %bitcast.34, bf16[1,2048,128]{2,1,0:T(8,128)(2,1)S(1)} %bitcast.33), kind=kLoop, calls=%fused_computation | loop fusion | flops 3145728 | bytes 4194304 | tf_op jit(solution)/shard_map/stack | solution.py:329
  10.3 5.2 %all-to-all-done.got_ref = bf16[4,272,128]{2,1,0:T(8,128)(2,1)S(1)} async-done(((bf16[4,272,128]{2,1,0:T(8,128)(2,1)}), bf16[4,272,128]{2,1,0:T(8,128)(2,1)S(1)}, u32[]{:S(2)}, u32[]{:S(2)}) %all-to-all-start) | async-done | bytes 278560 | tf_op jit(solution)/shard_map/all_to_all | solution.py:327
  15.5 3.6 %all-to-all-start.1 = ((bf16[4,2048,128]{2,1,0:T(8,128)(2,1)}), bf16[4,2048,128]{2,1,0:T(8,128)(2,1)S(1)}, u32[]{:S(2)}, u32[]{:S(2)}) async-start(bf16[4,2048,128]{2,1,0:T(8,128)(2,1)} %pad_maximum_fusion), calls=%async_computation.1 | async-start | bytes 4194304 | tf_op jit(solution)/shard_map/all_to_all | solution.py:327
  19.3 1.6 %collective-permute-start.1 = (bf16[4,208,128]{2,1,0:T(8,128)(2,1)S(1)}, bf16[4,208,128]{2,1,0:T(8,128)(2,1)S(1)}, u32[]{:S(2)}, u32[]{:S(2)}) collective-permute-start(bf16[4,208,128]{2,1,0:T(8,128)(2,1)S(1)} %get-tuple-element.22.refs_0_), channel_id=1, source_target_pairs={{0,4},{1,5},{2,6},{3,7},{4,8},{5,9},{6,10},{7,11},{8,12},{9,13},{1... | collective-permute-start | bytes 638984 | tf_op jit(solution)/shard_map/ppermute | solution.py:314
  20.9 2.9 %collective-permute-start.2 = (bf16[4,208,128]{2,1,0:T(8,128)(2,1)S(1)}, bf16[4,208,128]{2,1,0:T(8,128)(2,1)S(1)}, u32[]{:S(2)}, u32[]{:S(2)}) collective-permute-start(bf16[4,208,128]{2,1,0:T(8,128)(2,1)S(1)} %get-tuple-element.22.refs_0_), channel_id=1, source_target_pairs={{0,8},{1,9},{2,10},{3,11},{4,12},{5,13},{6,14},{7,15},{8,0},{9,1},... | collective-permute-start | bytes 638984 | tf_op jit(solution)/shard_map/ppermute | solution.py:314
  23.8 1.3 %collective-permute-start.3 = (bf16[4,208,128]{2,1,0:T(8,128)(2,1)S(1)}, bf16[4,208,128]{2,1,0:T(8,128)(2,1)S(1)}, u32[]{:S(2)}, u32[]{:S(2)}) collective-permute-start(bf16[4,208,128]{2,1,0:T(8,128)(2,1)S(1)} %get-tuple-element.22.refs_0_), channel_id=1, source_target_pairs={{0,12},{1,13},{2,14},{3,15},{4,0},{5,1},{6,2},{7,3},{8,4},{9,5},{1... | collective-permute-start | bytes 638984 | tf_op jit(solution)/shard_map/ppermute | solution.py:314
  25.2 1.9 %collective-permute-start.4 = (bf16[2,128,128]{2,1,0:T(8,128)(2,1)S(1)}, bf16[2,128,128]{2,1,0:T(8,128)(2,1)S(1)}, u32[]{:S(2)}, u32[]{:S(2)}) collective-permute-start(bf16[2,128,128]{2,1,0:T(8,128)(2,1)S(1)} %get-tuple-element.24.refs_5_), channel_id=1, source_target_pairs={{0,32},{1,33},{2,34},{3,35},{4,36},{5,37},{6,38},{7,39},{8,40},{9,... | collective-permute-start | bytes 196616 | tf_op jit(solution)/shard_map/ppermute | solution.py:354
  27.1 0.1 select_reduce_fusion.owner_ref
  27.2 3.7 %collective-permute-start.5 = (bf16[2,128,128]{2,1,0:T(8,128)(2,1)S(1)}, bf16[2,128,128]{2,1,0:T(8,128)(2,1)S(1)}, u32[]{:S(2)}, u32[]{:S(2)}) collective-permute-start(bf16[2,128,128]{2,1,0:T(8,128)(2,1)S(1)} %get-tuple-element.24.refs_5_), channel_id=1, source_target_pairs={{0,64},{1,65},{2,66},{3,67},{4,68},{5,69},{6,70},{7,71},{8,72},{9,... | collective-permute-start | bytes 196616 | tf_op jit(solution)/shard_map/ppermute | solution.py:354
  30.9 0.7 collective-permute-done.4.refs_6_
  31.5 1.9 %collective-permute-start.6 = (bf16[2,128,128]{2,1,0:T(8,128)(2,1)S(1)}, bf16[2,128,128]{2,1,0:T(8,128)(2,1)S(1)}, u32[]{:S(2)}, u32[]{:S(2)}) collective-permute-start(bf16[2,128,128]{2,1,0:T(8,128)(2,1)S(1)} %get-tuple-element.24.refs_5_), channel_id=1, source_target_pairs={{0,96},{1,97},{2,98},{3,99},{4,100},{5,101},{6,102},{7,103},{8,104... | collective-permute-start | bytes 196616 | tf_op jit(solution)/shard_map/ppermute | solution.py:354
  33.5 0.1 collective-permute-done.5.refs_7_
  33.6 2.2 %collective-permute-done.6.refs_8_ = bf16[2,128,128]{2,1,0:T(8,128)(2,1)S(1)} collective-permute-done((bf16[2,128,128]{2,1,0:T(8,128)(2,1)S(1)}, bf16[2,128,128]{2,1,0:T(8,128)(2,1)S(1)}, u32[]{:S(2)}, u32[]{:S(2)}) %collective-permute-start.6) | collective-permute-done | bytes 65568 | tf_op jit(solution)/shard_map/ppermute | solution.py:354
  35.8 3.3 %all-to-all-done.1.refs_4_ = bf16[4,2048,128]{2,1,0:T(8,128)(2,1)S(1)} async-done(((bf16[4,2048,128]{2,1,0:T(8,128)(2,1)}), bf16[4,2048,128]{2,1,0:T(8,128)(2,1)S(1)}, u32[]{:S(2)}, u32[]{:S(2)}) %all-to-all-start.1) | async-done | bytes 2097184 | tf_op jit(solution)/shard_map/all_to_all | solution.py:327
  39.1 12.3 %attend.1 = (bf16[4,208,128]{2,1,0:T(8,128)(2,1)S(1)}, bf16[4,208,128]{2,1,0:T(8,128)(2,1)S(1)}, bf16[4,208,128]{2,1,0:T(8,128)(2,1)S(1)}, bf16[4,208,128]{2,1,0:T(8,128)(2,1)S(1)}) custom-call(s32[8]{0:T(128)S(1)} %stack.41.meta_ref, s32[128]{0:T(128)S(1)} %select_reduce_fusion.owner_ref, bf16[4,208,128]{2,1,0:T(8,128)(2,1)S(1)} %get-tuple-element.22.refs_0_, ...), custom_call_target="tpu_custom_call" | custom-call | flops 8589934592 | bytes 4194304 | tf_op jit(solution)/shard_map/attend/pallas_call | solution.py:359
  51.5 2.9 %collective-permute-start.7 = (bf16[4,208,128]{2,1,0:T(8,128)(2,1)S(1)}, bf16[4,208,128]{2,1,0:T(8,128)(2,1)S(1)}, u32[]{:S(2)}, u32[]{:S(2)}) collective-permute-start(bf16[4,208,128]{2,1,0:T(8,128)(2,1)S(1)} %get-tuple-element.27), channel_id=1, source_target_pairs={{0,12},{1,13},{2,14},{3,15},{4,0},{5,1},{6,2},{7,3},{8,4},{9,5},{1... | collective-permute-start | bytes 638984 | tf_op jit(solution)/shard_map/ppermute | solution.py:314
  54.4 0.8 %collective-permute-start.8 = (bf16[4,208,128]{2,1,0:T(8,128)(2,1)S(1)}, bf16[4,208,128]{2,1,0:T(8,128)(2,1)S(1)}, u32[]{:S(2)}, u32[]{:S(2)}) collective-permute-start(bf16[4,208,128]{2,1,0:T(8,128)(2,1)S(1)} %get-tuple-element.28), channel_id=1, source_target_pairs={{0,8},{1,9},{2,10},{3,11},{4,12},{5,13},{6,14},{7,15},{8,0},{9,1},... | collective-permute-start | bytes 638984 | tf_op jit(solution)/shard_map/ppermute | solution.py:314
  55.2 0.9 %collective-permute-start.9 = (bf16[4,208,128]{2,1,0:T(8,128)(2,1)S(1)}, bf16[4,208,128]{2,1,0:T(8,128)(2,1)S(1)}, u32[]{:S(2)}, u32[]{:S(2)}) collective-permute-start(bf16[4,208,128]{2,1,0:T(8,128)(2,1)S(1)} %get-tuple-element.29), channel_id=1, source_target_pairs={{0,4},{1,5},{2,6},{3,7},{4,8},{5,9},{6,10},{7,11},{8,12},{9,13},{1... | collective-permute-start | bytes 638984 | tf_op jit(solution)/shard_map/ppermute | solution.py:314
  56.1 1.5 %fusion.1 = (bf16[4,256,2,128]{3,2,1,0:T(2,128)(2,1)S(1)}, bf16[4,256,2,128]{3,2,1,0:T(2,128)(2,1)S(1)}, bf16[4,256,2,128]{3,2,1,0:T(2,128)(2,1)S(1)}, bf16[4,256,2,128]{3,2,1,0:T(2,128)(2,1)S(1)}) fusion(bf16[4,256,2,512]{3,2,1,0:T(2,128)(2,1)S(1)} %copy-done.6), kind=kLoop, calls=%fused_computation.6 | loop fusion | bytes 4194304 | tf_op jit(solution)/shard_map/slice | solution.py:324
  57.6 2.5 %collective-permute-done.7.c1 = bf16[4,208,128]{2,1,0:T(8,128)(2,1)S(1)} collective-permute-done((bf16[4,208,128]{2,1,0:T(8,128)(2,1)S(1)}, bf16[4,208,128]{2,1,0:T(8,128)(2,1)S(1)}, u32[]{:S(2)}, u32[]{:S(2)}) %collective-permute-start.7) | collective-permute-done | bytes 213024 | tf_op jit(solution)/shard_map/ppermute | solution.py:314
  60.1 1.8 %collective-permute-done.8.c2 = bf16[4,208,128]{2,1,0:T(8,128)(2,1)S(1)} collective-permute-done((bf16[4,208,128]{2,1,0:T(8,128)(2,1)S(1)}, bf16[4,208,128]{2,1,0:T(8,128)(2,1)S(1)}, u32[]{:S(2)}, u32[]{:S(2)}) %collective-permute-start.8) | collective-permute-done | bytes 213024 | tf_op jit(solution)/shard_map/ppermute | solution.py:314
  61.8 2.2 %collective-permute-done.9.c3 = bf16[4,208,128]{2,1,0:T(8,128)(2,1)S(1)} collective-permute-done((bf16[4,208,128]{2,1,0:T(8,128)(2,1)S(1)}, bf16[4,208,128]{2,1,0:T(8,128)(2,1)S(1)}, u32[]{:S(2)}, u32[]{:S(2)}) %collective-permute-start.9) | collective-permute-done | bytes 213024 | tf_op jit(solution)/shard_map/ppermute | solution.py:314
  64.0 1.2 %combine.1 = (bf16[208,128]{1,0:T(8,128)(2,1)S(1)}, bf16[208,128]{1,0:T(8,128)(2,1)S(1)}, bf16[208,128]{1,0:T(8,128)(2,1)S(1)}, bf16[208,128]{1,0:T(8,128)(2,1)S(1)}) custom-call(s32[8]{0:T(128)S(1)} %stack.41.meta_ref, bf16[4,208,128]{2,1,0:T(8,128)(2,1)S(1)} %get-tuple-element.26.c0, bf16[4,208,128]{2,1,0:T(8,128)(2,1)S(1)} %collective-permute-done.7.c1, ...), custom_call_target="tpu_custom_call" | custom-call | bytes 1048576 | tf_op jit(solution)/shard_map/combine/pallas_call | solution.py:398
  65.3 2.3 %collective-permute-start.10 = (bf16[208,128]{1,0:T(8,128)(2,1)S(1)}, bf16[208,128]{1,0:T(8,128)(2,1)S(1)}, u32[]{:S(2)}, u32[]{:S(2)}) collective-permute-start(bf16[208,128]{1,0:T(8,128)(2,1)S(1)} %get-tuple-element.31), channel_id=1, source_target_pairs={{0,3},{1,0},{2,1},{3,2},{4,7},{5,4},{6,5},{7,6},{8,11},{9,8},{10,9... | collective-permute-start | bytes 159752 | tf_op jit(solution)/shard_map/ppermute | solution.py:314
  67.6 1.5 %collective-permute-start.11 = (bf16[208,128]{1,0:T(8,128)(2,1)S(1)}, bf16[208,128]{1,0:T(8,128)(2,1)S(1)}, u32[]{:S(2)}, u32[]{:S(2)}) collective-permute-start(bf16[208,128]{1,0:T(8,128)(2,1)S(1)} %get-tuple-element.32), channel_id=1, source_target_pairs={{0,2},{1,3},{2,0},{3,1},{4,6},{5,7},{6,4},{7,5},{8,10},{9,11},{10,... | collective-permute-start | bytes 159752 | tf_op jit(solution)/shard_map/ppermute | solution.py:314
  69.1 3.2 %own_tokens.1 = (f32[4,192,128]{2,1,0:T(8,128)S(1)}, f32[4,8,128]{2,1,0:T(8,128)S(1)}) custom-call(s32[4]{0:T(128)S(1)} %copy-done.5, bf16[4,272,128]{2,1,0:T(8,128)(2,1)} %query_messages.1.q_ref, bf16[2048,128]{1,0:T(8,128)(2,1)S(1)} %bitcast.29, bf16[2048,128]{1,0:T(8,128)(2,1)S(1)} %bitcast.28, bf16[2048,128]{1,0:T(8,128)(2,1)S(1)} %bitcast.30, ...), custom_call_target="tpu_custom_call" | custom-call | flops 1073741824 | bytes 4194304 | tf_op jit(solution)/shard_map/own_tokens/pallas_call | solution.py:384
  72.3 1.0 %collective-permute-done.11.r2 = bf16[208,128]{1,0:T(8,128)(2,1)S(1)} collective-permute-done((bf16[208,128]{1,0:T(8,128)(2,1)S(1)}, bf16[208,128]{1,0:T(8,128)(2,1)S(1)}, u32[]{:S(2)}, u32[]{:S(2)}) %collective-permute-start.11) | collective-permute-done | bytes 53280 | tf_op jit(solution)/shard_map/ppermute | solution.py:314
  73.2 1.2 %collective-permute-done.12.r3 = bf16[208,128]{1,0:T(8,128)(2,1)S(1)} collective-permute-done((bf16[208,128]{1,0:T(8,128)(2,1)S(1)}, bf16[208,128]{1,0:T(8,128)(2,1)S(1)}, u32[]{:S(2)}, u32[]{:S(2)}) %collective-permute-start.12) | collective-permute-done | bytes 53280 | tf_op jit(solution)/shard_map/ppermute | solution.py:314
  74.4 1.7 %final.1 = bf16[3,4,64,128]{3,2,1,0:T(8,128)(2,1)} custom-call(s32[8]{0:T(128)S(1)} %stack.41.meta_ref, bf16[208,128]{1,0:T(8,128)(2,1)S(1)} %get-tuple-element.30.r0, bf16[208,128]{1,0:T(8,128)(2,1)S(1)} %collective-permute-done.10.r1, bf16[208,128]{1,0:T(8,128)(2,1)S(1)} %collective-permute-done.11.r2, bf16[208,128]{1,0:T(8,128)(2,1)S(1)} %collective-permute-done.12.r3, ...), custom_call_target="tpu_custom_call" | custom-call | tf_op jit(solution)/shard_map/final/pallas_call | solution.py:408
  (28 shorter events, 0.3 us)
Async XLA Ops:
  0.0 2.8 %copy-start.1 = (bf16[16,2,512]{2,1,0:T(2,128)(2,1)S(1)}, bf16[16,2,512]{2,1,0:T(2,128)(2,1)}, u32[]{:S(2)}) copy-start(bf16[16,2,512]{2,1,0:T(2,128)(2,1)} %sys_ref.1) | copy-start | bytes 98308
  0.0 2.9 %copy-start.4 = (s32[1,128]{1,0:T(1,128)S(1)}, s32[1,128]{1,0:T(1,128)}, u32[]{:S(2)}) copy-start(s32[1,128]{1,0:T(1,128)} %slot_ref.1) | copy-start | bytes 1540
  0.0 2.9 %copy-start.2 = (s32[4,64]{1,0:T(4,128)S(1)}, s32[4,64]{1,0:T(4,128)}, u32[]{:S(2)}) copy-start(s32[4,64]{1,0:T(4,128)} %list_ref.1) | copy-start | bytes 3076
  0.0 2.9 %copy-start.3 = (s32[4]{0:T(128)S(1)}, s32[4]{0:T(128)}, u32[]{:S(2)}) copy-start(s32[4]{0:T(128)} %used_ref.1) | copy-start | bytes 52
  0.0 2.9 %copy-start = (bf16[4,3,8192]{2,0,1:T(4,128)(2,1)S(1)}, bf16[4,3,8192]{2,0,1:T(4,128)(2,1)}, u32[]{:S(2)}) copy-start(bf16[4,3,8192]{2,0,1:T(4,128)(2,1)} %param.9) | copy-start | bytes 589828
  0.0 2.8 %collective-permute-start = (bf16[16,2,512]{2,1,0:T(2,128)(2,1)}, bf16[16,2,512]{2,1,0:T(2,128)(2,1)S(1)}, u32[]{:S(2)}, u32[]{:S(2)}) collective-permute-start(bf16[16,2,512]{2,1,0:T(2,128)(2,1)} %sys_ref.1), channel_id=1, source_target_pairs={{0,16},{1,17},{2,18},{3,19},{4,20},{5,21},{6,22},{7,23},{8,24},{9,... | collective-permute-start | bytes 98312 | tf_op jit(solution)/shard_map/ppermute | solution.py:321
  4.3 11.1 %all-to-all-start = ((bf16[4,272,128]{2,1,0:T(8,128)(2,1)}), bf16[4,272,128]{2,1,0:T(8,128)(2,1)S(1)}, u32[]{:S(2)}, u32[]{:S(2)}) async-start(bf16[4,272,128]{2,1,0:T(8,128)(2,1)} %query_messages.1.q_ref), calls=%async_computation | async-start | bytes 557056 | tf_op jit(solution)/shard_map/all_to_all | solution.py:327
  10.3 8.9 %copy-start.7 = (bf16[4,3,2,512]{3,2,1,0:T(2,128)(2,1)S(1)}, bf16[4,3,2,512]{3,2,1,0:T(2,128)(2,1)}, u32[]{:S(2)}) copy-start(bf16[4,3,2,512]{3,2,1,0:T(2,128)(2,1)} %param.10) | copy-start | bytes 73732
  15.5 23.7 %all-to-all-start.1 = ((bf16[4,2048,128]{2,1,0:T(8,128)(2,1)}), bf16[4,2048,128]{2,1,0:T(8,128)(2,1)S(1)}, u32[]{:S(2)}, u32[]{:S(2)}) async-start(bf16[4,2048,128]{2,1,0:T(8,128)(2,1)} %pad_maximum_fusion), calls=%async_computation.1 | async-start | bytes 4194304 | tf_op jit(solution)/shard_map/all_to_all | solution.py:327
  19.3 16.5 %collective-permute-start.1 = (bf16[4,208,128]{2,1,0:T(8,128)(2,1)S(1)}, bf16[4,208,128]{2,1,0:T(8,128)(2,1)S(1)}, u32[]{:S(2)}, u32[]{:S(2)}) collective-permute-start(bf16[4,208,128]{2,1,0:T(8,128)(2,1)S(1)} %get-tuple-element.22.refs_0_), channel_id=1, source_target_pairs={{0,4},{1,5},{2,6},{3,7},{4,8},{5,9},{6,10},{7,11},{8,12},{9,13},{1... | collective-permute-start | bytes 638984 | tf_op jit(solution)/shard_map/ppermute | solution.py:314
  20.9 14.9 %collective-permute-start.2 = (bf16[4,208,128]{2,1,0:T(8,128)(2,1)S(1)}, bf16[4,208,128]{2,1,0:T(8,128)(2,1)S(1)}, u32[]{:S(2)}, u32[]{:S(2)}) collective-permute-start(bf16[4,208,128]{2,1,0:T(8,128)(2,1)S(1)} %get-tuple-element.22.refs_0_), channel_id=1, source_target_pairs={{0,8},{1,9},{2,10},{3,11},{4,12},{5,13},{6,14},{7,15},{8,0},{9,1},... | collective-permute-start | bytes 638984 | tf_op jit(solution)/shard_map/ppermute | solution.py:314
  23.8 12.0 %collective-permute-start.3 = (bf16[4,208,128]{2,1,0:T(8,128)(2,1)S(1)}, bf16[4,208,128]{2,1,0:T(8,128)(2,1)S(1)}, u32[]{:S(2)}, u32[]{:S(2)}) collective-permute-start(bf16[4,208,128]{2,1,0:T(8,128)(2,1)S(1)} %get-tuple-element.22.refs_0_), channel_id=1, source_target_pairs={{0,12},{1,13},{2,14},{3,15},{4,0},{5,1},{6,2},{7,3},{8,4},{9,5},{1... | collective-permute-start | bytes 638984 | tf_op jit(solution)/shard_map/ppermute | solution.py:314
  25.2 6.4 %collective-permute-start.4 = (bf16[2,128,128]{2,1,0:T(8,128)(2,1)S(1)}, bf16[2,128,128]{2,1,0:T(8,128)(2,1)S(1)}, u32[]{:S(2)}, u32[]{:S(2)}) collective-permute-start(bf16[2,128,128]{2,1,0:T(8,128)(2,1)S(1)} %get-tuple-element.24.refs_5_), channel_id=1, source_target_pairs={{0,32},{1,33},{2,34},{3,35},{4,36},{5,37},{6,38},{7,39},{8,40},{9,... | collective-permute-start | bytes 196616 | tf_op jit(solution)/shard_map/ppermute | solution.py:354
  27.2 6.4 %collective-permute-start.5 = (bf16[2,128,128]{2,1,0:T(8,128)(2,1)S(1)}, bf16[2,128,128]{2,1,0:T(8,128)(2,1)S(1)}, u32[]{:S(2)}, u32[]{:S(2)}) collective-permute-start(bf16[2,128,128]{2,1,0:T(8,128)(2,1)S(1)} %get-tuple-element.24.refs_5_), channel_id=1, source_target_pairs={{0,64},{1,65},{2,66},{3,67},{4,68},{5,69},{6,70},{7,71},{8,72},{9,... | collective-permute-start | bytes 196616 | tf_op jit(solution)/shard_map/ppermute | solution.py:354
  31.5 4.3 %collective-permute-start.6 = (bf16[2,128,128]{2,1,0:T(8,128)(2,1)S(1)}, bf16[2,128,128]{2,1,0:T(8,128)(2,1)S(1)}, u32[]{:S(2)}, u32[]{:S(2)}) collective-permute-start(bf16[2,128,128]{2,1,0:T(8,128)(2,1)S(1)} %get-tuple-element.24.refs_5_), channel_id=1, source_target_pairs={{0,96},{1,97},{2,98},{3,99},{4,100},{5,101},{6,102},{7,103},{8,104... | collective-permute-start | bytes 196616 | tf_op jit(solution)/shard_map/ppermute | solution.py:354
  39.1 17.0 %copy-start.6 = (bf16[4,256,2,512]{3,2,1,0:T(2,128)(2,1)S(1)}, bf16[4,256,2,512]{3,2,1,0:T(2,128)(2,1)}, u32[]{:S(2)}) copy-start(bf16[4,256,2,512]{3,2,1,0:T(2,128)(2,1)} %param.11) | copy-start | bytes 6291460
  51.5 8.6 %collective-permute-start.7 = (bf16[4,208,128]{2,1,0:T(8,128)(2,1)S(1)}, bf16[4,208,128]{2,1,0:T(8,128)(2,1)S(1)}, u32[]{:S(2)}, u32[]{:S(2)}) collective-permute-start(bf16[4,208,128]{2,1,0:T(8,128)(2,1)S(1)} %get-tuple-element.27), channel_id=1, source_target_pairs={{0,12},{1,13},{2,14},{3,15},{4,0},{5,1},{6,2},{7,3},{8,4},{9,5},{1... | collective-permute-start | bytes 638984 | tf_op jit(solution)/shard_map/ppermute | solution.py:314
  54.4 7.5 %collective-permute-start.8 = (bf16[4,208,128]{2,1,0:T(8,128)(2,1)S(1)}, bf16[4,208,128]{2,1,0:T(8,128)(2,1)S(1)}, u32[]{:S(2)}, u32[]{:S(2)}) collective-permute-start(bf16[4,208,128]{2,1,0:T(8,128)(2,1)S(1)} %get-tuple-element.28), channel_id=1, source_target_pairs={{0,8},{1,9},{2,10},{3,11},{4,12},{5,13},{6,14},{7,15},{8,0},{9,1},... | collective-permute-start | bytes 638984 | tf_op jit(solution)/shard_map/ppermute | solution.py:314
  55.2 13.8 %copy-start.5 = (s32[4]{0:T(128)S(1)}, s32[4]{0:T(128)}, u32[]{:S(2)}) copy-start(s32[4]{0:T(128)} %lens_ref) | copy-start | bytes 52
  55.2 8.8 %collective-permute-start.9 = (bf16[4,208,128]{2,1,0:T(8,128)(2,1)S(1)}, bf16[4,208,128]{2,1,0:T(8,128)(2,1)S(1)}, u32[]{:S(2)}, u32[]{:S(2)}) collective-permute-start(bf16[4,208,128]{2,1,0:T(8,128)(2,1)S(1)} %get-tuple-element.29), channel_id=1, source_target_pairs={{0,4},{1,5},{2,6},{3,7},{4,8},{5,9},{6,10},{7,11},{8,12},{9,13},{1... | collective-permute-start | bytes 638984 | tf_op jit(solution)/shard_map/ppermute | solution.py:314
  65.3 7.0 %collective-permute-start.10 = (bf16[208,128]{1,0:T(8,128)(2,1)S(1)}, bf16[208,128]{1,0:T(8,128)(2,1)S(1)}, u32[]{:S(2)}, u32[]{:S(2)}) collective-permute-start(bf16[208,128]{1,0:T(8,128)(2,1)S(1)} %get-tuple-element.31), channel_id=1, source_target_pairs={{0,3},{1,0},{2,1},{3,2},{4,7},{5,4},{6,5},{7,6},{8,11},{9,8},{10,9... | collective-permute-start | bytes 159752 | tf_op jit(solution)/shard_map/ppermute | solution.py:314
  67.6 5.6 %collective-permute-start.11 = (bf16[208,128]{1,0:T(8,128)(2,1)S(1)}, bf16[208,128]{1,0:T(8,128)(2,1)S(1)}, u32[]{:S(2)}, u32[]{:S(2)}) collective-permute-start(bf16[208,128]{1,0:T(8,128)(2,1)S(1)} %get-tuple-element.32), channel_id=1, source_target_pairs={{0,2},{1,3},{2,0},{3,1},{4,6},{5,7},{6,4},{7,5},{8,10},{9,11},{10,... | collective-permute-start | bytes 159752 | tf_op jit(solution)/shard_map/ppermute | solution.py:314
  69.1 5.3 %collective-permute-start.12 = (bf16[208,128]{1,0:T(8,128)(2,1)S(1)}, bf16[208,128]{1,0:T(8,128)(2,1)S(1)}, u32[]{:S(2)}, u32[]{:S(2)}) collective-permute-start(bf16[208,128]{1,0:T(8,128)(2,1)S(1)} %get-tuple-element.33), channel_id=1, source_target_pairs={{0,1},{1,2},{2,3},{3,0},{4,5},{5,6},{6,7},{7,4},{8,9},{9,10},{10,1... | collective-permute-start | bytes 159752 | tf_op jit(solution)/shard_map/ppermute | solution.py:314

commit v5 on v3

--- a/solution.py
+++ b/solution.py
@@ -102,6 +102,16 @@
         for side in range(2):
             at = pl.ds(k * SYS_PART, SYS_PART)
             sys_ref[side, at, :] = msg[pl.ds(MSG + side * SYS_PART, SYS_PART), :]
+
+
+def head_kernel(pool_ref, out_ref, sems):
+    copies = [
+        pltpu.make_async_copy(pool_ref.at[:, :, :, pl.ds(h * HD, HD)], out_ref.at[h], sems.at[h]) for h in range(KVH)
+    ]
+    for copy in copies:
+        copy.start()
+    for copy in copies:
+        copy.wait()
 
 
 def flatten_rows(lse):
@@ -322,7 +332,17 @@
     def one_head(array, k):
         return lax.dynamic_slice_in_dim(array, ((a + k) % SIDE) * HD, HD, array.ndim - 1).reshape(-1, HD)
 
-    by_head = jnp.stack([pool_kv[..., h * HD : (h + 1) * HD].reshape(-1, HD) for h in range(KVH)])
+    by_head = pl.pallas_call(
+        head_kernel,
+        in_specs=[pl.BlockSpec(memory_space=pltpu.HBM)],
+        out_specs=pl.BlockSpec(memory_space=pl.ANY),
+        out_shape=shaped((KVH, *pool_kv.shape[:3], HD)),
+        scratch_shapes=[pltpu.SemaphoreType.DMA((KVH,))],
+        compiler_params=room(4),
+        cost_estimate=cost(0, 2**22),
+        name="split_heads",
+    )(pool_kv).reshape(KVH, -1, HD)
+    by_head, far_sys = lax.optimization_barrier((by_head, far_sys))
 
     q_msgs = pl.pallas_call(
         query_kernel,

time: 74 us -> 73.4 us (level)
  waiting for transfers between devices: 15.1 us -> 17.2 us
  other arithmetic: 1.74 us -> 0.13 us
  local copies, waits for them, and re-layouts: 5.49 us -> 3.92 us
    slice x1 -> x0, local copies, waits for them, and re-layouts: 2.72 us -> none  [body(): pool_kv[..., h * HD:(h + 1) * HD].reshape(-1, HD)]
    ppermute x12, waiting for transfers between devices: 9.78 us -> 11.8 us  [send(): return lax.ppermute(array, AXES, ring_pairs(prompts, role, step % SIDE))]
    another operation x1 -> x0, other arithmetic: 1.61 us -> none  [body(): jnp.stack([pool_kv[..., h * HD:(h + 1) * HD].reshape(-1, HD) for h in ran...]
    unnamed x14 -> x16, local copies, waits for them, and re-layouts: 0.03 us -> 1.62 us
    pallas_call x0 -> x1, Pallas kernels: none -> 1.39 us  [body(): pl.pallas_call(head_kernel, in_specs=[pl.BlockSpec(memory_space=pltpu.HBM...]
  transfers between devices with their start and end apart: 17 -> 17, of which waited for: 9 -> 10; matrix products, arithmetic and copies ran while one was open for 10% -> 3% of each run, Pallas kernels for 5% -> 6%
where the time goes in v5:
time: 73.4 us; the launch traced here: 73.1 us
  starting transfers between devices  31.4 us (43%)
  Pallas kernels  20.2 us (28%)
  waiting for transfers between devices  17.2 us (23%)
  local copies, waits for them, and re-layouts  3.92 us (5%)
    ppermute x12, starting transfers between devices, send(): return lax.ppermute(array, AXES, ring_pairs(prompts, role, step % SIDE))  19.9 us
    ppermute x12, waiting for transfers between devices, send(): return lax.ppermute(array, AXES, ring_pairs(prompts, role, step % SIDE))  11.8 us
    pallas_call x1, Pallas kernels, body(): pl.pallas_call(main_kernel, grid_spec=pltpu.PrefetchScalarGridSpec(num_sc...  11.8 us
    ppermute x3, starting transfers between devices, body(): lax.ppermute(sys_one, AXES, plane_pairs(prompts, k))  7.6 us
    all_to_all x1, starting transfers between devices, body(): lax.all_to_all(by_head, AXES, 0, 0, axis_index_groups=ring_groups(prompts...  3.91 us
    all_to_all x1, waiting for transfers between devices, body(): lax.all_to_all(by_head, AXES, 0, 0, axis_index_groups=ring_groups(prompts...  3.34 us
    pallas_call x1, Pallas kernels, body(): pl.pallas_call(own_kernel, in_specs=[SMEM] + [VMEM] * 9, out_specs=[VMEM]...  2.8 us
    dynamic_slice x2, local copies, waits for them, and re-layouts, one_head(): lax.dynamic_slice_in_dim(array, (a + k) % SIDE * HD, HD, array.ndim - 1)  2.21 us
  transfers between devices with their start and end apart: 17, of which 10 were waited for; matrix products, arithmetic and copies ran while one was open for 3% of the time, Pallas kernels for 6%

profile of v5, /device:TPU:0, one launch (start us, length us, event | category | flops | bytes accessed | tf_op | source)
XLA Modules:
  0.0 73.1 jit_solution(13633801759357667374)
XLA Ops:
  0.0 1.6 %copy-done = bf16[8,128,2,512]{3,2,1,0:T(2,128)(2,1)S(1)} copy-done((bf16[8,128,2,512]{3,2,1,0:T(2,128)(2,1)S(1)}, bf16[8,128,2,512]{3,2,1,0:T(2,128)(2,1)}, u32[]{:S(2)}) %copy-start) | copy-done | bytes 2097176
  1.6 1.4 %split_heads.1 = bf16[4,8,128,2,128]{4,3,2,1,0:T(2,128)(2,1)} custom-call(bf16[8,128,2,512]{3,2,1,0:T(2,128)(2,1)S(1)} %copy-done), custom_call_target="tpu_custom_call" | custom-call | bytes 4194304 | tf_op jit(solution)/shard_map/split_heads/pallas_call | solution.py:335
  3.2 0.9 %query_messages.1 = (bf16[272,128]{1,0:T(8,128)(2,1)S(1)}, bf16[272,128]{1,0:T(8,128)(2,1)S(1)}, bf16[272,128]{1,0:T(8,128)(2,1)S(1)}, bf16[272,128]{1,0:T(8,128)(2,1)S(1)}) custom-call(s32[8]{0:T(128)S(1)} %stack.38.meta_ref, s32[1,128]{1,0:T(1,128)S(1)} %copy-done.5, s32[4,64]{1,0:T(4,128)S(1)} %copy-done.3, s32[4]{0:T(128)S(1)} %copy-done.4, ...), custom_call_target="tpu_custom_call" | custom-call | bytes 524288 | tf_op jit(solution)/shard_map/query_messages/pallas_call | solution.py:347
  4.0 1.6 %collective-permute-start.1 = (bf16[272,128]{1,0:T(8,128)(2,1)S(1)}, bf16[272,128]{1,0:T(8,128)(2,1)S(1)}, u32[]{:S(2)}, u32[]{:S(2)}) collective-permute-start(bf16[272,128]{1,0:T(8,128)(2,1)S(1)} %get-tuple-element.33.q1), channel_id=1, source_target_pairs={{0,1},{1,2},{2,3},{3,0},{4,5},{5,6},{6,7},{7,4},{8,9},{9,10},{10,1... | collective-permute-start | bytes 208904 | tf_op jit(solution)/shard_map/ppermute | solution.py:323
  5.7 2.7 %collective-permute-start.2 = (bf16[272,128]{1,0:T(8,128)(2,1)S(1)}, bf16[272,128]{1,0:T(8,128)(2,1)S(1)}, u32[]{:S(2)}, u32[]{:S(2)}) collective-permute-start(bf16[272,128]{1,0:T(8,128)(2,1)S(1)} %get-tuple-element.34.q2), channel_id=1, source_target_pairs={{0,2},{1,3},{2,0},{3,1},{4,6},{5,7},{6,4},{7,5},{8,10},{9,11},{10,... | collective-permute-start | bytes 208904 | tf_op jit(solution)/shard_map/ppermute | solution.py:323
  8.4 1.4 %collective-permute-start.3 = (bf16[272,128]{1,0:T(8,128)(2,1)S(1)}, bf16[272,128]{1,0:T(8,128)(2,1)S(1)}, u32[]{:S(2)}, u32[]{:S(2)}) collective-permute-start(bf16[272,128]{1,0:T(8,128)(2,1)S(1)} %get-tuple-element.35.q3), channel_id=1, source_target_pairs={{0,3},{1,0},{2,1},{3,2},{4,7},{5,4},{6,5},{7,6},{8,11},{9,8},{10,9... | collective-permute-start | bytes 208904 | tf_op jit(solution)/shard_map/ppermute | solution.py:323
  9.8 1.6 %collective-permute-done.2.m2 = bf16[272,128]{1,0:T(8,128)(2,1)S(1)} collective-permute-done((bf16[272,128]{1,0:T(8,128)(2,1)S(1)}, bf16[272,128]{1,0:T(8,128)(2,1)S(1)}, u32[]{:S(2)}, u32[]{:S(2)}) %collective-permute-start.2) | collective-permute-done | bytes 69664 | tf_op jit(solution)/shard_map/ppermute | solution.py:323
  11.5 1.2 %collective-permute-done.3.m3 = bf16[272,128]{1,0:T(8,128)(2,1)S(1)} collective-permute-done((bf16[272,128]{1,0:T(8,128)(2,1)S(1)}, bf16[272,128]{1,0:T(8,128)(2,1)S(1)}, u32[]{:S(2)}, u32[]{:S(2)}) %collective-permute-start.3) | collective-permute-done | bytes 69664 | tf_op jit(solution)/shard_map/ppermute | solution.py:323
  12.7 3.9 %all-to-all-start = ((bf16[4,2048,128]{2,1,0:T(8,128)(2,1)}), bf16[4,2048,128]{2,1,0:T(8,128)(2,1)S(1)}, u32[]{:S(2)}, u32[]{:S(2)}) async-start(bf16[4,2048,128]{2,1,0:T(8,128)(2,1)} %bitcast.9), calls=%async_computation | async-start | bytes 4194304 | tf_op jit(solution)/shard_map/all_to_all | solution.py:359
  17.2 1.6 %collective-permute-start.4 = (bf16[4,208,128]{2,1,0:T(8,128)(2,1)S(1)}, bf16[4,208,128]{2,1,0:T(8,128)(2,1)S(1)}, u32[]{:S(2)}, u32[]{:S(2)}) collective-permute-start(bf16[4,208,128]{2,1,0:T(8,128)(2,1)S(1)} %get-tuple-element.40.refs_0_), channel_id=1, source_target_pairs={{0,4},{1,5},{2,6},{3,7},{4,8},{5,9},{6,10},{7,11},{8,12},{9,13},{1... | collective-permute-start | bytes 638984 | tf_op jit(solution)/shard_map/ppermute | solution.py:323
  18.8 2.9 %collective-permute-start.5 = (bf16[4,208,128]{2,1,0:T(8,128)(2,1)S(1)}, bf16[4,208,128]{2,1,0:T(8,128)(2,1)S(1)}, u32[]{:S(2)}, u32[]{:S(2)}) collective-permute-start(bf16[4,208,128]{2,1,0:T(8,128)(2,1)S(1)} %get-tuple-element.40.refs_0_), channel_id=1, source_target_pairs={{0,8},{1,9},{2,10},{3,11},{4,12},{5,13},{6,14},{7,15},{8,0},{9,1},... | collective-permute-start | bytes 638984 | tf_op jit(solution)/shard_map/ppermute | solution.py:323
  21.7 1.3 %collective-permute-start.6 = (bf16[4,208,128]{2,1,0:T(8,128)(2,1)S(1)}, bf16[4,208,128]{2,1,0:T(8,128)(2,1)S(1)}, u32[]{:S(2)}, u32[]{:S(2)}) collective-permute-start(bf16[4,208,128]{2,1,0:T(8,128)(2,1)S(1)} %get-tuple-element.40.refs_0_), channel_id=1, source_target_pairs={{0,12},{1,13},{2,14},{3,15},{4,0},{5,1},{6,2},{7,3},{8,4},{9,5},{1... | collective-permute-start | bytes 638984 | tf_op jit(solution)/shard_map/ppermute | solution.py:323
  23.1 1.9 %collective-permute-start.7 = (bf16[2,128,128]{2,1,0:T(8,128)(2,1)S(1)}, bf16[2,128,128]{2,1,0:T(8,128)(2,1)S(1)}, u32[]{:S(2)}, u32[]{:S(2)}) collective-permute-start(bf16[2,128,128]{2,1,0:T(8,128)(2,1)S(1)} %get-tuple-element.42.refs_5_), channel_id=1, source_target_pairs={{0,32},{1,33},{2,34},{3,35},{4,36},{5,37},{6,38},{7,39},{8,40},{9,... | collective-permute-start | bytes 196616 | tf_op jit(solution)/shard_map/ppermute | solution.py:370
  25.1 3.7 %collective-permute-start.8 = (bf16[2,128,128]{2,1,0:T(8,128)(2,1)S(1)}, bf16[2,128,128]{2,1,0:T(8,128)(2,1)S(1)}, u32[]{:S(2)}, u32[]{:S(2)}) collective-permute-start(bf16[2,128,128]{2,1,0:T(8,128)(2,1)S(1)} %get-tuple-element.42.refs_5_), channel_id=1, source_target_pairs={{0,64},{1,65},{2,66},{3,67},{4,68},{5,69},{6,70},{7,71},{8,72},{9,... | collective-permute-start | bytes 196616 | tf_op jit(solution)/shard_map/ppermute | solution.py:370
  29.4 2.0 %collective-permute-start.9 = (bf16[2,128,128]{2,1,0:T(8,128)(2,1)S(1)}, bf16[2,128,128]{2,1,0:T(8,128)(2,1)S(1)}, u32[]{:S(2)}, u32[]{:S(2)}) collective-permute-start(bf16[2,128,128]{2,1,0:T(8,128)(2,1)S(1)} %get-tuple-element.42.refs_5_), channel_id=1, source_target_pairs={{0,96},{1,97},{2,98},{3,99},{4,100},{5,101},{6,102},{7,103},{8,104... | collective-permute-start | bytes 196616 | tf_op jit(solution)/shard_map/ppermute | solution.py:370
  32.2 1.5 %collective-permute-done.9.refs_8_ = bf16[2,128,128]{2,1,0:T(8,128)(2,1)S(1)} collective-permute-done((bf16[2,128,128]{2,1,0:T(8,128)(2,1)S(1)}, bf16[2,128,128]{2,1,0:T(8,128)(2,1)S(1)}, u32[]{:S(2)}, u32[]{:S(2)}) %collective-permute-start.9) | collective-permute-done | bytes 65568 | tf_op jit(solution)/shard_map/ppermute | solution.py:370
  33.6 3.3 %all-to-all-done.refs_4_ = bf16[4,2048,128]{2,1,0:T(8,128)(2,1)S(1)} async-done(((bf16[4,2048,128]{2,1,0:T(8,128)(2,1)}), bf16[4,2048,128]{2,1,0:T(8,128)(2,1)S(1)}, u32[]{:S(2)}, u32[]{:S(2)}) %all-to-all-start) | async-done | bytes 2097184 | tf_op jit(solution)/shard_map/all_to_all | solution.py:359
  37.0 11.8 %attend.1 = (bf16[4,208,128]{2,1,0:T(8,128)(2,1)S(1)}, bf16[4,208,128]{2,1,0:T(8,128)(2,1)S(1)}, bf16[4,208,128]{2,1,0:T(8,128)(2,1)S(1)}, bf16[4,208,128]{2,1,0:T(8,128)(2,1)S(1)}) custom-call(s32[8]{0:T(128)S(1)} %stack.38.meta_ref, s32[128]{0:T(128)S(1)} %select_reduce_fusion.owner_ref, bf16[4,208,128]{2,1,0:T(8,128)(2,1)S(1)} %get-tuple-element.40.refs_0_, ...), custom_call_target="tpu_custom_call" | custom-call | flops 8589934592 | bytes 4194304 | tf_op jit(solution)/shard_map/attend/pallas_call | solution.py:375
  48.8 2.9 %collective-permute-start.10 = (bf16[4,208,128]{2,1,0:T(8,128)(2,1)S(1)}, bf16[4,208,128]{2,1,0:T(8,128)(2,1)S(1)}, u32[]{:S(2)}, u32[]{:S(2)}) collective-permute-start(bf16[4,208,128]{2,1,0:T(8,128)(2,1)S(1)} %get-tuple-element.45), channel_id=1, source_target_pairs={{0,12},{1,13},{2,14},{3,15},{4,0},{5,1},{6,2},{7,3},{8,4},{9,5},{1... | collective-permute-start | bytes 638984 | tf_op jit(solution)/shard_map/ppermute | solution.py:323
  51.7 0.9 %collective-permute-start.11 = (bf16[4,208,128]{2,1,0:T(8,128)(2,1)S(1)}, bf16[4,208,128]{2,1,0:T(8,128)(2,1)S(1)}, u32[]{:S(2)}, u32[]{:S(2)}) collective-permute-start(bf16[4,208,128]{2,1,0:T(8,128)(2,1)S(1)} %get-tuple-element.46), channel_id=1, source_target_pairs={{0,8},{1,9},{2,10},{3,11},{4,12},{5,13},{6,14},{7,15},{8,0},{9,1},... | collective-permute-start | bytes 638984 | tf_op jit(solution)/shard_map/ppermute | solution.py:323
  52.5 0.9 %collective-permute-start.12 = (bf16[4,208,128]{2,1,0:T(8,128)(2,1)S(1)}, bf16[4,208,128]{2,1,0:T(8,128)(2,1)S(1)}, u32[]{:S(2)}, u32[]{:S(2)}) collective-permute-start(bf16[4,208,128]{2,1,0:T(8,128)(2,1)S(1)} %get-tuple-element.47), channel_id=1, source_target_pairs={{0,4},{1,5},{2,6},{3,7},{4,8},{5,9},{6,10},{7,11},{8,12},{9,13},{1... | collective-permute-start | bytes 638984 | tf_op jit(solution)/shard_map/ppermute | solution.py:323
  53.4 1.5 %constant_dynamic-slice_fusion.3 = (bf16[4,256,2,128]{3,2,1,0:T(2,128)(2,1)S(1)}, bf16[4,256,2,128]{3,2,1,0:T(2,128)(2,1)S(1)}, bf16[4,256,2,128]{3,2,1,0:T(2,128)(2,1)S(1)}, bf16[4,256,2,128]{3,2,1,0:T(2,128)(2,1)S(1)}) fusion(bf16[4,256,2,512]{3,2,1,0:T(2,128)(2,1)S(1)} %copy-done.7, s32[]{:T(128)S(6)} %select_n.90, s32[]{:T(128)S(6)} %select_n.86, ...), kind=kLoop, calls=%fused_computation.7 | loop fusion | bytes 4194320 | tf_op jit(solution)/shard_map/dynamic_slice | solution.py:333
  54.8 2.5 %collective-permute-done.10.c1 = bf16[4,208,128]{2,1,0:T(8,128)(2,1)S(1)} collective-permute-done((bf16[4,208,128]{2,1,0:T(8,128)(2,1)S(1)}, bf16[4,208,128]{2,1,0:T(8,128)(2,1)S(1)}, u32[]{:S(2)}, u32[]{:S(2)}) %collective-permute-start.10) | collective-permute-done | bytes 213024 | tf_op jit(solution)/shard_map/ppermute | solution.py:323
  57.3 1.8 %collective-permute-done.11.c2 = bf16[4,208,128]{2,1,0:T(8,128)(2,1)S(1)} collective-permute-done((bf16[4,208,128]{2,1,0:T(8,128)(2,1)S(1)}, bf16[4,208,128]{2,1,0:T(8,128)(2,1)S(1)}, u32[]{:S(2)}, u32[]{:S(2)}) %collective-permute-start.11) | collective-permute-done | bytes 213024 | tf_op jit(solution)/shard_map/ppermute | solution.py:323
  59.1 2.2 %collective-permute-done.12.c3 = bf16[4,208,128]{2,1,0:T(8,128)(2,1)S(1)} collective-permute-done((bf16[4,208,128]{2,1,0:T(8,128)(2,1)S(1)}, bf16[4,208,128]{2,1,0:T(8,128)(2,1)S(1)}, u32[]{:S(2)}, u32[]{:S(2)}) %collective-permute-start.12) | collective-permute-done | bytes 213024 | tf_op jit(solution)/shard_map/ppermute | solution.py:323
  61.3 1.2 %combine.1 = (bf16[208,128]{1,0:T(8,128)(2,1)S(1)}, bf16[208,128]{1,0:T(8,128)(2,1)S(1)}, bf16[208,128]{1,0:T(8,128)(2,1)S(1)}, bf16[208,128]{1,0:T(8,128)(2,1)S(1)}) custom-call(s32[8]{0:T(128)S(1)} %stack.38.meta_ref, bf16[4,208,128]{2,1,0:T(8,128)(2,1)S(1)} %get-tuple-element.44.c0, bf16[4,208,128]{2,1,0:T(8,128)(2,1)S(1)} %collective-permute-done.10.c1, ...), custom_call_target="tpu_custom_call" | custom-call | bytes 1048576 | tf_op jit(solution)/shard_map/combine/pallas_call | solution.py:414
  62.5 2.1 %collective-permute-start.13 = (bf16[208,128]{1,0:T(8,128)(2,1)S(1)}, bf16[208,128]{1,0:T(8,128)(2,1)S(1)}, u32[]{:S(2)}, u32[]{:S(2)}) collective-permute-start(bf16[208,128]{1,0:T(8,128)(2,1)S(1)} %get-tuple-element.49), channel_id=1, source_target_pairs={{0,3},{1,0},{2,1},{3,2},{4,7},{5,4},{6,5},{7,6},{8,11},{9,8},{10,9... | collective-permute-start | bytes 159752 | tf_op jit(solution)/shard_map/ppermute | solution.py:323
  64.6 1.5 %collective-permute-start.14 = (bf16[208,128]{1,0:T(8,128)(2,1)S(1)}, bf16[208,128]{1,0:T(8,128)(2,1)S(1)}, u32[]{:S(2)}, u32[]{:S(2)}) collective-permute-start(bf16[208,128]{1,0:T(8,128)(2,1)S(1)} %get-tuple-element.50), channel_id=1, source_target_pairs={{0,2},{1,3},{2,0},{3,1},{4,6},{5,7},{6,4},{7,5},{8,10},{9,11},{10,... | collective-permute-start | bytes 159752 | tf_op jit(solution)/shard_map/ppermute | solution.py:323
  66.1 2.8 %own_tokens.1 = (f32[4,192,128]{2,1,0:T(8,128)S(1)}, f32[4,8,128]{2,1,0:T(8,128)S(1)}) custom-call(s32[4]{0:T(128)S(1)} %copy-done.6, bf16[272,128]{1,0:T(8,128)(2,1)S(1)} %get-tuple-element.36.m0.q0, bf16[272,128]{1,0:T(8,128)(2,1)S(1)} %get-tuple-element.33.q1, bf16[272,128]{1,0:T(8,128)(2,1)S(1)} %get-tuple-element.34.q2, ...), custom_call_target="tpu_custom_call" | custom-call | flops 1073741824 | bytes 4194304 | tf_op jit(solution)/shard_map/own_tokens/pallas_call | solution.py:400
  68.9 1.4 %collective-permute-done.14.r2 = bf16[208,128]{1,0:T(8,128)(2,1)S(1)} collective-permute-done((bf16[208,128]{1,0:T(8,128)(2,1)S(1)}, bf16[208,128]{1,0:T(8,128)(2,1)S(1)}, u32[]{:S(2)}, u32[]{:S(2)}) %collective-permute-start.14) | collective-permute-done | bytes 53280 | tf_op jit(solution)/shard_map/ppermute | solution.py:323
  70.3 1.2 %collective-permute-done.15.r3 = bf16[208,128]{1,0:T(8,128)(2,1)S(1)} collective-permute-done((bf16[208,128]{1,0:T(8,128)(2,1)S(1)}, bf16[208,128]{1,0:T(8,128)(2,1)S(1)}, u32[]{:S(2)}, u32[]{:S(2)}) %collective-permute-start.15) | collective-permute-done | bytes 53280 | tf_op jit(solution)/shard_map/ppermute | solution.py:323
  71.5 1.7 %final.1 = bf16[3,4,64,128]{3,2,1,0:T(8,128)(2,1)} custom-call(s32[8]{0:T(128)S(1)} %stack.38.meta_ref, bf16[208,128]{1,0:T(8,128)(2,1)S(1)} %get-tuple-element.48.r0, bf16[208,128]{1,0:T(8,128)(2,1)S(1)} %collective-permute-done.13.r1, bf16[208,128]{1,0:T(8,128)(2,1)S(1)} %collective-permute-done.14.r2, bf16[208,128]{1,0:T(8,128)(2,1)S(1)} %collective-permute-done.15.r3, ...), custom_call_target="tpu_custom_call" | custom-call | tf_op jit(solution)/shard_map/final/pallas_call | solution.py:424
  (31 shorter events, 2.2 us)
Async XLA Ops:
  0.0 3.1 %collective-permute-start = (bf16[16,2,512]{2,1,0:T(2,128)(2,1)}, bf16[16,2,512]{2,1,0:T(2,128)(2,1)S(1)}, u32[]{:S(2)}, u32[]{:S(2)}) collective-permute-start(bf16[16,2,512]{2,1,0:T(2,128)(2,1)} %sys_ref.1), channel_id=1, source_target_pairs={{0,16},{1,17},{2,18},{3,19},{4,20},{5,21},{6,22},{7,23},{8,24},{9,... | collective-permute-start | bytes 98312 | tf_op jit(solution)/shard_map/ppermute | solution.py:330
  0.0 1.6 %copy-start = (bf16[8,128,2,512]{3,2,1,0:T(2,128)(2,1)S(1)}, bf16[8,128,2,512]{3,2,1,0:T(2,128)(2,1)}, u32[]{:S(2)}) copy-start(bf16[8,128,2,512]{3,2,1,0:T(2,128)(2,1)} %pool_ref.1) | copy-start | bytes 6291460
  1.6 1.5 %copy-start.1 = (bf16[4,3,8192]{2,0,1:T(4,128)(2,1)S(1)}, bf16[4,3,8192]{2,0,1:T(4,128)(2,1)}, u32[]{:S(2)}) copy-start(bf16[4,3,8192]{2,0,1:T(4,128)(2,1)} %param.9) | copy-start | bytes 589828
  1.6 1.5 %copy-start.2 = (bf16[16,2,512]{2,1,0:T(2,128)(2,1)S(1)}, bf16[16,2,512]{2,1,0:T(2,128)(2,1)}, u32[]{:S(2)}) copy-start(bf16[16,2,512]{2,1,0:T(2,128)(2,1)} %sys_ref.1) | copy-start | bytes 98308
  1.6 1.5 %copy-start.3 = (s32[4,64]{1,0:T(4,128)S(1)}, s32[4,64]{1,0:T(4,128)}, u32[]{:S(2)}) copy-start(s32[4,64]{1,0:T(4,128)} %list_ref.1) | copy-start | bytes 3076
  1.6 1.5 %copy-start.4 = (s32[4]{0:T(128)S(1)}, s32[4]{0:T(128)}, u32[]{:S(2)}) copy-start(s32[4]{0:T(128)} %used_ref.1) | copy-start | bytes 52
  1.6 1.5 %copy-start.5 = (s32[1,128]{1,0:T(1,128)S(1)}, s32[1,128]{1,0:T(1,128)}, u32[]{:S(2)}) copy-start(s32[1,128]{1,0:T(1,128)} %slot_ref.1) | copy-start | bytes 1540
  4.0 5.8 %collective-permute-start.1 = (bf16[272,128]{1,0:T(8,128)(2,1)S(1)}, bf16[272,128]{1,0:T(8,128)(2,1)S(1)}, u32[]{:S(2)}, u32[]{:S(2)}) collective-permute-start(bf16[272,128]{1,0:T(8,128)(2,1)S(1)} %get-tuple-element.33.q1), channel_id=1, source_target_pairs={{0,1},{1,2},{2,3},{3,0},{4,5},{5,6},{6,7},{7,4},{8,9},{9,10},{10,1... | collective-permute-start | bytes 208904 | tf_op jit(solution)/shard_map/ppermute | solution.py:323
  5.7 5.8 %collective-permute-start.2 = (bf16[272,128]{1,0:T(8,128)(2,1)S(1)}, bf16[272,128]{1,0:T(8,128)(2,1)S(1)}, u32[]{:S(2)}, u32[]{:S(2)}) collective-permute-start(bf16[272,128]{1,0:T(8,128)(2,1)S(1)} %get-tuple-element.34.q2), channel_id=1, source_target_pairs={{0,2},{1,3},{2,0},{3,1},{4,6},{5,7},{6,4},{7,5},{8,10},{9,11},{10,... | collective-permute-start | bytes 208904 | tf_op jit(solution)/shard_map/ppermute | solution.py:323
  8.4 4.3 %collective-permute-start.3 = (bf16[272,128]{1,0:T(8,128)(2,1)S(1)}, bf16[272,128]{1,0:T(8,128)(2,1)S(1)}, u32[]{:S(2)}, u32[]{:S(2)}) collective-permute-start(bf16[272,128]{1,0:T(8,128)(2,1)S(1)} %get-tuple-element.35.q3), channel_id=1, source_target_pairs={{0,3},{1,0},{2,1},{3,2},{4,7},{5,4},{6,5},{7,6},{8,11},{9,8},{10,9... | collective-permute-start | bytes 208904 | tf_op jit(solution)/shard_map/ppermute | solution.py:323
  12.7 24.3 %all-to-all-start = ((bf16[4,2048,128]{2,1,0:T(8,128)(2,1)}), bf16[4,2048,128]{2,1,0:T(8,128)(2,1)S(1)}, u32[]{:S(2)}, u32[]{:S(2)}) async-start(bf16[4,2048,128]{2,1,0:T(8,128)(2,1)} %bitcast.9), calls=%async_computation | async-start | bytes 4194304 | tf_op jit(solution)/shard_map/all_to_all | solution.py:359
  17.2 16.4 %collective-permute-start.4 = (bf16[4,208,128]{2,1,0:T(8,128)(2,1)S(1)}, bf16[4,208,128]{2,1,0:T(8,128)(2,1)S(1)}, u32[]{:S(2)}, u32[]{:S(2)}) collective-permute-start(bf16[4,208,128]{2,1,0:T(8,128)(2,1)S(1)} %get-tuple-element.40.refs_0_), channel_id=1, source_target_pairs={{0,4},{1,5},{2,6},{3,7},{4,8},{5,9},{6,10},{7,11},{8,12},{9,13},{1... | collective-permute-start | bytes 638984 | tf_op jit(solution)/shard_map/ppermute | solution.py:323
  18.8 14.8 %collective-permute-start.5 = (bf16[4,208,128]{2,1,0:T(8,128)(2,1)S(1)}, bf16[4,208,128]{2,1,0:T(8,128)(2,1)S(1)}, u32[]{:S(2)}, u32[]{:S(2)}) collective-permute-start(bf16[4,208,128]{2,1,0:T(8,128)(2,1)S(1)} %get-tuple-element.40.refs_0_), channel_id=1, source_target_pairs={{0,8},{1,9},{2,10},{3,11},{4,12},{5,13},{6,14},{7,15},{8,0},{9,1},... | collective-permute-start | bytes 638984 | tf_op jit(solution)/shard_map/ppermute | solution.py:323
  21.7 11.9 %collective-permute-start.6 = (bf16[4,208,128]{2,1,0:T(8,128)(2,1)S(1)}, bf16[4,208,128]{2,1,0:T(8,128)(2,1)S(1)}, u32[]{:S(2)}, u32[]{:S(2)}) collective-permute-start(bf16[4,208,128]{2,1,0:T(8,128)(2,1)S(1)} %get-tuple-element.40.refs_0_), channel_id=1, source_target_pairs={{0,12},{1,13},{2,14},{3,15},{4,0},{5,1},{6,2},{7,3},{8,4},{9,5},{1... | collective-permute-start | bytes 638984 | tf_op jit(solution)/shard_map/ppermute | solution.py:323
  23.1 6.3 %collective-permute-start.7 = (bf16[2,128,128]{2,1,0:T(8,128)(2,1)S(1)}, bf16[2,128,128]{2,1,0:T(8,128)(2,1)S(1)}, u32[]{:S(2)}, u32[]{:S(2)}) collective-permute-start(bf16[2,128,128]{2,1,0:T(8,128)(2,1)S(1)} %get-tuple-element.42.refs_5_), channel_id=1, source_target_pairs={{0,32},{1,33},{2,34},{3,35},{4,36},{5,37},{6,38},{7,39},{8,40},{9,... | collective-permute-start | bytes 196616 | tf_op jit(solution)/shard_map/ppermute | solution.py:370
  25.1 7.0 %collective-permute-start.8 = (bf16[2,128,128]{2,1,0:T(8,128)(2,1)S(1)}, bf16[2,128,128]{2,1,0:T(8,128)(2,1)S(1)}, u32[]{:S(2)}, u32[]{:S(2)}) collective-permute-start(bf16[2,128,128]{2,1,0:T(8,128)(2,1)S(1)} %get-tuple-element.42.refs_5_), channel_id=1, source_target_pairs={{0,64},{1,65},{2,66},{3,67},{4,68},{5,69},{6,70},{7,71},{8,72},{9,... | collective-permute-start | bytes 196616 | tf_op jit(solution)/shard_map/ppermute | solution.py:370
  29.4 4.3 %collective-permute-start.9 = (bf16[2,128,128]{2,1,0:T(8,128)(2,1)S(1)}, bf16[2,128,128]{2,1,0:T(8,128)(2,1)S(1)}, u32[]{:S(2)}, u32[]{:S(2)}) collective-permute-start(bf16[2,128,128]{2,1,0:T(8,128)(2,1)S(1)} %get-tuple-element.42.refs_5_), channel_id=1, source_target_pairs={{0,96},{1,97},{2,98},{3,99},{4,100},{5,101},{6,102},{7,103},{8,104... | collective-permute-start | bytes 196616 | tf_op jit(solution)/shard_map/ppermute | solution.py:370
  37.0 16.4 %copy-start.7 = (bf16[4,256,2,512]{3,2,1,0:T(2,128)(2,1)S(1)}, bf16[4,256,2,512]{3,2,1,0:T(2,128)(2,1)}, u32[]{:S(2)}) copy-start(bf16[4,256,2,512]{3,2,1,0:T(2,128)(2,1)} %param.11) | copy-start | bytes 6291460
  48.8 8.6 %collective-permute-start.10 = (bf16[4,208,128]{2,1,0:T(8,128)(2,1)S(1)}, bf16[4,208,128]{2,1,0:T(8,128)(2,1)S(1)}, u32[]{:S(2)}, u32[]{:S(2)}) collective-permute-start(bf16[4,208,128]{2,1,0:T(8,128)(2,1)S(1)} %get-tuple-element.45), channel_id=1, source_target_pairs={{0,12},{1,13},{2,14},{3,15},{4,0},{5,1},{6,2},{7,3},{8,4},{9,5},{1... | collective-permute-start | bytes 638984 | tf_op jit(solution)/shard_map/ppermute | solution.py:323
  51.7 7.5 %collective-permute-start.11 = (bf16[4,208,128]{2,1,0:T(8,128)(2,1)S(1)}, bf16[4,208,128]{2,1,0:T(8,128)(2,1)S(1)}, u32[]{:S(2)}, u32[]{:S(2)}) collective-permute-start(bf16[4,208,128]{2,1,0:T(8,128)(2,1)S(1)} %get-tuple-element.46), channel_id=1, source_target_pairs={{0,8},{1,9},{2,10},{3,11},{4,12},{5,13},{6,14},{7,15},{8,0},{9,1},... | collective-permute-start | bytes 638984 | tf_op jit(solution)/shard_map/ppermute | solution.py:323
  52.5 8.8 %collective-permute-start.12 = (bf16[4,208,128]{2,1,0:T(8,128)(2,1)S(1)}, bf16[4,208,128]{2,1,0:T(8,128)(2,1)S(1)}, u32[]{:S(2)}, u32[]{:S(2)}) collective-permute-start(bf16[4,208,128]{2,1,0:T(8,128)(2,1)S(1)} %get-tuple-element.47), channel_id=1, source_target_pairs={{0,4},{1,5},{2,6},{3,7},{4,8},{5,9},{6,10},{7,11},{8,12},{9,13},{1... | collective-permute-start | bytes 638984 | tf_op jit(solution)/shard_map/ppermute | solution.py:323
  53.4 12.7 %copy-start.6 = (s32[4]{0:T(128)S(1)}, s32[4]{0:T(128)}, u32[]{:S(2)}) copy-start(s32[4]{0:T(128)} %lens_ref) | copy-start | bytes 52
  62.5 6.4 %collective-permute-start.13 = (bf16[208,128]{1,0:T(8,128)(2,1)S(1)}, bf16[208,128]{1,0:T(8,128)(2,1)S(1)}, u32[]{:S(2)}, u32[]{:S(2)}) collective-permute-start(bf16[208,128]{1,0:T(8,128)(2,1)S(1)} %get-tuple-element.49), channel_id=1, source_target_pairs={{0,3},{1,0},{2,1},{3,2},{4,7},{5,4},{6,5},{7,6},{8,11},{9,8},{10,9... | collective-permute-start | bytes 159752 | tf_op jit(solution)/shard_map/ppermute | solution.py:323
  64.6 5.6 %collective-permute-start.14 = (bf16[208,128]{1,0:T(8,128)(2,1)S(1)}, bf16[208,128]{1,0:T(8,128)(2,1)S(1)}, u32[]{:S(2)}, u32[]{:S(2)}) collective-permute-start(bf16[208,128]{1,0:T(8,128)(2,1)S(1)} %get-tuple-element.50), channel_id=1, source_target_pairs={{0,2},{1,3},{2,0},{3,1},{4,6},{5,7},{6,4},{7,5},{8,10},{9,11},{10,... | collective-permute-start | bytes 159752 | tf_op jit(solution)/shard_map/ppermute | solution.py:323
  66.1 5.3 %collective-permute-start.15 = (bf16[208,128]{1,0:T(8,128)(2,1)S(1)}, bf16[208,128]{1,0:T(8,128)(2,1)S(1)}, u32[]{:S(2)}, u32[]{:S(2)}) collective-permute-start(bf16[208,128]{1,0:T(8,128)(2,1)S(1)} %get-tuple-element.51), channel_id=1, source_target_pairs={{0,1},{1,2},{2,3},{3,0},{4,5},{5,6},{6,7},{7,4},{8,9},{9,10},{10,1... | collective-permute-start | bytes 159752 | tf_op jit(solution)/shard_map/ppermute | solution.py:323
